TPU v7x, 32 devices: a whole 2x2x4 slice. The times are simulated.
32 devices in a mesh: seq: 16 (over z, x, core), head: 2 (over y).
Axes of the slice: x: 2, y: 2, z: 4, core: 2. Of those that a mesh axis runs over, the one named last changes fastest.
Arguments:
- tokens: bfloat16 [4096, 768], P(('seq', 'head')), may hold values from -6 to 6
- cotangent: bfloat16 [4096, 768], P(('seq', 'head')), may hold values from -6 to 6
- w_query: bfloat16 [768, 768], P(('seq', 'head')), may hold values from -0.21875 to 0.21875
- w_key: bfloat16 [768, 768], P(('seq', 'head')), may hold values from -0.21875 to 0.21875
- w_value: bfloat16 [768, 768], P(('seq', 'head')), may hold values from -0.21875 to 0.21875
- w_output: bfloat16 [768, 768], P(('seq', 'head')), may hold values from -1.75 to 1.75
- w_inner: bfloat16 [768, 3072], P(('seq', 'head')), may hold values from -0.21875 to 0.21875
- w_outer: bfloat16 [3072, 768], P(('seq', 'head')), may hold values from -0.109375 to 0.109375
- gain_first: float32 [768], replicated, may hold values from 0.1 to 1.9
- shift_first: float32 [768], replicated, may hold values from -1.5 to 1.5
- gain_second: float32 [768], replicated, may hold values from 0.1 to 1.9
- shift_second: float32 [768], replicated, may hold values from -1.5 to 1.5
- attn_down: bfloat16 [8, 4, 16, 768], replicated, may hold values from -0.21875 to 0.21875
- attn_up: bfloat16 [8, 4, 16, 768], replicated, may hold values from -1 to 1
- inner_down: bfloat16 [8, 16, 768], replicated, may hold values from -0.21875 to 0.21875
- inner_up: bfloat16 [8, 16, 3072], replicated, may hold values from -1 to 1
- outer_down: bfloat16 [8, 16, 3072], replicated, may hold values from -0.109375 to 0.109375
- outer_up: bfloat16 [8, 16, 768], replicated, may hold values from -1 to 1
- lengths: int32 [1], replicated, may hold values from 1024 to 4096, as said below
- rand_blocks: int32 [64, 3], P('seq'), may hold values from 2 to 63, as said below
- adapter_pick: int32 [1], replicated, may hold values from 0 to 7
Outputs:
- output: bfloat16 [4096, 768], P(('seq', 'head'))
- grad_tokens: float32 [4096, 768], P(('seq', 'head'))
- grad_attn_down: float32 [8, 4, 16, 768], replicated
- grad_attn_up: float32 [8, 4, 16, 768], replicated
- grad_inner_down: float32 [8, 16, 768], replicated
- grad_inner_up: float32 [8, 16, 3072], replicated
- grad_outer_down: float32 [8, 16, 3072], replicated
- grad_outer_up: float32 [8, 16, 768], replicated
Inputs may be any that keep to these rules, and one draw needn't show every extreme that they name: `lengths`: one sequence, drawn from the seed, has at least 3968 used slots. `rand_blocks`: row b names three different blocks of its own sequence, none of them 0, 1, b - 1, b or b + 1.
All inputs are finite; a program needn't handle non-finite values.
Results may differ from a plain program's by a relative error of at most 0.018.
The roundings to bfloat16 on the way count: a program that leaves them out, or rounds other values in their place, can miss the bound.
Values may be sent and summed in bfloat16 or wider, within the bound.
No kernel may reach another device: no remote copies, remote signals or barrier semaphores. Data moves between devices by JAX's collectives and lax.ppermute only.
A program may use at most 640 MiB of HBM per device.

v0:
```python
import functools

import jax
import jax.numpy as jnp
from jax import lax
from jax.experimental import pallas as pl
from jax.experimental.pallas import tpu as pltpu
from jax.sharding import PartitionSpec as P

D = 768
HEADS = 12
HDIM = 64
BLOCK = 64
ADAPTERS = 8
RANK = 16
FF = 3072

PEERS = (0, 1, 4, 5)
GROUP_HEADS = HEADS // 4
SHARE = GROUP_HEADS * HDIM
WIDE = 256
LSE_LANE = SHARE
DEL_LANE = SHARE + 9
MASK_LANE = SHARE + 18
FLOOR = -1e30
STACK = GROUP_HEADS * BLOCK
AXES = ("seq", "head")
norm_eps = 1e-12
f32 = jnp.float32
bf16 = jnp.bfloat16
VMEM_LIMIT = 60 * 1024 * 1024


def dense_mul(left_op, right_op):
    return jnp.dot(left_op, right_op, preferred_element_type=f32)


def dense_right_t(left_op, right_op):
    return lax.dot_general(left_op, right_op, (((1,), (1,)), ((), ())), preferred_element_type=f32)


def dense_left_t(left_op, right_op):
    return lax.dot_general(left_op, right_op, (((0,), (0,)), ((), ())), preferred_element_type=f32)


def lanes(rows):
    return lax.broadcasted_iota(jnp.int32, (rows, WIDE), 1)


def head_lanes(lane, head):
    return (lane >= HDIM * head) & (lane < HDIM * (head + 1))


def part_lanes(lane, first, head):
    return (lane >= first + 3 * head) & (lane < first + 3 * head + 3)


def project_rows(raw, u_ref, position, seq_length):
    lane = lanes(raw.shape[0])
    data = lane < SHARE

    def part(j):
        piece = raw[:, WIDE * j : WIDE * (j + 1)]
        return (piece + dense_mul(piece[:, WIDE // 2 :].astype(bf16), u_ref[j])).astype(bf16).astype(f32)

    mask = jnp.where(position < seq_length, 0.0, FLOOR)
    query = jnp.where(data, part(0) * 0.125, jnp.where(lane == MASK_LANE, 1.0, 0.0)).astype(bf16)
    key = jnp.where(
        data, part(1), jnp.where(lane < DEL_LANE, 1.0, jnp.where(lane == MASK_LANE, mask, 0.0))
    ).astype(bf16)
    value = jnp.where(
        data, part(2), jnp.where((lane >= DEL_LANE) & (lane < MASK_LANE), 1.0, 0.0)
    ).astype(bf16)
    return query, key, value


def project_kernel(meta_ref, tok_ref, w_ref, u_ref, q_ref, k_ref, v_ref):
    rows = tok_ref.shape[0]
    position = pl.program_id(0) * rows + lax.broadcasted_iota(jnp.int32, (rows, WIDE), 0)
    q_ref[...], k_ref[...], v_ref[...] = project_rows(
        dense_mul(tok_ref[...], w_ref[...]), u_ref, position, meta_ref[1]
    )


def gathered_kernel(meta_ref, rand_ref, slice_ref, down_ref, u_ref, *refs):
    pieces = refs[: len(SLICE_ORDER)]
    q_ref, k_ref, v_ref, *ctx_refs, aux_ref, s_ref, tok_ref, wide_ref, w_ref = refs[len(SLICE_ORDER) :]
    place = meta_ref[0]
    slab = D // len(SLICE_ORDER)
    for s, offset in enumerate(SLICE_ORDER):
        start = pl.multiple_of((place ^ offset) * slab, 8)
        wide_ref[pl.ds(start, slab), :] = slice_ref[slab * s : slab * (s + 1), :]
    column = lax.broadcasted_iota(jnp.int32, (D, 3 * WIDE), 1) & (WIDE - 1)
    w_ref[...] = jnp.where(column < SHARE, wide_ref[...].astype(bf16), down_ref[...])
    rows = 2 * BLOCK
    first = 4 - 3 * ((place >> 1) & 1)
    arrival = [
        side ^ depth ^ step
        for side, near in ((0, first), (2, 5 - first))
        for depth in DEPTHS
        for step in (0, near, 5 - near, 5)
    ]
    for piece, offset in zip(pieces, arrival, strict=True):
        tok_ref[pl.ds(pl.multiple_of((place ^ offset) * rows, rows), rows), :] = piece[...]
    chunk = 8 * BLOCK

    def project(c, carry):
        here = pl.ds(pl.multiple_of(c * chunk, chunk), chunk)
        position = c * chunk + lax.broadcasted_iota(jnp.int32, (chunk, WIDE), 0)
        q_ref[here, :], k_ref[here, :], v_ref[here, :] = project_rows(
            dense_mul(tok_ref[here, :], w_ref[...]), u_ref, position, meta_ref[1]
        )
        return carry

    lax.fori_loop(0, tok_ref.shape[0] // chunk, project, 0)
    forward_kernel(meta_ref, rand_ref, q_ref, k_ref, v_ref, *ctx_refs, aux_ref, s_ref)


def block_rows(ref, block, count=1):
    return ref[pl.ds(pl.multiple_of(block * BLOCK, BLOCK), count * BLOCK), :]


def merge_heads(stacked):
    lane = lanes(BLOCK)
    total = jnp.zeros((BLOCK, WIDE), f32)
    for head in range(GROUP_HEADS):
        total = jnp.where(head_lanes(lane, head), stacked[BLOCK * head : BLOCK * (head + 1)], total)
    return total


def key_set(ref, rand_ref, block, block_total, fill):
    own = block_rows(ref, block)
    left = block_rows(ref, jnp.maximum(block - 1, 0))
    right = block_rows(ref, jnp.minimum(block + 1, block_total - 1))
    if fill:
        blank = jnp.where(lanes(BLOCK) == MASK_LANE, FLOOR, 0.0).astype(bf16)
        left = jnp.where(block - 1 >= 2, left, blank)
        right = jnp.where(block + 1 < block_total, right, blank)
    rand = [block_rows(ref, rand_ref[block * 3 + r]) for r in range(3)]
    return jnp.concatenate([own, left, right, block_rows(ref, 0, 2)] + rand, axis=0)


def own_block(place, t):
    return 2 * (place ^ PEERS[t // 2]) + t % 2


def forward_kernel(meta_ref, rand_ref, q_ref, k_ref, v_ref, *refs):
    ctx_refs, aux_ref, s_ref = refs[:4], refs[4], refs[5]
    place = meta_ref[0]
    total_rows = q_ref.shape[0]
    block_total = total_rows // BLOCK
    chunk = 8 * BLOCK
    chunks = total_rows // chunk

    def queries(block):
        rows = block_rows(q_ref, block)
        lane = lanes(BLOCK)
        blank = jnp.zeros_like(rows)
        return jnp.concatenate(
            [
                jnp.where(head_lanes(lane, head) | (lane == MASK_LANE), rows, blank)
                for head in range(GROUP_HEADS)
            ],
            axis=0,
        )

    def finish(t, low, exact, top, total):
        lane = lanes(BLOCK)
        rows = pl.ds(t * BLOCK, BLOCK)
        ctx_refs[t // 2][pl.ds((t % 2) * BLOCK, BLOCK), :] = merge_heads(low).astype(bf16)
        aux = merge_heads(exact)
        lse = top + jnp.log(total)
        for head in range(GROUP_HEADS):
            aux = jnp.where(lane == LSE_LANE + head, lse[BLOCK * head : BLOCK * (head + 1)], aux)
        aux_ref[rows, :] = aux

    for t in range(8):
        block = own_block(place, t)

        @pl.when(block >= 2)
        def _(t=t, block=block):
            scores = dense_right_t(queries(block), key_set(k_ref, rand_ref, block, block_total, True))
            top = jnp.max(scores, axis=1, keepdims=True)
            weights = jnp.exp(scores - top)
            total = jnp.sum(weights, axis=1, keepdims=True)
            probs = weights / total
            low = probs.astype(bf16)
            rest = (probs - low.astype(f32)).astype(bf16)
            values = key_set(v_ref, rand_ref, block, block_total, False)
            context = dense_mul(low, values)
            finish(t, context, context + dense_mul(rest, values), top, total)

        if t < 2 or (t // 2) in (1, 2, 3):

            @pl.when(block < 2)
            def _(t=t, block=block):
                stack = queries(block)

                def score(c, top):
                    part = dense_right_t(stack, block_rows(k_ref, c * 8, 8))
                    s_ref[c] = part
                    return jnp.maximum(top, jnp.max(part, axis=1, keepdims=True))

                top = lax.fori_loop(0, chunks, score, jnp.full((STACK, 1), FLOOR, f32))

                def weigh(c, total):
                    part = jnp.exp(s_ref[c] - top)
                    s_ref[c] = part
                    return total + jnp.sum(part, axis=1, keepdims=True)

                total = lax.fori_loop(0, chunks, weigh, jnp.zeros((STACK, 1), f32))

                def mix(c, state):
                    context, rest_context = state
                    probs = s_ref[c] / total
                    low = probs.astype(bf16)
                    rest = (probs - low.astype(f32)).astype(bf16)
                    values = block_rows(v_ref, c * 8, 8)
                    return (context + dense_mul(low, values), rest_context + dense_mul(rest, values))

                zero = jnp.zeros((STACK, WIDE), f32)
                context, rest_context = lax.fori_loop(0, chunks, mix, (zero, zero))
                finish(t, context, context + rest_context, top, total)


def split_parts(value):
    high = value.astype(bf16).astype(f32)
    middle = (value - high).astype(bf16).astype(f32)
    return (high, middle, value - high - middle)


def delta_kernel(*refs):
    grad_refs, aux_ref, out_ref = refs[:4], refs[4], refs[5]
    rows = 2 * BLOCK
    lane = lanes(rows)
    for a in range(4):
        here = pl.ds(a * rows, rows)
        grad = grad_refs[a][...].astype(f32)
        aux = aux_ref[here, :]
        result = jnp.where(lane < SHARE, grad, 0.0)
        product = grad * aux
        for head in range(GROUP_HEADS):
            delta = jnp.sum(jnp.where(head_lanes(lane, head), product, 0.0), axis=1, keepdims=True)
            lse = jnp.sum(jnp.where(lane == LSE_LANE + head, aux, 0.0), axis=1, keepdims=True)
            for p, value in enumerate(split_parts(lse)):
                result = jnp.where(lane == LSE_LANE + 3 * head + p, -value, result)
            for p, value in enumerate(split_parts(delta)):
                result = jnp.where(lane == DEL_LANE + 3 * head + p, -value, result)
        out_ref[here, :] = result.astype(bf16)


def backward_kernel(meta_ref, rand_ref, q_ref, k_ref, v_ref, *refs):
    slab_refs, out_refs, (g_ref, dk_ref, dv_ref) = refs[:-7], refs[-7:-3], refs[-3:]
    place = meta_ref[0]
    total_rows = q_ref.shape[0]
    for number, slab_ref in enumerate(slab_refs):
        g_ref[8 * BLOCK * number : 8 * BLOCK * (number + 1), :] = slab_ref[...]
    block_total = total_rows // BLOCK
    chunks = block_total // 8
    half = block_total // 16

    def grad_rows(block):
        other = (block // 2) ^ place
        piece = (other & 1) | ((other >> 1) & 2)
        slab = (other >> 3) + ((other >> 1) & 1) * half
        return block_rows(g_ref, slab * 8 + piece * 2 + (block & 1))

    def stacks(block):
        rows = block_rows(q_ref, block)
        grads = grad_rows(block)
        lane = lanes(BLOCK)
        blank = jnp.zeros_like(rows)
        queries = []
        outers = []
        for head in range(GROUP_HEADS):
            here = head_lanes(lane, head)
            queries.append(
                jnp.where(
                    here | (lane == MASK_LANE),
                    rows,
                    jnp.where(part_lanes(lane, LSE_LANE, head), grads, blank),
                )
            )
            outers.append(jnp.where(here | part_lanes(lane, DEL_LANE, head), grads, blank))
        return jnp.concatenate(queries, axis=0), jnp.concatenate(outers, axis=0)

    def query_side(stack, outer, keys, values):
        probs = jnp.exp(dense_right_t(stack, keys))
        scored = (probs * dense_right_t(outer, values)).astype(bf16)
        return dense_mul(scored, keys)

    def key_side(rows, keys, values, block, allowed):
        stack, outer = stacks(block)
        probs = jnp.exp(dense_right_t(keys, stack))
        if allowed is not None:
            probs = jnp.where(allowed, probs, 0.0)
        scored = (probs * dense_right_t(values, outer)).astype(bf16)
        dk_ref[rows, :] += dense_mul(scored, stack)
        dv_ref[rows, :] += dense_mul(probs.astype(bf16), outer)

    def put_query(t, stacked):
        out_refs[t // 2][pl.ds((t % 2) * BLOCK, BLOCK), :WIDE] = (merge_heads(stacked) * 0.125).astype(bf16)

    for t in range(8):
        block = own_block(place, t)

        @pl.when(block >= 2)
        def _(t=t, block=block):
            stack, outer = stacks(block)
            put_query(
                t,
                query_side(
                    stack,
                    outer,
                    key_set(k_ref, rand_ref, block, block_total, True),
                    key_set(v_ref, rand_ref, block, block_total, False),
                ),
            )

        @pl.when(block < 2)
        def _(t=t, block=block):
            stack, outer = stacks(block)

            def add(c, total):
                return total + query_side(stack, outer, block_rows(k_ref, c * 8, 8), block_rows(v_ref, c * 8, 8))

            put_query(t, lax.fori_loop(0, chunks, add, jnp.zeros((STACK, WIDE), f32)))

    dk_ref[...] = jnp.zeros_like(dk_ref)
    dv_ref[...] = jnp.zeros_like(dv_ref)
    for run in range(2):
        first = 2 * ((place ^ (4 * run)) & ~1)
        keys = block_rows(k_ref, first, 4)
        values = block_rows(v_ref, first, 4)
        rows = pl.ds(run * 4 * BLOCK, 4 * BLOCK)
        key_block = first + lax.broadcasted_iota(jnp.int32, (4 * BLOCK, STACK), 0) // BLOCK

        def band(step, carry, first=first, keys=keys, values=values, rows=rows, key_block=key_block):
            block = first - 1 + step

            @pl.when((block >= 2) & (block < block_total))
            def _():
                near = (key_block - block <= 1) & (block - key_block <= 1) & (key_block >= 2)
                key_side(rows, keys, values, block, near)

            return carry

        lax.fori_loop(0, 6, band, 0)
        key_side(rows, keys, values, 0, None)
        key_side(rows, keys, values, 1, None)

    def random_pairs(block, carry):
        for r in range(3):
            target = rand_ref[block * 3 + r]
            other = (target // 2) ^ place

            @pl.when((other & ~5) == 0)
            def _(target=target, other=other):
                start = pl.multiple_of(((other >> 2) & 1) * 4 * BLOCK + (target & 3) * BLOCK, BLOCK)
                key_side(
                    pl.ds(start, BLOCK), block_rows(k_ref, target), block_rows(v_ref, target), block, None
                )

        return carry

    lax.fori_loop(2, block_total, random_pairs, 0)

    @pl.when((place & ~5) == 0)
    def _():
        start = pl.multiple_of(((place >> 2) & 1) * 4 * BLOCK, BLOCK)
        keys = block_rows(k_ref, 0, 2)
        values = block_rows(v_ref, 0, 2)

        def every(block, carry):
            key_side(pl.ds(start, 2 * BLOCK), keys, values, block, None)
            return carry

        lax.fori_loop(2, block_total, every, 0)

    for piece in range(4):
        start = pl.multiple_of((piece // 2) * 4 * BLOCK + 2 * BLOCK * ((place ^ piece) & 1), BLOCK)
        out_refs[piece][:, WIDE : 2 * WIDE] = dk_ref[pl.ds(start, 2 * BLOCK), :].astype(bf16)
        out_refs[piece][:, 2 * WIDE :] = dv_ref[pl.ds(start, 2 * BLOCK), :].astype(bf16)


def normal(hidden):
    center = hidden - jnp.mean(hidden, axis=-1, keepdims=True)
    root = lax.rsqrt(jnp.mean(center * center, axis=-1, keepdims=True) + norm_eps)
    return center * root, root


def normal_back(grad, normed, root):
    mean = jnp.mean(grad, axis=-1, keepdims=True)
    return root * (grad - mean - normed * jnp.mean(grad * normed, axis=-1, keepdims=True))


def middle_kernel(
    fast,
    meta_ref,
    ctx_refs,
    tok_ref,
    cot_ref,
    late_ref,
    gain_ref,
    down_ref,
    up_ref,
    inner_down_ref,
    inner_up_ref,
    outer_down_ref,
    outer_up_ref,
    wide_ref,
    out_ref,
    grad_ref,
    piece_refs,
    terms_ref,
    hold_ref,
    pre_ref,
    act_ref,
    gin_ref,
):
    group = meta_ref[2]
    rows = tok_ref.shape[0]
    if fast:
        slab = 24
        for pair in range(D // (2 * slab)):
            block = late_ref[2 * slab * pair : 2 * slab * (pair + 1), D + FF :].astype(f32)
            cut = [
                block[slab * side : slab * (side + 1), D * c : D * (c + 1)]
                for side in range(2)
                for c in range(FF // D)
            ]
            wide_ref[8 * slab * pair : 8 * slab * (pair + 1), :] = jnp.concatenate(cut, axis=0).astype(bf16)
    for a in range(4):
        hold_ref[a] = ctx_refs[a][...]
    context = jnp.concatenate([hold_ref[group ^ g][:, :SHARE] for g in range(4)], axis=1)
    context_red = dense_right_t(context, down_ref[...]).astype(bf16)
    attended = dense_mul(context, late_ref[:, :D]) + dense_mul(context_red, up_ref[...])
    first, first_root = normal(tok_ref[...].astype(f32) + attended)
    first_norm = first * gain_ref[0:1, :] + gain_ref[1:2, :]
    first_low = first_norm.astype(bf16)
    inner_red = dense_right_t(first_low, inner_down_ref[...]).astype(bf16)
    outer_red = jnp.zeros((rows, RANK), f32)
    outer_out = jnp.zeros((rows, D), f32)
    for c in range(FF // D):
        here = slice(D * c, D * (c + 1))
        pre = dense_mul(first_low, late_ref[:, D * (c + 1) : D * (c + 2)]) + dense_mul(
            inner_red, inner_up_ref[:, here]
        )
        pre_ref[:, here] = pre
        active = (0.5 * pre * (1.0 + lax.erf(pre * 0.7071067811865476))).astype(bf16)
        act_ref[:, here] = active
        outer_red = outer_red + dense_right_t(active, outer_down_ref[:, here])
        outer_out = outer_out + dense_mul(active, wide_ref[here, :])
    outer_red = outer_red.astype(bf16)
    outer_out = outer_out + dense_mul(outer_red, outer_up_ref[...])
    second, second_root = normal(first_norm + outer_out)
    position = meta_ref[0] * rows + lax.broadcasted_iota(jnp.int32, (rows, D), 0)
    valid = (position < meta_ref[1]).astype(f32)
    out_ref[...] = ((second * gain_ref[2:3, :] + gain_ref[3:4, :]) * valid).astype(bf16)
    grad_second = normal_back(valid * cot_ref[...].astype(f32) * gain_ref[2:3, :], second, second_root)
    grad_outer = grad_second.astype(bf16)
    first_up = RANK * 3
    first_down = RANK * (3 + FF // D)
    terms_ref[first_down + RANK * (FF // D) :, :] = dense_left_t(outer_red, grad_outer)
    outer_grad_red = dense_right_t(grad_outer, outer_up_ref[...]).astype(bf16)
    inner_grad_red = jnp.zeros((rows, RANK), f32)
    grad_first = grad_second
    for c in range(FF // D):
        here = slice(D * c, D * (c + 1))
        grad_active = dense_right_t(grad_outer, wide_ref[here, :]) + dense_mul(
            outer_grad_red, outer_down_ref[:, here]
        )
        pre = pre_ref[:, here]
        slope = 0.5 * (1.0 + lax.erf(pre * 0.7071067811865476)) + pre * (
            0.3989422804014327 * jnp.exp(-0.5 * pre * pre)
        )
        grad_inner = (slope * grad_active).astype(bf16)
        terms_ref[first_up + RANK * c : first_up + RANK * (c + 1), :] = dense_left_t(inner_red, grad_inner)
        terms_ref[first_down + RANK * c : first_down + RANK * (c + 1), :] = dense_left_t(
            outer_grad_red, act_ref[:, here]
        )
        inner_grad_red = inner_grad_red + dense_right_t(grad_inner, inner_up_ref[:, here])
        grad_first = grad_first + dense_right_t(grad_inner, late_ref[:, D * (c + 1) : D * (c + 2)])
    inner_grad_red = inner_grad_red.astype(bf16)
    terms_ref[2 * RANK : 3 * RANK, :] = dense_left_t(inner_grad_red, first_low)
    grad_first = grad_first + dense_mul(inner_grad_red, inner_down_ref[...])
    grad_attended = normal_back(grad_first * gain_ref[0:1, :], first, first_root)
    grad_ref[...] = grad_attended
    grad_low = grad_attended.astype(bf16)
    context_grad_red = dense_right_t(grad_low, up_ref[...]).astype(bf16)
    terms_ref[:RANK, :] = dense_left_t(context_grad_red, context)
    terms_ref[RANK : 2 * RANK, :] = dense_left_t(context_red, grad_low)
    grad_context = (
        dense_right_t(grad_low, late_ref[:, :D]) + dense_mul(context_grad_red, down_ref[...])
    ).astype(bf16)
    blank = jnp.zeros((rows, WIDE - SHARE), bf16)
    for g in range(4):
        hold_ref[group ^ g] = jnp.concatenate([grad_context[:, SHARE * g : SHARE * (g + 1)], blank], axis=1)
    for a in range(4):
        piece_refs[a][...] = hold_ref[a]


def finish_kernel(fast, meta_ref, *refs):
    part_refs = refs[:4]
    tok_ref, w_ref, down_ref, up_ref, grad_ref, early_ref, out_ref, terms_ref, hold_ref, sum_ref = refs[4:]
    group = meta_ref[2]
    core = (meta_ref[0] >> 1) & 1
    for a in range(4):
        hold_ref[a] = part_refs[a][...]
    tokens = tok_ref[...]
    total = grad_ref[...]
    for j in range(3):
        grad = jnp.concatenate(
            [hold_ref[group ^ g][:, WIDE * j : WIDE * j + SHARE] for g in range(4)], axis=1
        )
        reduced = dense_right_t(tokens, down_ref[j]).astype(bf16)
        grad_reduced = dense_right_t(grad, up_ref[j]).astype(bf16)
        sum_ref[RANK * j : RANK * (j + 1), :] = dense_left_t(grad_reduced, tokens)
        sum_ref[RANK * (4 + j) : RANK * (5 + j), :] = dense_left_t(reduced, grad)
        total = total + dense_right_t(grad, w_ref[:, D * j : D * (j + 1)]) + dense_mul(grad_reduced, down_ref[j])
    out_ref[...] = total
    sum_ref[RANK * 3 : RANK * 4, :] = early_ref[:RANK, :]
    sum_ref[RANK * 7 : RANK * 8, :] = early_ref[RANK : 2 * RANK, :]
    sum_ref[RANK * 8 : KINDS * RANK, :] = early_ref[2 * RANK :, :]
    sum_ref[KINDS * RANK :, :] = jnp.zeros((SUM_ROWS - KINDS * RANK, D), f32)
    if fast:
        for part in range(8):
            terms_ref[(part // 4) ^ core, (part % 4) ^ group] = sum_ref[PART_ROWS * part : PART_ROWS * (part + 1), :]
    else:
        terms_ref[...] = sum_ref[...]


def spread_kernel(meta_ref, *refs):
    near_refs, far_refs = refs[:4], refs[4:8]
    outs = refs[14:20]
    sum_ref, sems = refs[20:]
    group = meta_ref[2]
    core = (meta_ref[0] >> 1) & 1
    chosen = meta_ref[3]
    for a in range(4):
        for side, ref in ((0, near_refs[a]), (1, far_refs[a])):
            start = pl.multiple_of(((core ^ side) * 4 + (group ^ a)) * PART_ROWS, 8)
            sum_ref[pl.ds(start, PART_ROWS), :] = ref[...]
    places = [outs[0].at[chosen, j] for j in range(4)] + [outs[1].at[chosen, j] for j in range(4)]
    places.append(outs[2].at[chosen])
    places += [outs[n].at[chosen, :, pl.ds(D * c, D)] for n in (3, 4) for c in range(FF // D)]
    places.append(outs[5].at[chosen])
    copies = [
        pltpu.make_async_copy(sum_ref.at[pl.ds(RANK * n, RANK), :], where, sems.at[n])
        for n, where in enumerate(places)
    ]
    for copy in copies:
        copy.start()
    for copy in copies:
        copy.wait()


KINDS = 18
SUM_ROWS = 320
PART_ROWS = SUM_ROWS // 8
ANY = pl.BlockSpec(memory_space=pl.ANY)
SMEM = pl.BlockSpec(memory_space=pltpu.SMEM)
VMEM = pl.BlockSpec(memory_space=pltpu.VMEM)
DEPTHS = (0, 8, 16, 24)
SLICE_ORDER = tuple(side ^ depth ^ peer for side in (0, 2) for depth in DEPTHS for peer in PEERS)


def gather_rows(value, device_total):
    def send(piece, even, odd):
        return lax.ppermute(
            piece, AXES, [(j, j ^ (odd if (j >> 1) & 1 else even)) for j in range(device_total)]
        )

    held = []
    for depth in DEPTHS:
        start = value if depth == 0 else send(value, depth, depth)
        across = send(start, 4, 1)
        held += [start, across, send(start, 1, 4), send(across, 1, 4)]
    return held + [send(piece, 2, 2) for piece in held]


def shards(
    tokens,
    cotangent,
    w_query,
    w_key,
    w_value,
    w_output,
    w_inner,
    w_outer,
    gain_first,
    shift_first,
    gain_second,
    shift_second,
    attn_down,
    attn_up,
    inner_down,
    inner_up,
    outer_down,
    outer_up,
    lengths,
    rand_blocks,
    adapter_pick,
):
    device_total = lax.axis_size("seq") * lax.axis_size("head")
    local_rows = tokens.shape[0]
    seq_total = lengths.shape[0]
    members = device_total // seq_total
    rows_total = members * local_rows
    block_total = rows_total // BLOCK
    index = lax.axis_index("seq") * lax.axis_size("head") + lax.axis_index("head")
    place = index % members
    seq_number = index // members
    group = (place & 1) | ((place >> 1) & 2)
    seq_length = lengths[seq_number]
    chosen = adapter_pick[seq_number]

    def swap(value, mask):
        return lax.ppermute(value, AXES, [(j, j ^ mask) for j in range(device_total)])

    def select(table):
        return lax.dynamic_index_in_dim(table, chosen, 0, keepdims=False)

    down_sel, up_sel = select(attn_down), select(attn_up)
    inner_down_sel, inner_up_sel = select(inner_down), select(inner_up)
    outer_down_sel, outer_up_sel = select(outer_down), select(outer_up)

    def gather_all(value):
        return lax.all_gather(value, AXES, axis=0, tiled=True)

    slab = D // device_total
    full_qkv = gather_all(jnp.concatenate([w_query, w_key, w_value], axis=1))
    late = gather_all(
        jnp.concatenate([w_output, w_inner] + [w_outer[slab * c : slab * (c + 1)] for c in range(FF // D)], axis=1)
    )
    meta = jnp.stack([place, seq_length, group, chosen]).astype(jnp.int32)
    fast = device_total == 32 and members == 32

    def share_columns(table, which=group):
        return lax.dynamic_slice_in_dim(table, which * SHARE, SHARE, table.ndim - 1)

    side_up = jnp.stack(
        [
            jnp.pad(share_columns(up_sel[j]), ((WIDE // 4, WIDE // 4 - RANK), (0, WIDE - SHARE)))
            for j in range(3)
        ]
    )
    side_down = jnp.concatenate(
        [jnp.pad(down_sel[j].T, ((0, 0), (SHARE, WIDE - SHARE - RANK))) for j in range(3)], axis=1
    )
    chunk = 8 * BLOCK
    wide_rows = jax.ShapeDtypeStruct((rows_total, WIDE), bf16)
    piece_shapes = [jax.ShapeDtypeStruct((local_rows, WIDE), bf16)] * 4
    ctx_shapes = piece_shapes + [jax.ShapeDtypeStruct((chunk, WIDE), f32)]
    score_scratch = pltpu.VMEM((rows_total // chunk, STACK, chunk), f32)
    if fast:
        columns = jnp.stack([w_query, w_key, w_value], axis=1)
        marks = jnp.pad(
            rand_blocks.reshape(1, 1, -1).astype(bf16), ((0, slab - 1), (0, 2), (0, WIDE - SHARE - rand_blocks.size))
        )

        def slices(peer):
            return jnp.concatenate([share_columns(columns, group ^ peer), marks], axis=2).reshape(slab, 3 * WIDE)

        pieces = gather_rows(tokens, device_total)
        mine = jnp.concatenate([slices(0)] + [swap(slices(p), PEERS[p]) for p in range(1, 4)], axis=0)
        mine, pieces[5] = lax.optimization_barrier((mine, pieces[5]))
        mine = jnp.concatenate([mine] + [swap(mine, depth) for depth in DEPTHS[1:]], axis=0)
        mine = jnp.concatenate([mine, swap(mine, 2)], axis=0)
        marks_all = mine.reshape(device_total, slab, 3 * WIDE)[:, 0, SHARE : SHARE + rand_blocks.size]
        source = jnp.argsort(jnp.array(SLICE_ORDER))[(2 * jnp.arange(device_total // 2)) ^ place]
        rand_flat = marks_all[source].astype(jnp.int32).reshape(-1)
        query_all, key_all, value_all, *ctx, aux = pl.pallas_call(
            gathered_kernel,
            in_specs=[SMEM, SMEM] + [VMEM] * (3 + len(pieces)),
            out_specs=[VMEM] * 8,
            out_shape=[wide_rows] * 3 + ctx_shapes,
            scratch_shapes=[
                score_scratch,
                pltpu.VMEM((rows_total, D), bf16),
                pltpu.VMEM((D, 3 * WIDE), f32),
                pltpu.VMEM((D, 3 * WIDE), bf16),
            ],
            compiler_params=pltpu.CompilerParams(vmem_limit_bytes=VMEM_LIMIT),
            name="project_attend",
        )(meta, rand_flat, mine.astype(f32), side_down, side_up, *pieces)
    else:
        tok_all = lax.dynamic_slice_in_dim(gather_all(tokens), seq_number * rows_total, rows_total, 0)
        rand_all = lax.all_gather(rand_blocks, "seq", axis=0, tiled=True)
        rand_flat = lax.dynamic_slice_in_dim(rand_all, seq_number * block_total, block_total, 0).reshape(-1)
        side_weight = (
            jnp.concatenate(
                [
                    jnp.pad(share_columns(full_qkv[:, D * j : D * (j + 1)]), ((0, 0), (0, WIDE - SHARE)))
                    for j in range(3)
                ],
                axis=1,
            )
            + side_down
        )
        wide_block = pl.BlockSpec((chunk, WIDE), lambda c: (c, 0))
        query_all, key_all, value_all = pl.pallas_call(
            project_kernel,
            grid=(rows_total // chunk,),
            in_specs=[
                SMEM,
                pl.BlockSpec((chunk, D), lambda c: (c, 0)),
                pl.BlockSpec((D, 3 * WIDE), lambda c: (0, 0)),
                pl.BlockSpec((3, WIDE // 2, WIDE), lambda c: (0, 0, 0)),
            ],
            out_specs=[wide_block] * 3,
            out_shape=[wide_rows] * 3,
            compiler_params=pltpu.CompilerParams(vmem_limit_bytes=VMEM_LIMIT),
            name="project_all",
        )(meta, tok_all, side_weight, side_up)
        *ctx, aux = pl.pallas_call(
            forward_kernel,
            in_specs=[SMEM, SMEM, VMEM, VMEM, VMEM],
            out_specs=[VMEM] * 5,
            out_shape=ctx_shapes,
            scratch_shapes=[score_scratch],
            compiler_params=pltpu.CompilerParams(vmem_limit_bytes=VMEM_LIMIT),
            name="attend_forward",
        )(meta, rand_flat, query_all, key_all, value_all)

    def exchange(pieces):
        return [pieces[0]] + [swap(pieces[a], PEERS[a]) for a in range(1, 4)]

    gains = jnp.stack([gain_first, shift_first, gain_second, shift_second])
    middle_in = [tokens, cotangent, late, gains, down_sel[3], up_sel[3]]
    middle_in += [inner_down_sel, inner_up_sel, outer_down_sel, outer_up_sel]
    wide_shape = [pltpu.VMEM((FF, D), bf16)]
    if not fast:
        middle_in.append(
            late[:, D + FF :].reshape(device_total, slab, FF // D, D).transpose(0, 2, 1, 3).reshape(FF, D)
        )
        wide_shape = []
    count = len(middle_in)

    def middle(meta_ref, *refs):
        ins, outs, scratch = refs[4 : 4 + count], refs[4 + count : 11 + count], refs[11 + count :]
        wide_ref = scratch[-1] if fast else ins[-1]
        middle_kernel(
            fast, meta_ref, refs[:4], *ins[:10], wide_ref, *outs[:2], outs[2:6], outs[6], *scratch[:4]
        )

    output, grad_attended, *grad_pieces, early_terms = pl.pallas_call(
        middle,
        in_specs=[SMEM] + [VMEM] * (4 + count),
        out_specs=[VMEM] * 7,
        out_shape=[
            jax.ShapeDtypeStruct((local_rows, D), bf16),
            jax.ShapeDtypeStruct((local_rows, D), f32),
        ]
        + piece_shapes
        + [jax.ShapeDtypeStruct(((KINDS - 6) * RANK, D), f32)],
        scratch_shapes=[
            pltpu.VMEM((4, local_rows, WIDE), bf16),
            pltpu.VMEM((local_rows, FF), f32),
            pltpu.VMEM((local_rows, FF), bf16),
            pltpu.VMEM((local_rows, FF), bf16),
        ]
        + wide_shape,
        compiler_params=pltpu.CompilerParams(vmem_limit_bytes=VMEM_LIMIT),
        name="middle",
    )(meta, *exchange(ctx), *middle_in)
    grad_wide = pl.pallas_call(
        delta_kernel,
        in_specs=[VMEM] * 5,
        out_specs=VMEM,
        out_shape=jax.ShapeDtypeStruct((chunk, WIDE), bf16),
        name="delta",
    )(*exchange(grad_pieces), aux)
    slabs = [grad_wide] + [swap(grad_wide, 8 * r) for r in range(1, members // 8)]
    slabs = slabs + [swap(slab_rows, 2) for slab_rows in slabs]
    grad_qkv = pl.pallas_call(
        backward_kernel,
        in_specs=[SMEM, SMEM] + [VMEM] * (3 + len(slabs)),
        out_specs=[VMEM] * 4,
        out_shape=[jax.ShapeDtypeStruct((local_rows, 3 * WIDE), bf16)] * 4,
        scratch_shapes=[
            pltpu.VMEM((rows_total, WIDE), bf16),
            pltpu.VMEM((chunk, WIDE), f32),
            pltpu.VMEM((chunk, WIDE), f32),
        ],
        compiler_params=pltpu.CompilerParams(vmem_limit_bytes=VMEM_LIMIT),
        name="attend_backward",
    )(meta, rand_flat, query_all, key_all, value_all, *slabs)
    grad_tokens, terms = pl.pallas_call(
        functools.partial(finish_kernel, fast),
        in_specs=[SMEM] + [VMEM] * 10,
        out_specs=[VMEM, VMEM],
        out_shape=[
            jax.ShapeDtypeStruct((local_rows, D), f32),
            jax.ShapeDtypeStruct((2, 4, PART_ROWS, D) if fast else (SUM_ROWS, D), f32),
        ],
        scratch_shapes=[pltpu.VMEM((4, local_rows, 3 * WIDE), bf16), pltpu.VMEM((SUM_ROWS, D), f32)],
        compiler_params=pltpu.CompilerParams(vmem_limit_bytes=VMEM_LIMIT),
        name="finish",
    )(meta, *exchange(grad_qkv), tokens, full_qkv, down_sel[:3], up_sel[:3], grad_attended, early_terms)

    out_shapes = [
        (ADAPTERS, 4, RANK, D),
        (ADAPTERS, 4, RANK, D),
        (ADAPTERS, RANK, D),
        (ADAPTERS, RANK, FF),
        (ADAPTERS, RANK, FF),
        (ADAPTERS, RANK, D),
    ]
    if fast:
        paired = terms[0] + swap(terms[1], 2)
        moved = [paired[0]] + [swap(paired[a], PEERS[a]) for a in range(1, 4)]
        part = (moved[0] + moved[1]) + (moved[2] + moved[3])
        moved = [part] + [swap(part, depth) for depth in DEPTHS[1:]]
        part = (moved[0] + moved[1]) + (moved[2] + moved[3])
        near = exchange([part] * 4)
        far = [swap(value, 2) for value in near]
        sums = pl.pallas_call(
            spread_kernel,
            in_specs=[SMEM] + [VMEM] * 8 + [ANY] * 6,
            out_specs=[ANY] * 6,
            out_shape=[jax.ShapeDtypeStruct(shape, f32) for shape in out_shapes],
            scratch_shapes=[pltpu.VMEM((SUM_ROWS, D), f32), pltpu.SemaphoreType.DMA((KINDS,))],
            input_output_aliases={9 + n: n for n in range(6)},
            name="spread",
        )(meta, *near, *far, *[jnp.zeros(shape, f32) for shape in out_shapes])
        return (output, grad_tokens, *sums)

    slots = (jnp.arange(seq_total) == seq_number).astype(f32)[:, None, None]
    every = lax.psum(slots * terms[None], AXES)

    def spread(first, count, width):
        def term(s):
            rows = every[s, first * RANK : (first + count * (width // D)) * RANK]
            value = rows.reshape(count, width // D, RANK, D).transpose(0, 2, 1, 3).reshape(count, RANK, width)
            return (jnp.arange(ADAPTERS) == adapter_pick[s]).astype(f32)[:, None, None, None] * value[None]

        return functools.reduce(lambda x, y: x + y, [term(s) for s in range(seq_total)])

    wide = FF // D
    sums = [
        spread(0, 4, D),
        spread(4, 4, D),
        spread(8, 1, D),
        spread(9, 1, FF),
        spread(9 + wide, 1, FF),
        spread(9 + 2 * wide, 1, D),
    ]
    return (output, grad_tokens, *[value.reshape(shape) for value, shape in zip(sums, out_shapes, strict=True)])


def solution(mesh):
    rows = P(AXES, None)
    placed = (rows,) * 8 + (P(),) * 11 + (P("seq", None), P())
    return jax.shard_map(
        shards,
        mesh=mesh,
        in_specs=placed,
        out_specs=(rows, rows) + (P(),) * 6,
        check_vma=False,
    )
```

profile of v0, /device:TPU:0, one launch (start us, length us, event | category | flops | bytes accessed | tf_op | source)
XLA Modules:
  0.0 320.1 jit_solution(3156649240919424776)
XLA Ops:
  14.4 3.1 collective-permute-start.3
  17.5 2.6 collective-permute-start.14
  20.5 1.5 collective-permute-start
  22.0 1.5 collective-permute-start.1
  26.8 1.6 dynamic-slice_bitcast_fusion
  29.4 1.7 collective-permute-start.9
  31.1 1.5 collective-permute-start.10
  33.3 4.7 %collective-permute-done.18.refs_12_ = bf16[128,768]{1,0:T(8,128)(2,1)} collective-permute-done((bf16[128,768]{1,0:T(8,128)(2,1)S(1)}, bf16[128,768]{1,0:T(8,128)(2,1)}, u32[]{:S(2)}, u32[]{:S(2)}) %collective-permute-start.18) | collective-permute-done | bytes 196640 | tf_op jit(solution)/shard_map/ppermute | solution.py:570
  38.0 1.5 collective-permute-start.15
  40.2 7.2 %collective-permute-start.5 = (bf16[96,768]{1,0:T(8,128)(2,1)S(1)}, bf16[96,768]{1,0:T(8,128)(2,1)S(1)}, u32[]{:S(2)}, u32[]{:S(2)}) collective-permute-start(bf16[96,768]{1,0:T(8,128)(2,1)S(1)} %pad_maximum_fusion.2), channel_id=1, source_target_pairs={{0,8},{1,9},{2,10},{3,11},{4,12},{5,13},{6,14},{7,15},{8,0},{9,1},... | collective-permute-start | bytes 442376 | tf_op jit(solution)/shard_map/ppermute | solution.py:619
  47.4 2.6 collective-permute-start.6
  51.5 1.6 collective-permute-start.12
  54.7 2.4 collective-permute-start.20
  57.1 11.3 %collective-permute-done.6 = bf16[96,768]{1,0:T(8,128)(2,1)S(1)} collective-permute-done((bf16[96,768]{1,0:T(8,128)(2,1)S(1)}, bf16[96,768]{1,0:T(8,128)(2,1)S(1)}, u32[]{:S(2)}, u32[]{:S(2)}) %collective-permute-start.6) | collective-permute-done | bytes 147488 | tf_op jit(solution)/shard_map/ppermute | solution.py:619
  72.1 2.3 collective-permute-done.11.refs_3_
  82.5 1.5 collective-permute-done.13.refs_7_
  84.0 6.3 %collective-permute-done.17.refs_11_ = bf16[128,768]{1,0:T(8,128)(2,1)} collective-permute-done((bf16[128,768]{1,0:T(8,128)(2,1)}, bf16[128,768]{1,0:T(8,128)(2,1)}, u32[]{:S(2)}, u32[]{:S(2)}) %collective-permute-start.17) | collective-permute-done | bytes 196640 | tf_op jit(solution)/shard_map/ppermute | solution.py:570
  90.2 6.3 %collective-permute-done.21.refs_15_ = bf16[128,768]{1,0:T(8,128)(2,1)} collective-permute-done((bf16[128,768]{1,0:T(8,128)(2,1)}, bf16[128,768]{1,0:T(8,128)(2,1)}, u32[]{:S(2)}, u32[]{:S(2)}) %collective-permute-start.21) | collective-permute-done | bytes 196640 | tf_op jit(solution)/shard_map/ppermute | solution.py:570
  99.2 1.6 convert_element_type.38.slice_ref
  103.6 32.2 %project_attend.1 = (bf16[4096,256]{1,0:T(8,128)(2,1)}, bf16[4096,256]{1,0:T(8,128)(2,1)}, bf16[4096,256]{1,0:T(8,128)(2,1)}, bf16[128,256]{1,0:T(8,128)(2,1)}, ...) custom-call(s32[4]{0:T(128)} %pad_add_fusion.meta_ref, ...), custom_call_target="tpu_custom_call" | custom-call | tf_op jit(solution)/shard_map/project_attend/pallas_call | solution.py:673
  135.8 2.7 collective-permute-start.38
  141.0 2.0 collective-permute-done.39.refs_2_
  143.0 2.0 collective-permute-done.40.refs_3_
  145.6 15.0 %middle.1 = (bf16[128,768]{1,0:T(8,128)(2,1)}, f32[128,768]{1,0:T(8,128)}, bf16[128,256]{1,0:T(8,128)(2,1)}, bf16[128,256]{1,0:T(8,128)(2,1)}, bf16[128,256]{1,0...) custom-call(s32[4]{0:T(128)} %pad_add_fusion.meta_ref, bf16[128,256]{1,0:T(8,128)(2,1)} %get-tuple-element.41.refs_0_, ...), custom_call_target="tpu_custom_call" | custom-call | tf_op jit(solution)/shard_map/middle/pallas_call | solution.py:747
  161.9 2.2 collective-permute-start.43
  165.6 1.6 collective-permute-done.43.refs_3_
  167.9 2.9 delta.1.refs_0_
  172.5 2.7 collective-permute-start.46
  175.2 15.0 %collective-permute-done.44.refs_1_ = bf16[512,256]{1,0:T(8,128)(2,1)S(1)} collective-permute-done((bf16[512,256]{1,0:T(8,128)(2,1)}, bf16[512,256]{1,0:T(8,128)(2,1)S(1)}, u32[]{:S(2)}, u32[]{:S(2)}) %collective-permute-start.44) | collective-permute-done | bytes 262176 | tf_op jit(solution)/shard_map/ppermute | solution.py:619
  190.2 9.5 %collective-permute-done.45.refs_2_ = bf16[512,256]{1,0:T(8,128)(2,1)S(1)} collective-permute-done((bf16[512,256]{1,0:T(8,128)(2,1)}, bf16[512,256]{1,0:T(8,128)(2,1)S(1)}, u32[]{:S(2)}, u32[]{:S(2)}) %collective-permute-start.45) | collective-permute-done | bytes 262176 | tf_op jit(solution)/shard_map/ppermute | solution.py:619
  202.3 51.2 %attend_backward.1 = (bf16[128,768]{1,0:T(8,128)(2,1)}, bf16[128,768]{1,0:T(8,128)(2,1)}, bf16[128,768]{1,0:T(8,128)(2,1)}, bf16[128,768]{1,0:T(8,128)(2,1)}) custom-call(s32[4]{0:T(128)} %pad_add_fusion.meta_ref, s32[192]{0:T(256)} %reshape.107.rand_ref, bf16[4096,256]{1,0:T(8,128)(2,1)} %get-tuple-element.46.q_ref, ...), custom_call_target="tpu_custom_call" | custom-call | tf_op jit(solution)/shard_map/attend_backward/pallas_call | solution.py:776
  254.6 1.5 collective-permute-start.52
  257.0 1.5 dynamic-slice_bitcast_fusion.2.refs_7_
  258.5 1.5 dynamic-slice_bitcast_fusion.3.refs_6_
  260.5 2.4 collective-permute-done.53.refs_3_
  263.6 6.2 %finish.1 = (f32[128,768]{1,0:T(8,128)}, f32[2,4,40,768]{3,2,1,0:T(8,128)}) custom-call(s32[4]{0:T(128)} %pad_add_fusion.meta_ref, bf16[128,768]{1,0:T(8,128)(2,1)} %get-tuple-element.54.refs_0_, bf16[128,768]{1,0:T(8,128)(2,1)} %copy-done.12, bf16[128,768]{1,0:T(8,128)(2,1)} %copy-done.13, bf16[128,768]{1,0:T(8,128)(2,1)} %copy-done.14, ...), custom_call_target="tpu_custom_call" | custom-call | tf_op jit(solution)/shard_map/finish/pallas_call | solution.py:789
  271.1 1.9 collective-permute-done.54
  274.2 1.5 collective-permute-start.56
  276.6 1.9 collective-permute-done.55
  278.5 2.0 collective-permute-done.56
  280.4 1.9 collective-permute-done.57
  282.5 4.3 %collective-permute-start.60 = (f32[40,768]{1,0:T(8,128)S(1)}, f32[40,768]{1,0:T(8,128)S(1)}, u32[]{:S(2)}, u32[]{:S(2)}) collective-permute-start(f32[40,768]{1,0:T(8,128)S(1)} %fusion.7), channel_id=1, source_target_pairs={{0,24},{1,25},{2,26},{3,27},{4,28},{5,29},{6,30},{7,31},{8,16},{9,... | collective-permute-start | bytes 368648 | tf_op jit(solution)/shard_map/ppermute | solution.py:619
  286.8 2.2 collective-permute-done.58
  289.0 5.3 %collective-permute-done.59 = f32[40,768]{1,0:T(8,128)S(1)} collective-permute-done((f32[40,768]{1,0:T(8,128)S(1)}, f32[40,768]{1,0:T(8,128)S(1)}, u32[]{:S(2)}, u32[]{:S(2)}) %collective-permute-start.59) | collective-permute-done | bytes 122912 | tf_op jit(solution)/shard_map/ppermute | solution.py:619
  295.4 1.5 collective-permute-start.62
  297.9 2.2 collective-permute-done.61.refs_1_
  300.6 2.0 collective-permute-done.63.refs_3_
  310.9 2.4 spread.1
  (267 shorter events, 60.1 us)
Async XLA Ops:
  7.2 137.7 %all-gather.3.cloned.1.call-start = ((), (), s32[]{:S(2)}) async-start(), calls=%async_computation | async-start | bytes 10948608 | tf_op jit(solution)/shard_map/all_gather | solution.py:629
  12.9 247.1 %all-gather.5.cloned.1.call-start = ((), (), s32[]{:S(2)}) async-start(), calls=%async_computation.1 | async-start | bytes 3649536 | tf_op jit(solution)/shard_map/all_gather | solution.py:629
  14.4 18.2 %collective-permute-start.3 = (bf16[128,768]{1,0:T(8,128)(2,1)S(1)}, bf16[128,768]{1,0:T(8,128)(2,1)S(1)}, u32[]{:S(2)}, u32[]{:S(2)}) collective-permute-start(bf16[128,768]{1,0:T(8,128)(2,1)S(1)} %copy-done.1), channel_id=1, source_target_pairs={{0,8},{1,9},{2,10},{3,11},{4,12},{5,13},{6,14},{7,15},{8,0},{9,1},... | collective-permute-start | bytes 589832 | tf_op jit(solution)/shard_map/ppermute | solution.py:570
  17.5 15.1 %collective-permute-start.14 = (bf16[128,768]{1,0:T(8,128)(2,1)S(1)}, bf16[128,768]{1,0:T(8,128)(2,1)}, u32[]{:S(2)}, u32[]{:S(2)}) collective-permute-start(bf16[128,768]{1,0:T(8,128)(2,1)S(1)} %copy-done.1), channel_id=1, source_target_pairs={{0,16},{1,17},{2,18},{3,19},{4,20},{5,21},{6,22},{7,23},{8,24},{9,... | collective-permute-start | bytes 589832 | tf_op jit(solution)/shard_map/ppermute | solution.py:570
  20.5 8.9 %collective-permute-start = (bf16[24,768]{1,0:T(8,128)(2,1)S(1)}, bf16[24,768]{1,0:T(8,128)(2,1)S(1)}, u32[]{:S(2)}, u32[]{:S(2)}) collective-permute-start(bf16[24,768]{1,0:T(8,128)(2,1)S(1)} %bitcast.96), channel_id=1, source_target_pairs={{0,1},{1,0},{2,3},{3,2},{4,5},{5,4},{6,7},{7,6},{8,9},{9,8},{10,11... | collective-permute-start | bytes 110600 | tf_op jit(solution)/shard_map/ppermute | solution.py:619
  22.0 7.4 %collective-permute-start.1 = (bf16[24,768]{1,0:T(8,128)(2,1)S(1)}, bf16[24,768]{1,0:T(8,128)(2,1)S(1)}, u32[]{:S(2)}, u32[]{:S(2)}) collective-permute-start(bf16[24,768]{1,0:T(8,128)(2,1)S(1)} %bitcast.95), channel_id=1, source_target_pairs={{0,4},{1,5},{2,6},{3,7},{4,0},{5,1},{6,2},{7,3},{8,12},{9,13},{10,... | collective-permute-start | bytes 110600 | tf_op jit(solution)/shard_map/ppermute | solution.py:619
  23.5 7.6 %collective-permute-start.2 = (bf16[24,768]{1,0:T(8,128)(2,1)S(1)}, bf16[24,768]{1,0:T(8,128)(2,1)S(1)}, u32[]{:S(2)}, u32[]{:S(2)}) collective-permute-start(bf16[24,768]{1,0:T(8,128)(2,1)S(1)} %bitcast.94), channel_id=1, source_target_pairs={{0,5},{1,4},{2,7},{3,6},{4,1},{5,0},{6,3},{7,2},{8,13},{9,12},{10,... | collective-permute-start | bytes 110600 | tf_op jit(solution)/shard_map/ppermute | solution.py:619
  29.3 8.7 %collective-permute-start.18 = (bf16[128,768]{1,0:T(8,128)(2,1)S(1)}, bf16[128,768]{1,0:T(8,128)(2,1)}, u32[]{:S(2)}, u32[]{:S(2)}) collective-permute-start(bf16[128,768]{1,0:T(8,128)(2,1)S(1)} %copy-done.1), channel_id=1, source_target_pairs={{0,24},{1,25},{2,26},{3,27},{4,28},{5,29},{6,30},{7,31},{8,16},{9,... | collective-permute-start | bytes 589832 | tf_op jit(solution)/shard_map/ppermute | solution.py:570
  29.4 10.8 %collective-permute-start.9 = (bf16[128,768]{1,0:T(8,128)(2,1)S(1)}, bf16[128,768]{1,0:T(8,128)(2,1)}, u32[]{:S(2)}, u32[]{:S(2)}) collective-permute-start(bf16[128,768]{1,0:T(8,128)(2,1)S(1)} %copy-done.1), channel_id=1, source_target_pairs={{0,4},{1,5},{2,3},{3,2},{4,0},{5,1},{6,7},{7,6},{8,12},{9,13},{10,... | collective-permute-start | bytes 589832 | tf_op jit(solution)/shard_map/ppermute | solution.py:570
  31.1 16.3 %collective-permute-start.10 = (bf16[128,768]{1,0:T(8,128)(2,1)S(1)}, bf16[128,768]{1,0:T(8,128)(2,1)}, u32[]{:S(2)}, u32[]{:S(2)}) collective-permute-start(bf16[128,768]{1,0:T(8,128)(2,1)S(1)} %copy-done.1), channel_id=1, source_target_pairs={{0,1},{1,0},{2,6},{3,7},{4,5},{5,4},{6,2},{7,3},{8,9},{9,8},{10,14... | collective-permute-start | bytes 589832 | tf_op jit(solution)/shard_map/ppermute | solution.py:570
  32.6 17.4 %collective-permute-start.22 = (bf16[128,768]{1,0:T(8,128)(2,1)S(1)}, bf16[128,768]{1,0:T(8,128)(2,1)S(1)}, u32[]{:S(2)}, u32[]{:S(2)}) collective-permute-start(bf16[128,768]{1,0:T(8,128)(2,1)S(1)} %copy-done.1), channel_id=1, source_target_pairs={{0,2},{1,3},{2,0},{3,1},{4,6},{5,7},{6,4},{7,5},{8,10},{9,11},{10,... | collective-permute-start | bytes 589832 | tf_op jit(solution)/shard_map/ppermute | solution.py:570
  32.7 6.9 %collective-permute-start.4 = (bf16[128,768]{1,0:T(8,128)(2,1)S(1)}, bf16[128,768]{1,0:T(8,128)(2,1)S(1)}, u32[]{:S(2)}, u32[]{:S(2)}) collective-permute-start(bf16[128,768]{1,0:T(8,128)(2,1)S(1)} %collective-permute-done.3.refs_4_), channel_id=1, source_target_pairs={{0,4},{1,5},{2,3},{3,2},{4,0},{5,1},{6,7},{7,6},{8,12},{9,13},{10,... | collective-permute-start | bytes 589832 | tf_op jit(solution)/shard_map/ppermute | solution.py:570
  38.0 13.5 %collective-permute-start.15 = (bf16[128,768]{1,0:T(8,128)(2,1)}, bf16[128,768]{1,0:T(8,128)(2,1)S(1)}, u32[]{:S(2)}, u32[]{:S(2)}) collective-permute-start(bf16[128,768]{1,0:T(8,128)(2,1)} %collective-permute-done.14.refs_8_), channel_id=1, source_target_pairs={{0,4},{1,5},{2,3},{3,2},{4,0},{5,1},{6,7},{7,6},{8,12},{9,13},{10,... | collective-permute-start | bytes 589832 | tf_op jit(solution)/shard_map/ppermute | solution.py:570
  39.5 13.6 %collective-permute-start.19 = (bf16[128,768]{1,0:T(8,128)(2,1)}, bf16[128,768]{1,0:T(8,128)(2,1)S(1)}, u32[]{:S(2)}, u32[]{:S(2)}) collective-permute-start(bf16[128,768]{1,0:T(8,128)(2,1)} %collective-permute-done.18.refs_12_), channel_id=1, source_target_pairs={{0,4},{1,5},{2,3},{3,2},{4,0},{5,1},{6,7},{7,6},{8,12},{9,13},{10,... | collective-permute-start | bytes 589832 | tf_op jit(solution)/shard_map/ppermute | solution.py:570
  40.2 14.5 %collective-permute-start.5 = (bf16[96,768]{1,0:T(8,128)(2,1)S(1)}, bf16[96,768]{1,0:T(8,128)(2,1)S(1)}, u32[]{:S(2)}, u32[]{:S(2)}) collective-permute-start(bf16[96,768]{1,0:T(8,128)(2,1)S(1)} %pad_maximum_fusion.2), channel_id=1, source_target_pairs={{0,8},{1,9},{2,10},{3,11},{4,12},{5,13},{6,14},{7,15},{8,0},{9,1},... | collective-permute-start | bytes 442376 | tf_op jit(solution)/shard_map/ppermute | solution.py:619
  47.4 21.0 %collective-permute-start.6 = (bf16[96,768]{1,0:T(8,128)(2,1)S(1)}, bf16[96,768]{1,0:T(8,128)(2,1)S(1)}, u32[]{:S(2)}, u32[]{:S(2)}) collective-permute-start(bf16[96,768]{1,0:T(8,128)(2,1)S(1)} %pad_maximum_fusion.2), channel_id=1, source_target_pairs={{0,16},{1,17},{2,18},{3,19},{4,20},{5,21},{6,22},{7,23},{8,24},{9,... | collective-permute-start | bytes 442376 | tf_op jit(solution)/shard_map/ppermute | solution.py:619
  50.1 18.4 %collective-permute-start.7 = (bf16[96,768]{1,0:T(8,128)(2,1)S(1)}, bf16[96,768]{1,0:T(8,128)(2,1)S(1)}, u32[]{:S(2)}, u32[]{:S(2)}) collective-permute-start(bf16[96,768]{1,0:T(8,128)(2,1)S(1)} %pad_maximum_fusion.2), channel_id=1, source_target_pairs={{0,24},{1,25},{2,26},{3,27},{4,28},{5,29},{6,30},{7,31},{8,16},{9,... | collective-permute-start | bytes 442376 | tf_op jit(solution)/shard_map/ppermute | solution.py:619
  51.5 19.3 %collective-permute-start.12 = (bf16[128,768]{1,0:T(8,128)(2,1)S(1)}, bf16[128,768]{1,0:T(8,128)(2,1)S(1)}, u32[]{:S(2)}, u32[]{:S(2)}) collective-permute-start(bf16[128,768]{1,0:T(8,128)(2,1)S(1)} %collective-permute-done.3.refs_4_), channel_id=1, source_target_pairs={{0,1},{1,0},{2,6},{3,7},{4,5},{5,4},{6,2},{7,3},{8,9},{9,8},{10,14... | collective-permute-start | bytes 589832 | tf_op jit(solution)/shard_map/ppermute | solution.py:570
  53.1 18.5 %collective-permute-start.16 = (bf16[128,768]{1,0:T(8,128)(2,1)}, bf16[128,768]{1,0:T(8,128)(2,1)S(1)}, u32[]{:S(2)}, u32[]{:S(2)}) collective-permute-start(bf16[128,768]{1,0:T(8,128)(2,1)} %collective-permute-done.14.refs_8_), channel_id=1, source_target_pairs={{0,1},{1,0},{2,6},{3,7},{4,5},{5,4},{6,2},{7,3},{8,9},{9,8},{10,14... | collective-permute-start | bytes 589832 | tf_op jit(solution)/shard_map/ppermute | solution.py:570
  54.7 17.0 %collective-permute-start.20 = (bf16[128,768]{1,0:T(8,128)(2,1)}, bf16[128,768]{1,0:T(8,128)(2,1)}, u32[]{:S(2)}, u32[]{:S(2)}) collective-permute-start(bf16[128,768]{1,0:T(8,128)(2,1)} %collective-permute-done.18.refs_12_), channel_id=1, source_target_pairs={{0,1},{1,0},{2,6},{3,7},{4,5},{5,4},{6,2},{7,3},{8,9},{9,8},{10,14... | collective-permute-start | bytes 589832 | tf_op jit(solution)/shard_map/ppermute | solution.py:570
  68.4 6.0 %collective-permute-start.26 = (bf16[128,768]{1,0:T(8,128)(2,1)S(1)}, bf16[128,768]{1,0:T(8,128)(2,1)S(1)}, u32[]{:S(2)}, u32[]{:S(2)}) collective-permute-start(bf16[128,768]{1,0:T(8,128)(2,1)S(1)} %collective-permute-done.3.refs_4_), channel_id=1, source_target_pairs={{0,2},{1,3},{2,0},{3,1},{4,6},{5,7},{6,4},{7,5},{8,10},{9,11},{10,... | collective-permute-start | bytes 589832 | tf_op jit(solution)/shard_map/ppermute | solution.py:570
  68.4 6.0 %collective-permute-start.11 = (bf16[128,768]{1,0:T(8,128)(2,1)}, bf16[128,768]{1,0:T(8,128)(2,1)}, u32[]{:S(2)}, u32[]{:S(2)}) collective-permute-start(bf16[128,768]{1,0:T(8,128)(2,1)} %collective-permute-done.9.refs_1_), channel_id=1, source_target_pairs={{0,1},{1,0},{2,6},{3,7},{4,5},{5,4},{6,2},{7,3},{8,9},{9,8},{10,14... | collective-permute-start | bytes 589832 | tf_op jit(solution)/shard_map/ppermute | solution.py:570
  70.9 7.2 %collective-permute-start.30 = (bf16[128,768]{1,0:T(8,128)(2,1)}, bf16[128,768]{1,0:T(8,128)(2,1)}, u32[]{:S(2)}, u32[]{:S(2)}) collective-permute-start(bf16[128,768]{1,0:T(8,128)(2,1)} %collective-permute-done.14.refs_8_), channel_id=1, source_target_pairs={{0,2},{1,3},{2,0},{3,1},{4,6},{5,7},{6,4},{7,5},{8,10},{9,11},{10,... | collective-permute-start | bytes 589832 | tf_op jit(solution)/shard_map/ppermute | solution.py:570
  71.6 7.6 %collective-permute-start.34 = (bf16[128,768]{1,0:T(8,128)(2,1)}, bf16[128,768]{1,0:T(8,128)(2,1)}, u32[]{:S(2)}, u32[]{:S(2)}) collective-permute-start(bf16[128,768]{1,0:T(8,128)(2,1)} %collective-permute-done.18.refs_12_), channel_id=1, source_target_pairs={{0,2},{1,3},{2,0},{3,1},{4,6},{5,7},{6,4},{7,5},{8,10},{9,11},{10,... | collective-permute-start | bytes 589832 | tf_op jit(solution)/shard_map/ppermute | solution.py:570
  71.7 8.1 %collective-permute-start.23 = (bf16[128,768]{1,0:T(8,128)(2,1)}, bf16[128,768]{1,0:T(8,128)(2,1)}, u32[]{:S(2)}, u32[]{:S(2)}) collective-permute-start(bf16[128,768]{1,0:T(8,128)(2,1)} %collective-permute-done.9.refs_1_), channel_id=1, source_target_pairs={{0,2},{1,3},{2,0},{3,1},{4,6},{5,7},{6,4},{7,5},{8,10},{9,11},{10,... | collective-permute-start | bytes 589832 | tf_op jit(solution)/shard_map/ppermute | solution.py:570
  74.4 6.5 %collective-permute-start.24 = (bf16[128,768]{1,0:T(8,128)(2,1)}, bf16[128,768]{1,0:T(8,128)(2,1)}, u32[]{:S(2)}, u32[]{:S(2)}) collective-permute-start(bf16[128,768]{1,0:T(8,128)(2,1)} %collective-permute-done.10.refs_2_), channel_id=1, source_target_pairs={{0,2},{1,3},{2,0},{3,1},{4,6},{5,7},{6,4},{7,5},{8,10},{9,11},{10,... | collective-permute-start | bytes 589832 | tf_op jit(solution)/shard_map/ppermute | solution.py:570
  74.4 24.3 %collective-permute-start.8 = (bf16[384,768]{1,0:T(8,128)(2,1)S(1)}, bf16[384,768]{1,0:T(8,128)(2,1)S(1)}, u32[]{:S(2)}, u32[]{:S(2)}) collective-permute-start(bf16[384,768]{1,0:T(8,128)(2,1)S(1)} %pad_maximum_fusion), channel_id=1, source_target_pairs={{0,2},{1,3},{2,0},{3,1},{4,6},{5,7},{6,4},{7,5},{8,10},{9,11},{10,... | collective-permute-start | bytes 1769480 | tf_op jit(solution)/shard_map/ppermute | solution.py:619
  78.1 5.9 %collective-permute-start.13 = (bf16[128,768]{1,0:T(8,128)(2,1)}, bf16[128,768]{1,0:T(8,128)(2,1)S(1)}, u32[]{:S(2)}, u32[]{:S(2)}) collective-permute-start(bf16[128,768]{1,0:T(8,128)(2,1)} %copy-done.17), channel_id=1, source_target_pairs={{0,1},{1,0},{2,6},{3,7},{4,5},{5,4},{6,2},{7,3},{8,9},{9,8},{10,14... | collective-permute-start | bytes 589832 | tf_op jit(solution)/shard_map/ppermute | solution.py:570
  79.2 17.4 %collective-permute-start.27 = (bf16[128,768]{1,0:T(8,128)(2,1)}, bf16[128,768]{1,0:T(8,128)(2,1)S(1)}, u32[]{:S(2)}, u32[]{:S(2)}) collective-permute-start(bf16[128,768]{1,0:T(8,128)(2,1)} %copy-done.17), channel_id=1, source_target_pairs={{0,2},{1,3},{2,0},{3,1},{4,6},{5,7},{6,4},{7,5},{8,10},{9,11},{10,... | collective-permute-start | bytes 589832 | tf_op jit(solution)/shard_map/ppermute | solution.py:570
  79.8 10.5 %collective-permute-start.17 = (bf16[128,768]{1,0:T(8,128)(2,1)}, bf16[128,768]{1,0:T(8,128)(2,1)}, u32[]{:S(2)}, u32[]{:S(2)}) collective-permute-start(bf16[128,768]{1,0:T(8,128)(2,1)} %copy-done.18), channel_id=1, source_target_pairs={{0,1},{1,0},{2,6},{3,7},{4,5},{5,4},{6,2},{7,3},{8,9},{9,8},{10,14... | collective-permute-start | bytes 589832 | tf_op jit(solution)/shard_map/ppermute | solution.py:570
  80.9 15.7 %collective-permute-start.21 = (bf16[128,768]{1,0:T(8,128)(2,1)}, bf16[128,768]{1,0:T(8,128)(2,1)}, u32[]{:S(2)}, u32[]{:S(2)}) collective-permute-start(bf16[128,768]{1,0:T(8,128)(2,1)} %copy-done.19), channel_id=1, source_target_pairs={{0,1},{1,0},{2,6},{3,7},{4,5},{5,4},{6,2},{7,3},{8,9},{9,8},{10,14... | collective-permute-start | bytes 589832 | tf_op jit(solution)/shard_map/ppermute | solution.py:570
  84.0 13.2 %collective-permute-start.31 = (bf16[128,768]{1,0:T(8,128)(2,1)}, bf16[128,768]{1,0:T(8,128)(2,1)S(1)}, u32[]{:S(2)}, u32[]{:S(2)}) collective-permute-start(bf16[128,768]{1,0:T(8,128)(2,1)} %copy-done.18), channel_id=1, source_target_pairs={{0,2},{1,3},{2,0},{3,1},{4,6},{5,7},{6,4},{7,5},{8,10},{9,11},{10,... | collective-permute-start | bytes 589832 | tf_op jit(solution)/shard_map/ppermute | solution.py:570
  90.2 7.0 %collective-permute-start.35 = (bf16[128,768]{1,0:T(8,128)(2,1)}, bf16[128,768]{1,0:T(8,128)(2,1)S(1)}, u32[]{:S(2)}, u32[]{:S(2)}) collective-permute-start(bf16[128,768]{1,0:T(8,128)(2,1)} %copy-done.19), channel_id=1, source_target_pairs={{0,2},{1,3},{2,0},{3,1},{4,6},{5,7},{6,4},{7,5},{8,10},{9,11},{10,... | collective-permute-start | bytes 589832 | tf_op jit(solution)/shard_map/ppermute | solution.py:570
  170.8 19.4 %collective-permute-start.44 = (bf16[512,256]{1,0:T(8,128)(2,1)}, bf16[512,256]{1,0:T(8,128)(2,1)S(1)}, u32[]{:S(2)}, u32[]{:S(2)}) collective-permute-start(bf16[512,256]{1,0:T(8,128)(2,1)} %delta.1.refs_0_), channel_id=1, source_target_pairs={{0,8},{1,9},{2,10},{3,11},{4,12},{5,13},{6,14},{7,15},{8,0},{9,1},... | collective-permute-start | bytes 786440 | tf_op jit(solution)/shard_map/ppermute | solution.py:619
  171.9 27.8 %collective-permute-start.45 = (bf16[512,256]{1,0:T(8,128)(2,1)}, bf16[512,256]{1,0:T(8,128)(2,1)S(1)}, u32[]{:S(2)}, u32[]{:S(2)}) collective-permute-start(bf16[512,256]{1,0:T(8,128)(2,1)} %delta.1.refs_0_), channel_id=1, source_target_pairs={{0,16},{1,17},{2,18},{3,19},{4,20},{5,21},{6,22},{7,23},{8,24},{9,... | collective-permute-start | bytes 786440 | tf_op jit(solution)/shard_map/ppermute | solution.py:619
  172.5 27.2 %collective-permute-start.46 = (bf16[512,256]{1,0:T(8,128)(2,1)}, bf16[512,256]{1,0:T(8,128)(2,1)S(1)}, u32[]{:S(2)}, u32[]{:S(2)}) collective-permute-start(bf16[512,256]{1,0:T(8,128)(2,1)} %delta.1.refs_0_), channel_id=1, source_target_pairs={{0,24},{1,25},{2,26},{3,27},{4,28},{5,29},{6,30},{7,31},{8,16},{9,... | collective-permute-start | bytes 786440 | tf_op jit(solution)/shard_map/ppermute | solution.py:619
  175.2 25.0 %collective-permute-start.47 = (bf16[512,256]{1,0:T(8,128)(2,1)}, bf16[512,256]{1,0:T(8,128)(2,1)S(1)}, u32[]{:S(2)}, u32[]{:S(2)}) collective-permute-start(bf16[512,256]{1,0:T(8,128)(2,1)} %delta.1.refs_0_), channel_id=1, source_target_pairs={{0,2},{1,3},{2,0},{3,1},{4,6},{5,7},{6,4},{7,5},{8,10},{9,11},{10,... | collective-permute-start | bytes 786440 | tf_op jit(solution)/shard_map/ppermute | solution.py:619
  190.2 10.0 %collective-permute-start.48 = (bf16[512,256]{1,0:T(8,128)(2,1)S(1)}, bf16[512,256]{1,0:T(8,128)(2,1)S(1)}, u32[]{:S(2)}, u32[]{:S(2)}) collective-permute-start(bf16[512,256]{1,0:T(8,128)(2,1)S(1)} %collective-permute-done.44.refs_1_), channel_id=1, source_target_pairs={{0,2},{1,3},{2,0},{3,1},{4,6},{5,7},{6,4},{7,5},{8,10},{9,11},{10,... | collective-permute-start | bytes 786440 | tf_op jit(solution)/shard_map/ppermute | solution.py:619
  253.5 6.5 %collective-permute-start.51 = (bf16[128,768]{1,0:T(8,128)(2,1)}, bf16[128,768]{1,0:T(8,128)(2,1)S(1)}, u32[]{:S(2)}, u32[]{:S(2)}) collective-permute-start(bf16[128,768]{1,0:T(8,128)(2,1)} %get-tuple-element.55), channel_id=1, source_target_pairs={{0,1},{1,0},{2,3},{3,2},{4,5},{5,4},{6,7},{7,6},{8,9},{9,8},{10,11... | collective-permute-start | bytes 589832 | tf_op jit(solution)/shard_map/ppermute | solution.py:619
  254.6 5.9 %collective-permute-start.52 = (bf16[128,768]{1,0:T(8,128)(2,1)}, bf16[128,768]{1,0:T(8,128)(2,1)S(1)}, u32[]{:S(2)}, u32[]{:S(2)}) collective-permute-start(bf16[128,768]{1,0:T(8,128)(2,1)} %get-tuple-element.56), channel_id=1, source_target_pairs={{0,4},{1,5},{2,6},{3,7},{4,0},{5,1},{6,2},{7,3},{8,12},{9,13},{10,... | collective-permute-start | bytes 589832 | tf_op jit(solution)/shard_map/ppermute | solution.py:619
  256.1 6.8 %collective-permute-start.53 = (bf16[128,768]{1,0:T(8,128)(2,1)}, bf16[128,768]{1,0:T(8,128)(2,1)S(1)}, u32[]{:S(2)}, u32[]{:S(2)}) collective-permute-start(bf16[128,768]{1,0:T(8,128)(2,1)} %get-tuple-element.57), channel_id=1, source_target_pairs={{0,5},{1,4},{2,7},{3,6},{4,1},{5,0},{6,3},{7,2},{8,13},{9,12},{10,... | collective-permute-start | bytes 589832 | tf_op jit(solution)/shard_map/ppermute | solution.py:619
  274.2 6.2 %collective-permute-start.56 = (f32[40,768]{1,0:T(8,128)S(1)}, f32[40,768]{1,0:T(8,128)S(1)}, u32[]{:S(2)}, u32[]{:S(2)}) collective-permute-start(f32[40,768]{1,0:T(8,128)S(1)} %get-tuple-element.76), channel_id=1, source_target_pairs={{0,4},{1,5},{2,6},{3,7},{4,0},{5,1},{6,2},{7,3},{8,12},{9,13},{10,... | collective-permute-start | bytes 368648 | tf_op jit(solution)/shard_map/ppermute | solution.py:619
  275.7 6.6 %collective-permute-start.57 = (f32[40,768]{1,0:T(8,128)S(1)}, f32[40,768]{1,0:T(8,128)S(1)}, u32[]{:S(2)}, u32[]{:S(2)}) collective-permute-start(f32[40,768]{1,0:T(8,128)S(1)} %get-tuple-element.75), channel_id=1, source_target_pairs={{0,5},{1,4},{2,7},{3,6},{4,1},{5,0},{6,3},{7,2},{8,13},{9,12},{10,... | collective-permute-start | bytes 368648 | tf_op jit(solution)/shard_map/ppermute | solution.py:619
  282.3 6.7 %collective-permute-start.58 = (f32[40,768]{1,0:T(8,128)S(1)}, f32[40,768]{1,0:T(8,128)S(1)}, u32[]{:S(2)}, u32[]{:S(2)}) collective-permute-start(f32[40,768]{1,0:T(8,128)S(1)} %fusion.7), channel_id=1, source_target_pairs={{0,8},{1,9},{2,10},{3,11},{4,12},{5,13},{6,14},{7,15},{8,0},{9,1},... | collective-permute-start | bytes 368648 | tf_op jit(solution)/shard_map/ppermute | solution.py:619
  282.4 11.9 %collective-permute-start.59 = (f32[40,768]{1,0:T(8,128)S(1)}, f32[40,768]{1,0:T(8,128)S(1)}, u32[]{:S(2)}, u32[]{:S(2)}) collective-permute-start(f32[40,768]{1,0:T(8,128)S(1)} %fusion.7), channel_id=1, source_target_pairs={{0,16},{1,17},{2,18},{3,19},{4,20},{5,21},{6,22},{7,23},{8,24},{9,... | collective-permute-start | bytes 368648 | tf_op jit(solution)/shard_map/ppermute | solution.py:619
  282.5 11.9 %collective-permute-start.60 = (f32[40,768]{1,0:T(8,128)S(1)}, f32[40,768]{1,0:T(8,128)S(1)}, u32[]{:S(2)}, u32[]{:S(2)}) collective-permute-start(f32[40,768]{1,0:T(8,128)S(1)} %fusion.7), channel_id=1, source_target_pairs={{0,24},{1,25},{2,26},{3,27},{4,28},{5,29},{6,30},{7,31},{8,16},{9,... | collective-permute-start | bytes 368648 | tf_op jit(solution)/shard_map/ppermute | solution.py:619
  294.4 5.8 %collective-permute-start.61 = (f32[40,768]{1,0:T(8,128)S(1)}, f32[40,768]{1,0:T(8,128)S(1)}, u32[]{:S(2)}, u32[]{:S(2)}) collective-permute-start(f32[40,768]{1,0:T(8,128)S(1)} %add_add_fusion.refs_0_), channel_id=1, source_target_pairs={{0,1},{1,0},{2,3},{3,2},{4,5},{5,4},{6,7},{7,6},{8,9},{9,8},{10,11... | collective-permute-start | bytes 368648 | tf_op jit(solution)/shard_map/ppermute | solution.py:619
  296.9 5.8 %collective-permute-start.63 = (f32[40,768]{1,0:T(8,128)S(1)}, f32[40,768]{1,0:T(8,128)S(1)}, u32[]{:S(2)}, u32[]{:S(2)}) collective-permute-start(f32[40,768]{1,0:T(8,128)S(1)} %add_add_fusion.refs_0_), channel_id=1, source_target_pairs={{0,5},{1,4},{2,7},{3,6},{4,1},{5,0},{6,3},{7,2},{8,13},{9,12},{10,... | collective-permute-start | bytes 368648 | tf_op jit(solution)/shard_map/ppermute | solution.py:619
  (74 other events, 385.4 us)
Sparse Core Ops, SparseCore 0:
  13.0 110.7 all-gather.2
  126.7 66.0 all-gather.4
where the time goes:
time: 321 us; the launch traced here: 320 us
  Pallas kernels  110 us (34%)
  waiting for transfers between devices  91.1 us (28%)
  starting transfers between devices  66 us (21%)
  local copies, waits for them, and re-layouts  31.6 us (10%)
  between operations  16 us (5%)
  other arithmetic  5.41 us (2%)
    ppermute x37, waiting for transfers between devices, swap(): lax.ppermute(value, AXES, [(j, j ^ mask) for j in range(device_total)])  69.3 us
    pallas_call x1, Pallas kernels, shards(): pl.pallas_call(backward_kernel, in_specs=[SMEM, SMEM] + [VMEM] * (3 + len...  51.2 us
    ppermute x37, starting transfers between devices, swap(): lax.ppermute(value, AXES, [(j, j ^ mask) for j in range(device_total)])  42 us
    pallas_call x1, Pallas kernels, shards(): pl.pallas_call(gathered_kernel, in_specs=[SMEM, SMEM] + [VMEM] * (3 + len...  32.2 us
    ppermute x31, starting transfers between devices, send(): lax.ppermute(piece, AXES, [(j, j ^ (odd if j >> 1 & 1 else even)) for j i...  23.8 us
    ppermute x31, waiting for transfers between devices, send(): lax.ppermute(piece, AXES, [(j, j ^ (odd if j >> 1 & 1 else even)) for j i...  21.8 us
    pallas_call x1, Pallas kernels, shards(): pl.pallas_call(middle, in_specs=[SMEM] + [VMEM] * (4 + count), out_specs=...  15 us
    unnamed x114, local copies, waits for them, and re-layouts  9.41 us
  transfers between devices with their start and end apart: 70, of which 31 were waited for; matrix products, arithmetic and copies ran while one was open for 6% of the time, Pallas kernels for 32%

commit v1 on v0

v1 whole, which is shorter than its diff:
```python
import functools

import jax
import jax.numpy as jnp
from jax import lax
from jax.experimental import pallas as pl
from jax.experimental.pallas import tpu as pltpu
from jax.sharding import PartitionSpec as P

D = 768
HEADS = 12
HDIM = 64
BLOCK = 64
ADAPTERS = 8
RANK = 16
FF = 3072

PEERS = (0, 8, 16, 24)
PLANE = (0, 1, 4, 5)
GROUP_HEADS = HEADS // 4
SHARE = GROUP_HEADS * HDIM
WIDE = 256
LSE_LANE = SHARE
DEL_LANE = SHARE + 9
MASK_LANE = SHARE + 18
FLOOR = -1e30
STACK = GROUP_HEADS * BLOCK
AXES = ("seq", "head")
norm_eps = 1e-12
f32 = jnp.float32
bf16 = jnp.bfloat16
VMEM_LIMIT = 60 * 1024 * 1024


def dense_mul(left_op, right_op):
    return jnp.dot(left_op, right_op, preferred_element_type=f32)


def dense_right_t(left_op, right_op):
    return lax.dot_general(left_op, right_op, (((1,), (1,)), ((), ())), preferred_element_type=f32)


def dense_left_t(left_op, right_op):
    return lax.dot_general(left_op, right_op, (((0,), (0,)), ((), ())), preferred_element_type=f32)


def lanes(rows):
    return lax.broadcasted_iota(jnp.int32, (rows, WIDE), 1)


def head_lanes(lane, head):
    return (lane >= HDIM * head) & (lane < HDIM * (head + 1))


def part_lanes(lane, first, head):
    return (lane >= first + 3 * head) & (lane < first + 3 * head + 3)


def project_rows(raw, u_ref):
    lane = lanes(raw.shape[0])
    data = lane < SHARE

    def part(j):
        piece = raw[:, WIDE * j : WIDE * (j + 1)]
        return (piece + dense_mul(piece[:, WIDE // 2 :].astype(bf16), u_ref[j])).astype(bf16).astype(f32)

    query = jnp.where(data, part(0) * 0.125, jnp.where(lane == MASK_LANE, 1.0, 0.0)).astype(bf16)
    return query, jnp.concatenate([part(1)[:, :SHARE], part(2)[:, :SHARE]], axis=1).astype(bf16)


def widen_pair(pair, position, seq_length):
    lane = lanes(pair.shape[0])
    data = lane < SHARE
    blank = jnp.zeros((pair.shape[0], WIDE - SHARE), bf16)
    key = jnp.concatenate([pair[:, :SHARE], blank], axis=1)
    value = jnp.concatenate([pair[:, SHARE:], blank], axis=1)
    mask = jnp.where(position < seq_length, 0.0, FLOOR)
    key_side = jnp.where(lane < DEL_LANE, 1.0, jnp.where(lane == MASK_LANE, mask, 0.0)).astype(bf16)
    value_side = jnp.where((lane >= DEL_LANE) & (lane < MASK_LANE), 1.0, 0.0).astype(bf16)
    return jnp.where(data, key, key_side), jnp.where(data, value, value_side)


def slab_offset(n, place, fast):
    if not fast:
        return (n & 7) | ((n >> 3) << 5)
    core = (place >> 1) & 1
    near = 4 - 3 * core if n < 4 else 1 + 3 * core
    return (0, near, 5 - near, 5)[n % 4] ^ (2 * (n // 4))


def slab_row(offset):
    return (offset & 7) | ((offset >> 5) << 3)


def plane_quarter(place):
    return (place & 1) | ((place >> 1) & 2)


def rand_at(fast, rand_ref, block, r):
    if not fast:
        return rand_ref[block * 3 + r]
    return rand_ref[(block // 4) * 2, WIDE // 4 + (block & 3) * 3 + r]


def pack_kernel(rand_ref, query_ref, key_ref, value_ref, output_ref, inner_ref, outer_ref, late_ref, *slice_refs):
    slab = query_ref.shape[0]
    group = ((lax.axis_index("seq") * lax.axis_size("head") + lax.axis_index("head")) >> 3) & 3
    late_ref[:, :D] = output_ref[...]
    late_ref[:, D : D + FF] = inner_ref[...]
    outer = outer_ref[...].astype(f32)
    for c in range(FF // D):
        late_ref[:, D + FF + D * c : D + FF + D * (c + 1)] = outer[slab * c : slab * (c + 1)].astype(bf16)
    spare = (slab, WIDE - SHARE)
    lane = lax.broadcasted_iota(jnp.int32, spare, 1)
    marks = jnp.zeros(spare, f32)
    for n in range(12):
        marks = jnp.where(lane == n, rand_ref[n // 3, n % 3].astype(f32), marks)
    marks = jnp.where(lax.broadcasted_iota(jnp.int32, spare, 0) == 0, marks, 0.0)
    sources = [ref[...].astype(f32) for ref in (query_ref, key_ref, value_ref)]
    for p in range(4):
        pieces = []
        for source in sources:
            mine = source[:, :SHARE]
            for g in range(1, 4):
                mine = jnp.where((group ^ p) == g, source[:, SHARE * g : SHARE * (g + 1)], mine)
            pieces += [mine, marks]
        slice_refs[p][...] = jnp.concatenate(pieces, axis=1).astype(bf16)


def put_tokens(fast, token_refs, tok_ref):
    rows = 2 * BLOCK
    if fast:
        own, far, near = token_refs
        parts = [own[...], near[:rows, :], far[...], near[rows:, :]]
    else:
        parts = [ref[...] for ref in token_refs]
    for a in range(4):
        tok_ref[rows * a : rows * (a + 1), :] = parts[a]


def project_kernel(fast, meta_ref, down_ref, up_ref, *refs):
    count = 3 if fast else 4
    tok_refs, refs = refs[:count], refs[count:]
    w_refs, (w_ref, u_ref, q_ref, pair_ref, rand_ref, tok_ref, wide_ref) = refs[:-7], refs[-7:]
    place = meta_ref[0]
    group = meta_ref[2]
    chosen = meta_ref[3]
    half = WIDE // 2
    lead = WIDE // 4
    rand_ref[...] = jnp.zeros_like(rand_ref)
    if fast:
        slab = D // 32
        for n, piece in enumerate(w_refs):
            rows = piece[...].astype(f32)
            for a in range(4):
                device = place ^ slab_offset(n, place, fast) ^ PEERS[a]
                wide_ref[pl.ds(pl.multiple_of(device * slab, 8), slab), :] = rows[slab * a : slab * (a + 1)]
                rand_ref[pl.ds(device, 1), :] = rows[slab * a : slab * a + 1, half:WIDE].astype(jnp.int32)
    else:
        wide_ref[...] = w_refs[0][...].astype(f32)
    own = lax.broadcasted_iota(jnp.int32, (D, half), 1) < lead
    above = jnp.zeros((lead, D), f32)
    below = jnp.zeros((half - lead - RANK, D), f32)
    side = jnp.zeros((RANK, WIDE - SHARE), f32)
    for j in range(3):
        low = slice(WIDE * j, WIDE * j + half)
        high = slice(WIDE * j + half, WIDE * (j + 1))
        turned = jnp.concatenate([above, down_ref[chosen, j].astype(f32), below], axis=0).T
        w_ref[:, low] = wide_ref[:, low].astype(bf16)
        w_ref[:, high] = jnp.where(own, wide_ref[:, high], turned).astype(bf16)
        up = up_ref[chosen, j].astype(f32)
        mine = jnp.zeros((RANK, SHARE), f32)
        for g in range(4):
            mine = mine + jnp.where(group == g, up[:, SHARE * g : SHARE * (g + 1)], 0.0)
        mine = jnp.concatenate([mine, side], axis=1)
        u_ref[j] = jnp.concatenate([above[:, :WIDE], mine, below[:, :WIDE]], axis=0).astype(bf16)
    put_tokens(fast, tok_refs, tok_ref)
    q_ref[...], pair_ref[...] = project_rows(dense_mul(tok_ref[...], w_ref[...]), u_ref)


def block_rows(ref, block, count=1):
    return ref[pl.ds(pl.multiple_of(block * BLOCK, BLOCK), count * BLOCK), :]


def merge_heads(stacked):
    lane = lanes(BLOCK)
    total = jnp.zeros((BLOCK, WIDE), f32)
    for head in range(GROUP_HEADS):
        total = jnp.where(head_lanes(lane, head), stacked[BLOCK * head : BLOCK * (head + 1)], total)
    return total


def key_set(ref, picks, block, block_total, fill):
    own = block_rows(ref, block)
    left = block_rows(ref, jnp.maximum(block - 1, 0))
    right = block_rows(ref, jnp.minimum(block + 1, block_total - 1))
    if fill:
        blank = jnp.where(lanes(BLOCK) == MASK_LANE, FLOOR, 0.0).astype(bf16)
        left = jnp.where(block - 1 >= 2, left, blank)
        right = jnp.where(block + 1 < block_total, right, blank)
    rand = [block_rows(ref, pick) for pick in picks]
    return jnp.concatenate([own, left, right, block_rows(ref, 0, 2)] + rand, axis=0)


def own_block(place, t):
    return 2 * (place ^ PEERS[t // 2]) + t % 2


def attend_kernel(fast, meta_ref, rand_ref, q_ref, *refs):
    slab_refs, (k_ref, v_ref, *ctx_refs, aux_ref, s_ref) = refs[:-8], refs[-8:]
    place = meta_ref[0]
    piece = 2 * BLOCK
    for n, slab_ref in enumerate(slab_refs):
        for a in range(4):
            device = place ^ slab_offset(n, place, fast) ^ PEERS[a]
            here = pl.ds(pl.multiple_of(device * piece, piece), piece)
            position = device * piece + lax.broadcasted_iota(jnp.int32, (piece, WIDE), 0)
            k_ref[here, :], v_ref[here, :] = widen_pair(
                slab_ref[piece * a : piece * (a + 1), :], position, meta_ref[1]
            )
    total_rows = k_ref.shape[0]
    block_total = total_rows // BLOCK
    chunks = total_rows // (8 * BLOCK)

    def queries(t):
        rows = q_ref[pl.ds(t * BLOCK, BLOCK), :]
        lane = lanes(BLOCK)
        blank = jnp.zeros_like(rows)
        return jnp.concatenate(
            [
                jnp.where(head_lanes(lane, head) | (lane == MASK_LANE), rows, blank)
                for head in range(GROUP_HEADS)
            ],
            axis=0,
        )

    def finish(t, low, exact, top, total):
        lane = lanes(BLOCK)
        rows = pl.ds(t * BLOCK, BLOCK)
        ctx_refs[t // 2][pl.ds((t % 2) * BLOCK, BLOCK), :] = merge_heads(low).astype(bf16)
        aux = merge_heads(exact)
        lse = top + jnp.log(total)
        for head in range(GROUP_HEADS):
            aux = jnp.where(lane == LSE_LANE + head, lse[BLOCK * head : BLOCK * (head + 1)], aux)
        aux_ref[rows, :] = aux

    def split(probs):
        low = probs.astype(bf16)
        return low, (probs - low.astype(f32)).astype(bf16)

    def sparse(t):
        block = own_block(place, t)
        picks = [rand_at(fast, rand_ref, block, r) for r in range(3)]
        scores = dense_right_t(queries(t), key_set(k_ref, picks, block, block_total, True))
        top = jnp.max(scores, axis=1, keepdims=True)
        weights = jnp.exp(scores - top)
        total = jnp.sum(weights, axis=1, keepdims=True)
        low, rest = split(weights * (1.0 / total))
        values = key_set(v_ref, picks, block, block_total, False)
        context = dense_mul(low, values)
        return context, context + dense_mul(rest, values), top, total

    for a in range(4):

        @pl.when((place ^ PEERS[a]) != 0)
        def _(a=a):
            results = [sparse(2 * a), sparse(2 * a + 1)]
            finish(2 * a, *results[0])
            finish(2 * a + 1, *results[1])

    at_once = s_ref.shape[1] // STACK

    def full(a, first):
        stack = jnp.concatenate([queries(2 * a + first + n) for n in range(at_once)], axis=0)
        height = at_once * STACK

        def score(c, state):
            top, total, tops = state
            part = dense_right_t(stack, block_rows(k_ref, c * 8, 8))
            here = jnp.max(part, axis=1, keepdims=True)
            weights = jnp.exp(part - here)
            s_ref[c] = weights
            later = jnp.maximum(top, here)
            total = total * jnp.exp(top - later) + jnp.sum(weights, axis=1, keepdims=True) * jnp.exp(here - later)
            return later, total, jnp.where(turn == c, here, tops)

        turn = lax.broadcasted_iota(jnp.int32, (height, 128), 1)
        top, total, tops = lax.fori_loop(
            0,
            chunks,
            score,
            (jnp.full((height, 1), FLOOR, f32), jnp.zeros((height, 1), f32), jnp.full((height, 128), FLOOR, f32)),
        )
        scales = jnp.exp(tops - top) * (1.0 / total)

        def mix(c, state):
            scale = jnp.sum(jnp.where(turn == c, scales, 0.0), axis=1, keepdims=True)
            low, rest = split(s_ref[c] * scale)
            values = block_rows(v_ref, c * 8, 8)
            return (state[0] + dense_mul(low, values), state[1] + dense_mul(rest, values))

        zero = jnp.zeros((height, WIDE), f32)
        context, rest = lax.fori_loop(0, chunks, mix, (zero, zero))
        for n in range(at_once):
            here = slice(STACK * n, STACK * (n + 1))
            finish(2 * a + first + n, context[here], (context + rest)[here], top[here], total[here])

    for a in range(4):

        @pl.when((place ^ PEERS[a]) == 0)
        def _(a=a):
            for first in range(0, 2, at_once):
                full(a, first)


def split_parts(value):
    high = value.astype(bf16).astype(f32)
    middle = (value - high).astype(bf16).astype(f32)
    return (high, middle, value - high - middle)


def delta_kernel(*refs):
    grad_refs, aux_ref, out_ref = refs[:4], refs[4], refs[5]
    rows = 2 * BLOCK
    lane = lanes(rows)
    for a in range(4):
        here = pl.ds(a * rows, rows)
        grad = grad_refs[a][...].astype(f32)
        aux = aux_ref[here, :]
        result = jnp.where(lane < SHARE, grad, 0.0)
        product = grad * aux
        for head in range(GROUP_HEADS):
            delta = jnp.sum(jnp.where(head_lanes(lane, head), product, 0.0), axis=1, keepdims=True)
            lse = jnp.sum(jnp.where(lane == LSE_LANE + head, aux, 0.0), axis=1, keepdims=True)
            for p, value in enumerate(split_parts(lse)):
                result = jnp.where(lane == LSE_LANE + 3 * head + p, -value, result)
            for p, value in enumerate(split_parts(delta)):
                result = jnp.where(lane == DEL_LANE + 3 * head + p, -value, result)
        out_ref[here, :] = result.astype(bf16)


def query_stacks(rows, grads):
    lane = lanes(BLOCK)
    blank = jnp.zeros_like(rows)
    queries = []
    outers = []
    for head in range(GROUP_HEADS):
        here = head_lanes(lane, head)
        queries.append(
            jnp.where(
                here | (lane == MASK_LANE), rows, jnp.where(part_lanes(lane, LSE_LANE, head), grads, blank)
            )
        )
        outers.append(jnp.where(here | part_lanes(lane, DEL_LANE, head), grads, blank))
    return jnp.concatenate(queries, axis=0), jnp.concatenate(outers, axis=0)


def near_kernel(fast, meta_ref, rand_ref, q_ref, k_ref, v_ref, g_ref, dq_ref, *refs):
    zero_outs, (blank_ref, sems) = refs[:-2], refs[-2:]
    place = meta_ref[0]
    block_total = k_ref.shape[0] // BLOCK
    copies = []
    if zero_outs:
        blank_ref[...] = jnp.zeros_like(blank_ref)
        for n, where in enumerate(zero_outs):
            shape = where.shape
            source = blank_ref if len(shape) == 4 else blank_ref.at[0 : shape[2] // D]
            for adapter in range(ADAPTERS):
                if len(shape) == 4:
                    copies.append((blank_ref, where.at[adapter], n))
                else:
                    for c in range(shape[2] // D):
                        copies.append((blank_ref.at[c], where.at[adapter, :, pl.ds(D * c, D)], n))
        copies = [pltpu.make_async_copy(source, where, sems.at[n]) for n, (source, where, _) in enumerate(copies)]
        for copy in copies:
            copy.start()

    def query_side(stack, outer, keys, values):
        probs = jnp.exp(dense_right_t(stack, keys))
        scored = (probs * dense_right_t(outer, values)).astype(bf16)
        return dense_mul(scored, keys)

    def put_query(t, stacked):
        dq_ref[pl.ds(t * BLOCK, BLOCK), :] = (merge_heads(stacked) * 0.125).astype(bf16)

    def stacks(t):
        here = slice(t * BLOCK, (t + 1) * BLOCK)
        return query_stacks(q_ref[here, :], g_ref[here, :])

    def sparse(t):
        block = own_block(place, t)
        picks = [rand_at(fast, rand_ref, block, r) for r in range(3)]
        return query_side(
            *stacks(t),
            key_set(k_ref, picks, block, block_total, True),
            key_set(v_ref, picks, block, block_total, False),
        )

    for a in range(4):

        @pl.when((place ^ PEERS[a]) != 0)
        def _(a=a):
            results = [sparse(2 * a), sparse(2 * a + 1)]
            put_query(2 * a, results[0])
            put_query(2 * a + 1, results[1])

        @pl.when((place ^ PEERS[a]) == 0)
        def _(a=a):
            pairs = [stacks(2 * a), stacks(2 * a + 1)]
            stack = jnp.concatenate([pair[0] for pair in pairs], axis=0)
            outer = jnp.concatenate([pair[1] for pair in pairs], axis=0)

            def add(c, total):
                return total + query_side(stack, outer, block_rows(k_ref, c * 8, 8), block_rows(v_ref, c * 8, 8))

            total = lax.fori_loop(0, block_total // 8, add, jnp.zeros((2 * STACK, WIDE), f32))
            put_query(2 * a, total[:STACK])
            put_query(2 * a + 1, total[STACK:])

    for copy in copies:
        copy.wait()


def far_kernel(fast, meta_ref, rand_ref, k_ref, v_ref, dq_ref, w_ref, u_ref, early_ref, *refs):
    count = 3 if fast else 4
    tok_refs, refs = refs[:count], refs[count:]
    slab_refs, refs = refs[:-14], refs[-14:]
    part_refs, near_ref, away_ref, refs = refs[:4], refs[4], refs[5], refs[6:]
    q_ref, g_ref, dk_ref, dv_ref, grad_ref, tok_ref, terms_ref, pair_ref = refs
    place = meta_ref[0]
    group = meta_ref[2]
    block_total = k_ref.shape[0] // BLOCK
    count = len(slab_refs) // 2
    rows = 2 * BLOCK
    for n in range(count):
        here = pl.ds(pl.multiple_of(slab_row(slab_offset(n, place, fast)) * 4 * rows, rows), 4 * rows)
        q_ref[here, :] = slab_refs[n][...]
        g_ref[here, :] = slab_refs[count + n][...]

    def stacks(blocks):
        pairs = []
        for block in blocks:
            other = (block // 2) ^ place
            where = slab_row(other) * 8 + ((other >> 3) & 3) * 2 + (block & 1)
            pairs.append(query_stacks(block_rows(q_ref, where), block_rows(g_ref, where)))
        return (
            jnp.concatenate([pair[0] for pair in pairs], axis=0),
            jnp.concatenate([pair[1] for pair in pairs], axis=0),
        )

    def key_side(keys, values, blocks, allowed):
        stack, outer = stacks(blocks)
        probs = jnp.exp(dense_right_t(keys, stack))
        if allowed is not None:
            probs = jnp.where(allowed, probs, 0.0)
        scored = (probs * dense_right_t(values, outer)).astype(bf16)
        return dense_mul(scored, stack), dense_mul(probs.astype(bf16), outer)

    def put(here, grads):
        dk_ref[here, :] += grads[0]
        dv_ref[here, :] += grads[1]

    key_local = lax.broadcasted_iota(jnp.int32, (rows, 6 * STACK), 0) // BLOCK
    turn = lax.broadcasted_iota(jnp.int32, (rows, 6 * STACK), 1) // STACK
    for a in range(4):
        first = 2 * (place ^ PEERS[a])
        here = slice(rows * a, rows * (a + 1))
        blocks = [0, 1, jnp.maximum(first - 1, 0), first, first + 1, jnp.minimum(first + 2, block_total - 1)]
        key_block = first + key_local
        block = first - 3 + turn
        near = (key_block - block <= 1) & (block - key_block <= 1) & (block >= 2) & (block < block_total)
        allowed = ((turn < 2) | near) & (key_block >= 2)
        keys = block_rows(k_ref, first, 2)
        values = block_rows(v_ref, first, 2)
        dk_ref[here, :], dv_ref[here, :] = key_side(keys, values, blocks, allowed)

    def collect(block, count):
        for r in range(3):
            target = rand_at(fast, rand_ref, block, r)
            mine = (((target // 2) ^ place) & ~24) == 0

            @pl.when(mine)
            def _(target=target, count=count):
                pair_ref[count] = target * 65536 + block

            count = count + mine.astype(jnp.int32)
        return count

    pair_total = lax.fori_loop(2, block_total, collect, jnp.int32(0))

    def random_pairs(step, carry):
        grads = []
        for k in range(4):
            number = 4 * step + k
            live = number < pair_total
            code = pair_ref[jnp.minimum(number, pair_total - 1)]
            target = code // 65536
            block = code - target * 65536
            start = ((((target // 2) ^ place) >> 3) & 3) * rows + (target & 1) * BLOCK
            grads.append(
                (
                    pl.ds(pl.multiple_of(start, BLOCK), BLOCK),
                    key_side(block_rows(k_ref, target), block_rows(v_ref, target), (block,), live),
                )
            )
        for here, parts in grads:
            put(here, parts)
        return carry

    lax.fori_loop(0, (pair_total + 3) // 4, random_pairs, 0)

    @pl.when((place & ~24) == 0)
    def _():
        here = pl.ds(pl.multiple_of(group * rows, rows), rows)
        keys = block_rows(k_ref, 0, 2)
        values = block_rows(v_ref, 0, 2)

        def every(step, carry):
            put(here, key_side(keys, values, [4 * step + k for k in range(4)], None))
            return carry

        lax.fori_loop(0, block_total // 4, every, 0)

    data = lanes(rows) < SHARE
    for a in range(4):
        here = slice(rows * a, rows * (a + 1))
        grad_ref[here, :WIDE] = dq_ref[here, :]
        grad_ref[here, WIDE : 2 * WIDE] = jnp.where(data, dk_ref[here, :], 0.0).astype(bf16)
        grad_ref[here, 2 * WIDE :] = jnp.where(data, dv_ref[here, :], 0.0).astype(bf16)
    put_tokens(fast, tok_refs, tok_ref)
    tokens = tok_ref[...]
    lead = WIDE // 4
    terms = []
    ups = []
    for j in range(3):
        high = slice(WIDE * j + WIDE // 2, WIDE * (j + 1))
        grad = grad_ref[:, WIDE * j : WIDE * (j + 1)]
        reduced = dense_mul(tokens, w_ref[:, high]).astype(bf16)
        grad_reduced = dense_right_t(grad, u_ref[j]).astype(bf16)
        terms.append(dense_left_t(grad_reduced, tokens)[lead : lead + RANK])
        up = dense_left_t(reduced, grad)[lead : lead + RANK, :SHARE]
        ups.append(jnp.concatenate([jnp.where(group == g, up, 0.0) for g in range(4)], axis=1))
        grad_ref[:, high] = grad_ref[:, high] + grad_reduced
    terms += ups + [jnp.zeros((RANK, D), f32)] * 2
    core = (place >> 1) & 1
    quarter = plane_quarter(place)
    for part, value in enumerate(terms):
        early = early_ref[EARLY_PART * part : EARLY_PART * (part + 1), :]
        where = (((part // 4) ^ core) * 4 + ((part % 4) ^ quarter)) if fast else part
        terms_ref[where, :RANK] = value
        terms_ref[where, RANK:] = early
    near_ref[...] = terms_ref[:4]
    away_ref[...] = terms_ref[4:].astype(away_ref.dtype)
    for a in range(4):
        part_refs[a][...] = dense_right_t(grad_ref[rows * a : rows * (a + 1), :], w_ref[...]).astype(bf16)


def normal(hidden):
    center = hidden - jnp.mean(hidden, axis=-1, keepdims=True)
    root = lax.rsqrt(jnp.mean(center * center, axis=-1, keepdims=True) + norm_eps)
    return center * root, root


def normal_back(grad, normed, root):
    mean = jnp.mean(grad, axis=-1, keepdims=True)
    return root * (grad - mean - normed * jnp.mean(grad * normed, axis=-1, keepdims=True))


def middle_kernel(
    fast,
    meta_ref,
    ctx_refs,
    tok_ref,
    cot_ref,
    late_hbm,
    gain_ref,
    down_table,
    up_table,
    inner_down_table,
    inner_up_table,
    outer_down_table,
    outer_up_table,
    wide_ref,
    out_ref,
    grad_ref,
    piece_refs,
    terms_ref,
    hold_ref,
    pre_ref,
    act_ref,
    late_ref,
    sems,
):
    group = meta_ref[2]
    chosen = meta_ref[3]
    rows = tok_ref.shape[0]
    down_ref = down_table.at[chosen, 3]
    up_ref = up_table.at[chosen, 3]
    inner_down_ref = inner_down_table.at[chosen]
    inner_up_ref = inner_up_table.at[chosen]
    outer_down_ref = outer_down_table.at[chosen]
    outer_up_ref = outer_up_table.at[chosen]
    share = D // (FF // D)
    places = [(slice(None), slice(D * c, D * (c + 1))) for c in range(1 + FF // D)]
    if fast:
        places += [(slice(share * c, share * (c + 1)), slice(D + FF, D + 2 * FF)) for c in range(FF // D)]
    copies = [
        pltpu.make_async_copy(late_hbm.at[place], late_ref.at[place], sems.at[n]) for n, place in enumerate(places)
    ]
    order = [0] + [n for c in range(FF // D) for n in (1 + c, 1 + FF // D + c) if n < len(copies)]
    for n in order:
        copies[n].start()

    def build(c):
        copies[1 + FF // D + c].wait()
        slab = 24
        for pair in range(share // (2 * slab)):
            first = share * c + 2 * slab * pair
            block = late_ref[first : first + 2 * slab, D + FF :].astype(f32)
            cut = [
                block[slab * side : slab * (side + 1), D * n : D * (n + 1)]
                for side in range(2)
                for n in range(FF // D)
            ]
            wide_ref[4 * first : 4 * first + 8 * slab, :] = jnp.concatenate(cut, axis=0).astype(bf16)

    for a in range(4):
        hold_ref[a] = ctx_refs[a][...]
    context = jnp.concatenate([hold_ref[group ^ g][:, :SHARE] for g in range(4)], axis=1)
    context_red = dense_right_t(context, down_ref[...]).astype(bf16)
    copies[0].wait()
    attended = dense_mul(context, late_ref[:, :D]) + dense_mul(context_red, up_ref[...])
    first, first_root = normal(tok_ref[...].astype(f32) + attended)
    first_norm = first * gain_ref[0:1, :] + gain_ref[1:2, :]
    first_low = first_norm.astype(bf16)
    inner_red = dense_right_t(first_low, inner_down_ref[...]).astype(bf16)
    outer_red = jnp.zeros((rows, RANK), f32)
    outer_out = jnp.zeros((rows, D), f32)
    for c in range(FF // D):
        here = slice(D * c, D * (c + 1))
        copies[1 + c].wait()
        if fast:
            build(c)
        pre = dense_mul(first_low, late_ref[:, D * (c + 1) : D * (c + 2)]) + dense_mul(
            inner_red, inner_up_ref[:, here]
        )
        pre_ref[:, here] = pre
        active = (0.5 * pre * (1.0 + lax.erf(pre * 0.7071067811865476))).astype(bf16)
        act_ref[:, here] = active
        outer_red = outer_red + dense_right_t(active, outer_down_ref[:, here])
        outer_out = outer_out + dense_mul(active, wide_ref[here, :])
    outer_red = outer_red.astype(bf16)
    outer_out = outer_out + dense_mul(outer_red, outer_up_ref[...])
    second, second_root = normal(first_norm + outer_out)
    position = meta_ref[0] * rows + lax.broadcasted_iota(jnp.int32, (rows, D), 0)
    valid = (position < meta_ref[1]).astype(f32)
    out_ref[...] = ((second * gain_ref[2:3, :] + gain_ref[3:4, :]) * valid).astype(bf16)
    grad_second = normal_back(valid * cot_ref[...].astype(f32) * gain_ref[2:3, :], second, second_root)
    grad_outer = grad_second.astype(bf16)
    first_up = RANK * 3
    first_down = RANK * (3 + FF // D)
    terms_ref[first_down + RANK * (FF // D) :, :] = dense_left_t(outer_red, grad_outer)
    outer_grad_red = dense_right_t(grad_outer, outer_up_ref[...]).astype(bf16)
    inner_grad_red = jnp.zeros((rows, RANK), f32)
    grad_first = grad_second
    for c in range(FF // D):
        here = slice(D * c, D * (c + 1))
        grad_active = dense_right_t(grad_outer, wide_ref[here, :]) + dense_mul(
            outer_grad_red, outer_down_ref[:, here]
        )
        pre = pre_ref[:, here]
        slope = 0.5 * (1.0 + lax.erf(pre * 0.7071067811865476)) + pre * (
            0.3989422804014327 * jnp.exp(-0.5 * pre * pre)
        )
        grad_inner = (slope * grad_active).astype(bf16)
        terms_ref[first_up + RANK * c : first_up + RANK * (c + 1), :] = dense_left_t(inner_red, grad_inner)
        terms_ref[first_down + RANK * c : first_down + RANK * (c + 1), :] = dense_left_t(
            outer_grad_red, act_ref[:, here]
        )
        inner_grad_red = inner_grad_red + dense_right_t(grad_inner, inner_up_ref[:, here])
        grad_first = grad_first + dense_right_t(grad_inner, late_ref[:, D * (c + 1) : D * (c + 2)])
    inner_grad_red = inner_grad_red.astype(bf16)
    terms_ref[2 * RANK : 3 * RANK, :] = dense_left_t(inner_grad_red, first_low)
    grad_first = grad_first + dense_mul(inner_grad_red, inner_down_ref[...])
    grad_attended = normal_back(grad_first * gain_ref[0:1, :], first, first_root)
    grad_ref[...] = grad_attended
    grad_low = grad_attended.astype(bf16)
    context_grad_red = dense_right_t(grad_low, up_ref[...]).astype(bf16)
    terms_ref[:RANK, :] = dense_left_t(context_grad_red, context)
    terms_ref[RANK : 2 * RANK, :] = dense_left_t(context_red, grad_low)
    grad_context = (
        dense_right_t(grad_low, late_ref[:, :D]) + dense_mul(context_grad_red, down_ref[...])
    ).astype(bf16)
    blank = jnp.zeros((rows, WIDE - SHARE), bf16)
    for g in range(4):
        hold_ref[group ^ g] = jnp.concatenate([grad_context[:, SHARE * g : SHARE * (g + 1)], blank], axis=1)
    for a in range(4):
        piece_refs[a][...] = hold_ref[a]


def spread_kernel(meta_ref, *refs):
    part_refs = refs[:8]
    outs = refs[14:20]
    sum_ref, sems = refs[20:]
    quarter = plane_quarter(meta_ref[0])
    core = (meta_ref[0] >> 1) & 1
    chosen = meta_ref[3]
    for n in range(8):
        part = (core ^ (n // 4)) * 4 + (quarter ^ (n % 4))
        sum_ref[pl.ds(pl.multiple_of(part * RANK, RANK), RANK), :] = part_refs[n][:RANK, :].astype(f32)
        sum_ref[pl.ds(pl.multiple_of(LATE_ROWS + part * EARLY_PART, 8), EARLY_PART), :] = part_refs[n][RANK:, :].astype(f32)
    places = [outs[0].at[chosen, j] for j in range(3)] + [outs[1].at[chosen, j] for j in range(3)]
    places += [None, None, outs[0].at[chosen, 3], outs[1].at[chosen, 3], outs[2].at[chosen]]
    places += [outs[n].at[chosen, :, pl.ds(D * c, D)] for n in (3, 4) for c in range(FF // D)]
    places.append(outs[5].at[chosen])
    copies = [
        pltpu.make_async_copy(sum_ref.at[pl.ds(RANK * n, RANK), :], where, sems.at[n])
        for n, where in enumerate(places)
        if where is not None
    ]
    for copy in copies:
        copy.start()
    for copy in copies:
        copy.wait()


LATE_ROWS = 8 * RANK
EARLY_KINDS = 12
EARLY_PART = EARLY_KINDS * RANK // 8
ANY = pl.BlockSpec(memory_space=pl.ANY)
SMEM = pl.BlockSpec(memory_space=pltpu.SMEM)
VMEM = pl.BlockSpec(memory_space=pltpu.VMEM)


def shards(
    tokens,
    cotangent,
    w_query,
    w_key,
    w_value,
    w_output,
    w_inner,
    w_outer,
    gain_first,
    shift_first,
    gain_second,
    shift_second,
    attn_down,
    attn_up,
    inner_down,
    inner_up,
    outer_down,
    outer_up,
    lengths,
    rand_blocks,
    adapter_pick,
):
    device_total = lax.axis_size("seq") * lax.axis_size("head")
    local_rows = tokens.shape[0]
    seq_total = lengths.shape[0]
    members = device_total // seq_total
    rows_total = members * local_rows
    block_total = rows_total // BLOCK
    chunk = 4 * local_rows
    index = lax.axis_index("seq") * lax.axis_size("head") + lax.axis_index("head")
    place = index % members
    seq_number = index // members
    group = (place >> 3) & 3
    seq_length = lengths[seq_number]
    chosen = adapter_pick[seq_number]
    fast = device_total == 32 and members == 32
    together = lax.optimization_barrier

    def send(value, even, odd):
        return lax.ppermute(
            value, AXES, [(j, j ^ (odd if (j >> 1) & 1 else even)) for j in range(device_total)]
        )

    def swap(value, mask):
        return send(value, mask, mask)

    def one(value):
        return send(value, 4, 1)

    def two(value):
        return send(value, 1, 4)

    def exchange(pieces, masks=PEERS):
        return [pieces[0]] + [swap(pieces[a], masks[a]) for a in range(1, 4)]

    def gather_start(value):
        if not fast:
            masks = [slab_offset(n, place, False) for n in range(members // 4)]
            return [value] + [swap(value, mask) for mask in masks[1:]]
        return [value, one(value), two(value)]

    def gather_end(slabs):
        if not fast:
            return slabs
        slabs = slabs + [two(slabs[1])]
        return slabs + [swap(slab, 2) for slab in slabs]

    def gather_group(value):
        return gather_end(gather_start(value))

    def gather_all(value):
        return lax.all_gather(value, AXES, axis=0, tiled=True)

    def share_columns(table, which=group):
        return lax.dynamic_slice_in_dim(table, which * SHARE, SHARE, table.ndim - 1)

    slab = D // device_total
    meta = jnp.stack([place, seq_length, group, chosen]).astype(jnp.int32)
    if fast:
        late_local, *slices = pl.pallas_call(
            pack_kernel,
            in_specs=[SMEM] + [VMEM] * 6,
            out_specs=[VMEM] * 5,
            out_shape=[jax.ShapeDtypeStruct((slab, D + 2 * FF), bf16)]
            + [jax.ShapeDtypeStruct((slab, 3 * WIDE), bf16)] * 4,
            name="pack",
        )(rand_blocks, w_query, w_key, w_value, w_output, w_inner, w_outer)
        late = gather_all(late_local)
        mine = exchange(slices)
        far_tokens = swap(tokens, PEERS[2])
        near_tokens = swap(jnp.concatenate([tokens, far_tokens], axis=0), PEERS[1])
        token_refs = [tokens, far_tokens, near_tokens]
        w_slabs = gather_group(jnp.concatenate(mine, axis=0))
    else:
        late = gather_all(
            jnp.concatenate([w_output, w_inner] + [w_outer[slab * c : slab * (c + 1)] for c in range(FF // D)], axis=1)
        )
        full_qkv = gather_all(jnp.concatenate([w_query, w_key, w_value], axis=1))
        rand_all = lax.all_gather(rand_blocks, "seq", axis=0, tiled=True)
        rand_flat = lax.dynamic_slice_in_dim(rand_all, seq_number * block_total, block_total, 0).reshape(-1)
        token_refs = exchange([tokens] * 4)
        w_slabs = [
            jnp.concatenate(
                [
                    jnp.pad(share_columns(full_qkv[:, D * j : D * (j + 1)]), ((0, 0), (0, WIDE - SHARE)))
                    for j in range(3)
                ],
                axis=1,
            )
        ]

    wide_rows = jax.ShapeDtypeStruct((rows_total, WIDE), bf16)
    piece_shapes = [jax.ShapeDtypeStruct((local_rows, WIDE), bf16)] * 4
    side_weight, side_up, query_own, pair_own, rand_table = pl.pallas_call(
        functools.partial(project_kernel, fast),
        in_specs=[SMEM] + [VMEM] * (2 + len(token_refs) + len(w_slabs)),
        out_specs=[VMEM] * 5,
        out_shape=[
            jax.ShapeDtypeStruct((D, 3 * WIDE), bf16),
            jax.ShapeDtypeStruct((3, WIDE // 2, WIDE), bf16),
            jax.ShapeDtypeStruct((chunk, WIDE), bf16),
            jax.ShapeDtypeStruct((chunk, 2 * SHARE), bf16),
            jax.ShapeDtypeStruct((32, WIDE // 2), jnp.int32),
        ],
        scratch_shapes=[pltpu.VMEM((chunk, D), bf16), pltpu.VMEM((D, 3 * WIDE), f32)],
        compiler_params=pltpu.CompilerParams(vmem_limit_bytes=VMEM_LIMIT),
        name="project",
    )(meta, attn_down, attn_up, *token_refs, *w_slabs)
    if fast:
        rand_flat = rand_table
    pair_slabs = gather_group(pair_own)
    key_all, value_all, *ctx, aux = pl.pallas_call(
        functools.partial(attend_kernel, fast),
        in_specs=[SMEM, SMEM] + [VMEM] * (1 + len(pair_slabs)),
        out_specs=[VMEM] * 7,
        out_shape=[wide_rows] * 2 + piece_shapes + [jax.ShapeDtypeStruct((chunk, WIDE), f32)],
        scratch_shapes=[pltpu.VMEM((rows_total // chunk, (2 if fast else 1) * STACK, chunk), f32)],
        compiler_params=pltpu.CompilerParams(vmem_limit_bytes=VMEM_LIMIT),
        name="attend",
    )(meta, rand_flat, query_own, *pair_slabs)
    ctx_pieces = exchange(ctx)
    query_send, ctx_pieces[1] = together((query_own, ctx_pieces[1]))
    query_slabs = gather_group(query_send)

    gains = jnp.stack([gain_first, shift_first, gain_second, shift_second])
    middle_in = [tokens, cotangent, late, gains, attn_down, attn_up, inner_down, inner_up, outer_down, outer_up]
    wide_shape = [pltpu.VMEM((FF, D), bf16)]
    if not fast:
        middle_in.append(
            late[:, D + FF :].reshape(device_total, slab, FF // D, D).transpose(0, 2, 1, 3).reshape(FF, D)
        )
        wide_shape = []
    count = len(middle_in)

    def middle(meta_ref, *refs):
        ins, outs, scratch = refs[4 : 4 + count], refs[4 + count : 11 + count], refs[11 + count :]
        wide_ref = scratch[-1] if fast else ins[-1]
        middle_kernel(
            fast, meta_ref, refs[:4], *ins[:10], wide_ref, *outs[:2], outs[2:6], outs[6], *scratch[:5]
        )


    output, grad_attended, *grad_pieces, early_terms = pl.pallas_call(
        middle,
        in_specs=[SMEM] + [VMEM] * 6 + [ANY] + [VMEM] * (count - 3),
        out_specs=[VMEM] * 7,
        out_shape=[
            jax.ShapeDtypeStruct((local_rows, D), bf16),
            jax.ShapeDtypeStruct((local_rows, D), f32),
        ]
        + piece_shapes
        + [jax.ShapeDtypeStruct((EARLY_KINDS * RANK, D), f32)],
        scratch_shapes=[
            pltpu.VMEM((4, local_rows, WIDE), bf16),
            pltpu.VMEM((local_rows, FF), f32),
            pltpu.VMEM((local_rows, FF), bf16),
            pltpu.VMEM(late.shape, bf16),
            pltpu.SemaphoreType.DMA((1 + 2 * (FF // D),)),
        ]
        + wide_shape,
        compiler_params=pltpu.CompilerParams(vmem_limit_bytes=VMEM_LIMIT),
        name="middle",
    )(meta, *ctx_pieces, *middle_in)
    grad_wide = pl.pallas_call(
        delta_kernel,
        in_specs=[VMEM] * 5,
        out_specs=VMEM,
        out_shape=jax.ShapeDtypeStruct((chunk, WIDE), bf16),
        name="delta",
    )(*exchange(grad_pieces), aux)
    def reduced(terms):
        paired = terms[0] + swap(terms[1], 2)
        moved = exchange([paired[a] for a in range(4)])
        part = (moved[0] + moved[1]) + (moved[2] + moved[3])
        moved = [part] + [swap(part, depth) for depth in DEPTHS[1:]]
        return (moved[0] + moved[1]) + (moved[2] + moved[3])

    grad_slabs = gather_start(grad_wide)
    out_shapes = [
        jax.ShapeDtypeStruct(shape, f32)
        for shape in (
            (ADAPTERS, 4, RANK, D),
            (ADAPTERS, 4, RANK, D),
            (ADAPTERS, RANK, D),
            (ADAPTERS, RANK, FF),
            (ADAPTERS, RANK, FF),
            (ADAPTERS, RANK, D),
        )
    ]
    zero_shapes = out_shapes if fast else []
    query_grad, *zeros = pl.pallas_call(
        functools.partial(near_kernel, fast),
        in_specs=[SMEM, SMEM] + [VMEM] * 4,
        out_specs=[VMEM] + [ANY] * len(zero_shapes),
        out_shape=[jax.ShapeDtypeStruct((chunk, WIDE), bf16)] + zero_shapes,
        scratch_shapes=[pltpu.VMEM((4, RANK, D), f32), pltpu.SemaphoreType.DMA((ADAPTERS * 12,))],
        compiler_params=pltpu.CompilerParams(vmem_limit_bytes=VMEM_LIMIT),
        cost_estimate=pl.CostEstimate(flops=4000000000, bytes_accessed=8000000, transcendentals=1000000),
        name="near",
    )(meta, rand_flat, query_own, key_all, value_all, grad_wide)
    query_grad, *grad_slabs = together((query_grad, *grad_slabs))
    grad_slabs = gather_end(grad_slabs)
    *parts, near_terms, away_terms = pl.pallas_call(
        functools.partial(far_kernel, fast),
        in_specs=[SMEM, SMEM] + [VMEM] * (6 + len(token_refs) + 2 * len(grad_slabs)),
        out_specs=[VMEM] * 6,
        out_shape=[jax.ShapeDtypeStruct((local_rows, D), bf16)] * 4
        + [jax.ShapeDtypeStruct((4, RANK + EARLY_PART, D), kind) for kind in (f32, bf16 if fast else f32)],
        scratch_shapes=[
            pltpu.VMEM((rows_total, WIDE), bf16),
            pltpu.VMEM((rows_total, WIDE), bf16),
            pltpu.VMEM((chunk, WIDE), f32),
            pltpu.VMEM((chunk, WIDE), f32),
            pltpu.VMEM((chunk, 3 * WIDE), bf16),
            pltpu.VMEM((chunk, D), bf16),
            pltpu.VMEM((8, RANK + EARLY_PART, D), f32),
            pltpu.SMEM((3 * block_total + 8,), jnp.int32),
        ],
        compiler_params=pltpu.CompilerParams(vmem_limit_bytes=VMEM_LIMIT),
        name="far",
    )(
        meta,
        rand_flat,
        key_all,
        value_all,
        query_grad,
        side_weight,
        side_up,
        early_terms,
        *token_refs,
        *query_slabs,
        *grad_slabs,
    )
    def token_sum(pieces):
        pieces = [piece.astype(f32) for piece in pieces]
        return grad_attended + ((pieces[0] + pieces[1]) + (pieces[2] + pieces[3]))

    arrived = [parts[0], swap(parts[1], PEERS[1])]
    if fast:
        paired = near_terms + swap(away_terms, 2).astype(f32)
        moved = [paired[0]] + [swap(paired[a].astype(bf16), PLANE[a]).astype(f32) for a in range(1, 4)]
        part = ((moved[0] + moved[1]) + (moved[2] + moved[3])).astype(bf16)
        moved = [piece.astype(f32) for piece in exchange([part] * 4)]
        part = ((moved[0] + moved[1]) + (moved[2] + moved[3])).astype(bf16)
        part, parts[2], parts[3] = together((part, parts[2], parts[3]))
    arrived += [swap(parts[a], PEERS[a]) for a in (2, 3)]
    if fast:
        part_list = exchange([part] * 4, PLANE)
        part_list = part_list + [swap(value, 2) for value in part_list]
        sums = pl.pallas_call(
            spread_kernel,
            in_specs=[SMEM] + [VMEM] * 8 + [ANY] * 6,
            out_specs=[ANY] * 6,
            out_shape=out_shapes,
            scratch_shapes=[
                pltpu.VMEM((LATE_ROWS + EARLY_KINDS * RANK, D), f32),
                pltpu.SemaphoreType.DMA((8 + EARLY_KINDS,)),
            ],
            input_output_aliases={9 + n: n for n in range(6)},
            name="spread",
        )(meta, *part_list, *zeros)
        return (output, token_sum(arrived), *sums)

    terms = jnp.concatenate([near_terms, away_terms], axis=0)
    terms = jnp.concatenate([terms[:, :RANK].reshape(-1, D), terms[:, RANK:].reshape(-1, D)], axis=0)
    slots = (jnp.arange(seq_total) == seq_number).astype(f32)[:, None, None]
    every = lax.psum(slots * terms[None], AXES)

    def spread(kinds, width):
        def term(s):
            rows = jnp.concatenate([every[s, kind * RANK : (kind + width // D) * RANK] for kind in kinds], axis=0)
            value = rows.reshape(len(kinds), width // D, RANK, D).transpose(0, 2, 1, 3)
            value = value.reshape(len(kinds), RANK, width)
            return (jnp.arange(ADAPTERS) == adapter_pick[s]).astype(f32)[:, None, None, None] * value[None]

        return functools.reduce(lambda x, y: x + y, [term(s) for s in range(seq_total)])

    wide = FF // D
    sums = [
        spread((0, 1, 2, 8), D),
        spread((3, 4, 5, 9), D),
        spread((10,), D),
        spread((11,), FF),
        spread((11 + wide,), FF),
        spread((11 + 2 * wide,), D),
    ]
    return (
        output,
        token_sum(arrived),
        *[value.reshape(leaf.shape) for value, leaf in zip(sums, out_shapes, strict=True)],
    )


def solution(mesh):
    rows = P(AXES, None)
    placed = (rows,) * 8 + (P(),) * 11 + (P("seq", None), P())
    return jax.shard_map(
        shards,
        mesh=mesh,
        in_specs=placed,
        out_specs=(rows, rows) + (P(),) * 6,
        check_vma=False,
    )
```

time: 321 us -> 236 us (0.74)
  Pallas kernels: 110 us -> 82.3 us
  local copies, waits for them, and re-layouts: 31.6 us -> 4.9 us
  waiting for transfers between devices: 91.1 us -> 71 us
  starting transfers between devices: 66 us -> 57.8 us
    pallas_call x4 -> x6, Pallas kernels: 105 us -> 77.4 us  [the longest x1 28.2 us: shards(): pl.pallas_call(functools.partial(far_kernel, fast), in_specs=[SMEM, SMEM]...]
    ppermute x68 -> x56, waiting for transfers between devices: 91.1 us -> 71 us  [send(): lax.ppermute(value, AXES, [(j, j ^ (odd if j >> 1 & 1 else even)) for j i...]
    ppermute x68 -> x56, starting transfers between devices: 65.9 us -> 57.7 us  [send(): lax.ppermute(value, AXES, [(j, j ^ (odd if j >> 1 & 1 else even)) for j i...]
    squeeze x6 -> x0, local copies, waits for them, and re-layouts: 7.02 us -> none  [the longest x2 3.1 us: select(): return lax.dynamic_index_in_dim(table, chosen, 0, keepdims=False)]
    another operation x8 -> x0, local copies, waits for them, and re-layouts: 6.84 us -> none
    unnamed x114 -> x115, local copies, waits for them, and re-layouts: 9.41 us -> 4.87 us
  transfers between devices with their start and end apart: 70 -> 57, of which waited for: 31 -> 29; matrix products, arithmetic and copies ran while one was open for 6% -> 1% of each run, Pallas kernels for 32% -> 22%
where the time goes in v1:
time: 236 us
  Pallas kernels  82.3 us (35%)
  waiting for transfers between devices  71 us (30%)
  starting transfers between devices  57.8 us (24%)
  between operations  16.1 us (7%)
  local copies, waits for them, and re-layouts  4.9 us (2%)
  other arithmetic  4.32 us (2%)
    ppermute x56, waiting for transfers between devices, send(): lax.ppermute(value, AXES, [(j, j ^ (odd if j >> 1 & 1 else even)) for j i...  71 us
    ppermute x56, starting transfers between devices, send(): lax.ppermute(value, AXES, [(j, j ^ (odd if j >> 1 & 1 else even)) for j i...  57.7 us
    pallas_call x1, Pallas kernels, shards(): pl.pallas_call(functools.partial(far_kernel, fast), in_specs=[SMEM, SMEM]...  28.2 us
    pallas_call x1, Pallas kernels, shards(): pl.pallas_call(functools.partial(attend_kernel, fast), in_specs=[SMEM, SM...  16.4 us
    pallas_call x1, Pallas kernels, shards(): pl.pallas_call(middle, in_specs=[SMEM] + [VMEM] * 6 + [ANY] + [VMEM] * (c...  14.5 us
    pallas_call x1, Pallas kernels, shards(): pl.pallas_call(functools.partial(near_kernel, fast), in_specs=[SMEM, SMEM...  11 us
    unnamed x115, local copies, waits for them, and re-layouts  4.87 us
  transfers between devices with their start and end apart: 57, of which 29 were waited for; matrix products, arithmetic and copies ran while one was open for 1% of the time, Pallas kernels for 22%

profile of v1, /device:TPU:0, one launch (start us, length us, event | category | flops | bytes accessed | tf_op | source)
XLA Modules:
  0.0 236.4 jit_solution(5283641751505081894)
XLA Ops:
  7.2 2.8 %pack.1 = (bf16[24,6912]{1,0:T(8,128)(2,1)}, bf16[24,768]{1,0:T(8,128)(2,1)}, bf16[24,768]{1,0:T(8,128)(2,1)}, bf16[24,768]{1,0:T(8,128)(2,1)}, bf16[24,768]{1,0:T(8,128)(2,1)}) custom-call(s32[4,3]{1,0:T(4,128)} %rand_ref.1, bf16[24,768]{1,0:T(8,128)(2,1)} %query_ref.1, bf16[24,768]{1,0:T(8,128)(2,1)} %key_ref.1, bf16[24,768]{1,0:T(8,128)(2,1)} %value_ref.1, ...), custom_call_target="tpu_custom_call" | custom-call | tf_op jit(solution)/shard_map/pack/pallas_call | solution.py:815
  10.0 4.1 %collective-permute-start = (bf16[128,768]{1,0:T(8,128)(2,1)}, bf16[128,768]{1,0:T(8,128)(2,1)S(1)}, u32[]{:S(2)}, u32[]{:S(2)}) collective-permute-start(bf16[128,768]{1,0:T(8,128)(2,1)} %refs_0_.3), channel_id=1, source_target_pairs={{0,16},{1,17},{2,18},{3,19},{4,20},{5,21},{6,22},{7,23},{8,24},{9,... | collective-permute-start | bytes 589832 | tf_op jit(solution)/shard_map/ppermute | solution.py:775
  14.1 1.6 collective-permute-start.2
  16.0 2.5 %collective-permute-start.4 = (bf16[24,768]{1,0:T(8,128)(2,1)}, bf16[24,768]{1,0:T(8,128)(2,1)S(1)}, u32[]{:S(2)}, u32[]{:S(2)}) collective-permute-start(bf16[24,768]{1,0:T(8,128)(2,1)} %get-tuple-element.63), channel_id=1, source_target_pairs={{0,24},{1,25},{2,26},{3,27},{4,28},{5,29},{6,30},{7,31},{8,16},{9,... | collective-permute-start | bytes 110600 | tf_op jit(solution)/shard_map/ppermute | solution.py:775
  20.2 6.1 %collective-permute-done.3 = bf16[24,768]{1,0:T(8,128)(2,1)S(1)} collective-permute-done((bf16[24,768]{1,0:T(8,128)(2,1)}, bf16[24,768]{1,0:T(8,128)(2,1)S(1)}, u32[]{:S(2)}, u32[]{:S(2)}) %collective-permute-start.3) | collective-permute-done | bytes 36896 | tf_op jit(solution)/shard_map/ppermute | solution.py:775
  26.4 1.7 collective-permute-start.5
  28.1 1.0 pad_maximum_fusion
  29.1 5.6 %collective-permute-start.1 = (bf16[256,768]{1,0:T(8,128)(2,1)S(1)}, bf16[256,768]{1,0:T(8,128)(2,1)S(1)}, u32[]{:S(2)}, u32[]{:S(2)}) collective-permute-start(bf16[256,768]{1,0:T(8,128)(2,1)S(1)} %pad_maximum_fusion), channel_id=1, source_target_pairs={{0,8},{1,9},{2,10},{3,11},{4,12},{5,13},{6,14},{7,15},{8,0},{9,1},... | collective-permute-start | bytes 1179656 | tf_op jit(solution)/shard_map/ppermute | solution.py:775
  34.7 1.6 collective-permute-start.6
  37.2 2.6 %collective-permute-done.6.refs_5_ = bf16[96,768]{1,0:T(8,128)(2,1)S(1)} collective-permute-done((bf16[96,768]{1,0:T(8,128)(2,1)S(1)}, bf16[96,768]{1,0:T(8,128)(2,1)S(1)}, u32[]{:S(2)}, u32[]{:S(2)}) %collective-permute-start.6) | collective-permute-done | bytes 147488 | tf_op jit(solution)/shard_map/ppermute | solution.py:775
  39.8 1.6 collective-permute-done.7.refs_6_
  45.3 4.5 %project.1 = (bf16[768,768]{1,0:T(8,128)(2,1)}, bf16[3,128,256]{2,1,0:T(8,128)(2,1)}, bf16[512,256]{1,0:T(8,128)(2,1)}, bf16[512,384]{1,0:T(8,128)(2,1)}, s32[32,128]{1,0:T(8,128)}) custom-call(s32[4]{0:T(128)} %pad_add_fusion.meta_ref, bf16[8,4,16,768]{3,2,1,0:T(8,128)(2,1)} %refs_8_.1, bf16[8,4,16,768]{3,2,1,0:T(8,128)(2,1)} %refs_9_.1, ...), custom_call_target="tpu_custom_call" | custom-call | tf_op jit(solution)/shard_map/project/pallas_call | solution.py:849
  49.8 1.5 collective-permute-start.12
  51.8 9.8 %collective-permute-done.12.refs_1_ = bf16[512,384]{1,0:T(8,128)(2,1)S(1)} collective-permute-done((bf16[512,384]{1,0:T(8,128)(2,1)}, bf16[512,384]{1,0:T(8,128)(2,1)S(1)}, u32[]{:S(2)}, u32[]{:S(2)}) %collective-permute-start.12) | collective-permute-done | bytes 393248 | tf_op jit(solution)/shard_map/ppermute | solution.py:775
  61.6 1.3 collective-permute-start.14
  63.5 10.4 %collective-permute-done.14.refs_3_ = bf16[512,384]{1,0:T(8,128)(2,1)S(1)} collective-permute-done((bf16[512,384]{1,0:T(8,128)(2,1)S(1)}, bf16[512,384]{1,0:T(8,128)(2,1)S(1)}, u32[]{:S(2)}, u32[]{:S(2)}) %collective-permute-start.14) | collective-permute-done | bytes 393248 | tf_op jit(solution)/shard_map/ppermute | solution.py:775
  74.1 1.7 collective-permute-done.18.refs_7_
  76.5 16.4 %attend.1 = (bf16[4096,256]{1,0:T(8,128)(2,1)}, bf16[4096,256]{1,0:T(8,128)(2,1)}, bf16[128,256]{1,0:T(8,128)(2,1)}, bf16[128,256]{1,0:T(8,128)(2,1)}, bf16[128,...) custom-call(s32[4]{0:T(128)} %pad_add_fusion.meta_ref, s32[32,128]{1,0:T(8,128)} %get-tuple-element.64.rand_ref, ...), custom_call_target="tpu_custom_call" | custom-call | tf_op jit(solution)/shard_map/attend/pallas_call | solution.py:867
  92.9 3.6 %collective-permute-start.19 = (bf16[128,256]{1,0:T(8,128)(2,1)}, bf16[128,256]{1,0:T(8,128)(2,1)S(1)}, u32[]{:S(2)}, u32[]{:S(2)}) collective-permute-start(bf16[128,256]{1,0:T(8,128)(2,1)} %get-tuple-element.68), channel_id=1, source_target_pairs={{0,8},{1,9},{2,10},{3,11},{4,12},{5,13},{6,14},{7,15},{8,0},{9,1},... | collective-permute-start | bytes 196616 | tf_op jit(solution)/shard_map/ppermute | solution.py:775
  96.5 5.0 %collective-permute-done.19.refs_1_ = bf16[128,256]{1,0:T(8,128)(2,1)S(1)} collective-permute-done((bf16[128,256]{1,0:T(8,128)(2,1)}, bf16[128,256]{1,0:T(8,128)(2,1)S(1)}, u32[]{:S(2)}, u32[]{:S(2)}) %collective-permute-start.19) | collective-permute-done | bytes 65568 | tf_op jit(solution)/shard_map/ppermute | solution.py:775
  101.6 6.4 %collective-permute-start.20 = (bf16[128,256]{1,0:T(8,128)(2,1)}, bf16[128,256]{1,0:T(8,128)(2,1)S(1)}, u32[]{:S(2)}, u32[]{:S(2)}) collective-permute-start(bf16[128,256]{1,0:T(8,128)(2,1)} %get-tuple-element.70), channel_id=1, source_target_pairs={{0,16},{1,17},{2,18},{3,19},{4,20},{5,21},{6,22},{7,23},{8,24},{9,... | collective-permute-start | bytes 196616 | tf_op jit(solution)/shard_map/ppermute | solution.py:775
  108.6 1.9 collective-permute-done.20.refs_2_
  110.5 3.8 %collective-permute-done.21.refs_3_ = bf16[128,256]{1,0:T(8,128)(2,1)S(1)} collective-permute-done((bf16[128,256]{1,0:T(8,128)(2,1)}, bf16[128,256]{1,0:T(8,128)(2,1)S(1)}, u32[]{:S(2)}, u32[]{:S(2)}) %collective-permute-start.21) | collective-permute-done | bytes 65568 | tf_op jit(solution)/shard_map/ppermute | solution.py:775
  114.9 14.5 %middle.1 = (bf16[128,768]{1,0:T(8,128)(2,1)}, f32[128,768]{1,0:T(8,128)}, bf16[128,256]{1,0:T(8,128)(2,1)}, bf16[128,256]{1,0:T(8,128)(2,1)}, bf16[128,256]{1,0...) custom-call(s32[4]{0:T(128)} %pad_add_fusion.meta_ref, bf16[128,256]{1,0:T(8,128)(2,1)} %get-tuple-element.67.refs_0_, ...), custom_call_target="tpu_custom_call" | custom-call | tf_op jit(solution)/shard_map/middle/pallas_call | solution.py:898
  129.5 1.3 collective-permute-start.23
  130.7 3.1 %collective-permute-start.24 = (bf16[128,256]{1,0:T(8,128)(2,1)}, bf16[128,256]{1,0:T(8,128)(2,1)S(1)}, u32[]{:S(2)}, u32[]{:S(2)}) collective-permute-start(bf16[128,256]{1,0:T(8,128)(2,1)} %get-tuple-element.80), channel_id=1, source_target_pairs={{0,24},{1,25},{2,26},{3,27},{4,28},{5,29},{6,30},{7,31},{8,16},{9,... | collective-permute-start | bytes 196616 | tf_op jit(solution)/shard_map/ppermute | solution.py:775
  134.0 2.0 collective-permute-start.29
  136.0 1.0 collective-permute-done.24.refs_3_
  137.7 2.6 %delta.1.g_ref.refs_11_ = bf16[512,256]{1,0:T(8,128)(2,1)} custom-call(bf16[128,256]{1,0:T(8,128)(2,1)} %get-tuple-element.77.refs_0_, bf16[128,256]{1,0:T(8,128)(2,1)} %copy-done.39, bf16[128,256]{1,0:T(8,128)(2,1)} %copy-done.40, bf16[128,256]{1,0:T(8,128)(2,1)} %copy-done.41, f32[512,256]{1,0:T(8,128)} %get-tuple-element.81.refs_4_), custom_call_target="tpu_custom_call" | custom-call | tf_op jit(solution)/shard_map/delta/pallas_call | solution.py:919
  140.3 2.0 collective-permute-start.25
  142.3 11.0 %near.1 = (bf16[512,256]{1,0:T(8,128)(2,1)}, f32[8,4,16,768]{3,2,1,0:T(8,128)}, f32[8,4,16,768]{3,2,1,0:T(8,128)}, f32[8,16,768]{2,1,0:T(8,128)}, f32[8,16,3072]...) custom-call(s32[4]{0:T(128)} %pad_add_fusion.meta_ref, s32[32,128]{1,0:T(8,128)} %get-tuple-element.64.rand_ref, ...), custom_call_target="tpu_custom_call" | custom-call | flops 4000000000 | bytes 8000000 | tf_op jit(solution)/shard_map/near/pallas_call | solution.py:946
  155.5 4.8 %collective-permute-done.34.refs_14_ = bf16[512,256]{1,0:T(8,128)(2,1)S(1)} collective-permute-done((bf16[512,256]{1,0:T(8,128)(2,1)S(1)}, bf16[512,256]{1,0:T(8,128)(2,1)S(1)}, u32[]{:S(2)}, u32[]{:S(2)}) %collective-permute-start.34) | collective-permute-done | bytes 262176 | tf_op jit(solution)/shard_map/ppermute | solution.py:775
  160.4 1.5 collective-permute-done.38.refs_18_
  162.6 28.2 %far.1 = (bf16[128,768]{1,0:T(8,128)(2,1)}, bf16[128,768]{1,0:T(8,128)(2,1)}, bf16[128,768]{1,0:T(8,128)(2,1)}, bf16[128,768]{1,0:T(8,128)(2,1)}, f32[4,40,768]{2,1,0:T(8,128)}, /*index=5*/bf16[4,40,768]{2,1,0:T(8,128)(2,1)}) custom-call(s32[4]{0:T(128)} %pad_add_fusion.meta_ref, s32[32,128]{1,0:T(8,128)} %get-tuple-element.64.rand_ref, ...), custom_call_target="tpu_custom_call" | custom-call | tf_op jit(solution)/shard_map/far/pallas_call | solution.py:958
  190.9 1.7 collective-permute-done.40
  192.6 1.1 fusion.3
  193.9 3.4 %collective-permute-start.41 = (bf16[40,768]{1,0:T(8,128)(2,1)S(1)}, bf16[40,768]{1,0:T(8,128)(2,1)S(1)}, u32[]{:S(2)}, u32[]{:S(2)}) collective-permute-start(bf16[40,768]{1,0:T(8,128)(2,1)S(1)} %get-tuple-element.114), channel_id=1, source_target_pairs={{0,1},{1,0},{2,3},{3,2},{4,5},{5,4},{6,7},{7,6},{8,9},{9,8},{10,11... | collective-permute-start | bytes 184328 | tf_op jit(solution)/shard_map/ppermute | solution.py:775
  197.3 2.1 collective-permute-done.43
  200.1 3.1 %collective-permute-start.46 = (bf16[40,768]{1,0:T(8,128)(2,1)S(1)}, bf16[40,768]{1,0:T(8,128)(2,1)S(1)}, u32[]{:S(2)}, u32[]{:S(2)}) collective-permute-start(bf16[40,768]{1,0:T(8,128)(2,1)S(1)} %fusion.2), channel_id=1, source_target_pairs={{0,24},{1,25},{2,26},{3,27},{4,28},{5,29},{6,30},{7,31},{8,16},{9,... | collective-permute-start | bytes 184328 | tf_op jit(solution)/shard_map/ppermute | solution.py:775
  203.2 1.3 collective-permute-start.44
  204.5 1.7 collective-permute-done.46
  206.3 2.1 collective-permute-done.45
  208.7 1.2 collective-permute-start.49
  210.4 3.0 %collective-permute-start.48 = (bf16[128,768]{1,0:T(8,128)(2,1)S(1)}, bf16[128,768]{1,0:T(8,128)(2,1)S(1)}, u32[]{:S(2)}, u32[]{:S(2)}) collective-permute-start(bf16[128,768]{1,0:T(8,128)(2,1)S(1)} %copy-done.54), channel_id=1, source_target_pairs={{0,24},{1,25},{2,26},{3,27},{4,28},{5,29},{6,30},{7,31},{8,16},{9,... | collective-permute-start | bytes 589832 | tf_op jit(solution)/shard_map/ppermute | solution.py:775
  213.5 2.3 collective-permute-start.51
  215.8 1.8 collective-permute-done.50.refs_2_
  221.8 2.2 spread.1
  224.0 4.6 %collective-permute-done.47 = bf16[128,768]{1,0:T(8,128)(2,1)S(1)} collective-permute-done((bf16[128,768]{1,0:T(8,128)(2,1)S(1)}, bf16[128,768]{1,0:T(8,128)(2,1)S(1)}, u32[]{:S(2)}, u32[]{:S(2)}) %collective-permute-start.47) | collective-permute-done | bytes 196640 | tf_op jit(solution)/shard_map/ppermute | solution.py:775
  (203 shorter events, 19.0 us)
Async XLA Ops:
  7.2 107.1 %all-gather.2.cloned.1.call-start = ((), (), s32[]{:S(2)}) async-start(), calls=%async_computation | async-start | bytes 10948608 | tf_op jit(solution)/shard_map/all_gather | solution.py:807
  10.0 18.0 %collective-permute-start = (bf16[128,768]{1,0:T(8,128)(2,1)}, bf16[128,768]{1,0:T(8,128)(2,1)S(1)}, u32[]{:S(2)}, u32[]{:S(2)}) collective-permute-start(bf16[128,768]{1,0:T(8,128)(2,1)} %refs_0_.3), channel_id=1, source_target_pairs={{0,16},{1,17},{2,18},{3,19},{4,20},{5,21},{6,22},{7,23},{8,24},{9,... | collective-permute-start | bytes 589832 | tf_op jit(solution)/shard_map/ppermute | solution.py:775
  14.1 6.1 %collective-permute-start.2 = (bf16[24,768]{1,0:T(8,128)(2,1)}, bf16[24,768]{1,0:T(8,128)(2,1)S(1)}, u32[]{:S(2)}, u32[]{:S(2)}) collective-permute-start(bf16[24,768]{1,0:T(8,128)(2,1)} %get-tuple-element.61), channel_id=1, source_target_pairs={{0,8},{1,9},{2,10},{3,11},{4,12},{5,13},{6,14},{7,15},{8,0},{9,1},... | collective-permute-start | bytes 110600 | tf_op jit(solution)/shard_map/ppermute | solution.py:775
  15.7 10.7 %collective-permute-start.3 = (bf16[24,768]{1,0:T(8,128)(2,1)}, bf16[24,768]{1,0:T(8,128)(2,1)S(1)}, u32[]{:S(2)}, u32[]{:S(2)}) collective-permute-start(bf16[24,768]{1,0:T(8,128)(2,1)} %get-tuple-element.62), channel_id=1, source_target_pairs={{0,16},{1,17},{2,18},{3,19},{4,20},{5,21},{6,22},{7,23},{8,24},{9,... | collective-permute-start | bytes 110600 | tf_op jit(solution)/shard_map/ppermute | solution.py:775
  16.0 10.3 %collective-permute-start.4 = (bf16[24,768]{1,0:T(8,128)(2,1)}, bf16[24,768]{1,0:T(8,128)(2,1)S(1)}, u32[]{:S(2)}, u32[]{:S(2)}) collective-permute-start(bf16[24,768]{1,0:T(8,128)(2,1)} %get-tuple-element.63), channel_id=1, source_target_pairs={{0,24},{1,25},{2,26},{3,27},{4,28},{5,29},{6,30},{7,31},{8,16},{9,... | collective-permute-start | bytes 110600 | tf_op jit(solution)/shard_map/ppermute | solution.py:775
  26.4 9.9 %collective-permute-start.5 = (bf16[96,768]{1,0:T(8,128)(2,1)S(1)}, bf16[96,768]{1,0:T(8,128)(2,1)S(1)}, u32[]{:S(2)}, u32[]{:S(2)}) collective-permute-start(bf16[96,768]{1,0:T(8,128)(2,1)S(1)} %constant_dynamic-update-slice_fusion.refs_3_), channel_id=1, source_target_pairs={{0,4},{1,5},{2,3},{3,2},{4,0},{5,1},{6,7},{7,6},{8,12},{9,13},{10,... | collective-permute-start | bytes 442376 | tf_op jit(solution)/shard_map/ppermute | solution.py:775
  29.1 15.4 %collective-permute-start.1 = (bf16[256,768]{1,0:T(8,128)(2,1)S(1)}, bf16[256,768]{1,0:T(8,128)(2,1)S(1)}, u32[]{:S(2)}, u32[]{:S(2)}) collective-permute-start(bf16[256,768]{1,0:T(8,128)(2,1)S(1)} %pad_maximum_fusion), channel_id=1, source_target_pairs={{0,8},{1,9},{2,10},{3,11},{4,12},{5,13},{6,14},{7,15},{8,0},{9,1},... | collective-permute-start | bytes 1179656 | tf_op jit(solution)/shard_map/ppermute | solution.py:775
  34.7 5.1 %collective-permute-start.6 = (bf16[96,768]{1,0:T(8,128)(2,1)S(1)}, bf16[96,768]{1,0:T(8,128)(2,1)S(1)}, u32[]{:S(2)}, u32[]{:S(2)}) collective-permute-start(bf16[96,768]{1,0:T(8,128)(2,1)S(1)} %constant_dynamic-update-slice_fusion.refs_3_), channel_id=1, source_target_pairs={{0,1},{1,0},{2,6},{3,7},{4,5},{5,4},{6,2},{7,3},{8,9},{9,8},{10,14... | collective-permute-start | bytes 442376 | tf_op jit(solution)/shard_map/ppermute | solution.py:775
  36.3 5.2 %collective-permute-start.7 = (bf16[96,768]{1,0:T(8,128)(2,1)S(1)}, bf16[96,768]{1,0:T(8,128)(2,1)S(1)}, u32[]{:S(2)}, u32[]{:S(2)}) collective-permute-start(bf16[96,768]{1,0:T(8,128)(2,1)S(1)} %collective-permute-done.5.refs_4_), channel_id=1, source_target_pairs={{0,1},{1,0},{2,6},{3,7},{4,5},{5,4},{6,2},{7,3},{8,9},{9,8},{10,14... | collective-permute-start | bytes 442376 | tf_op jit(solution)/shard_map/ppermute | solution.py:775
  36.7 6.7 %collective-permute-start.8 = (bf16[96,768]{1,0:T(8,128)(2,1)S(1)}, bf16[96,768]{1,0:T(8,128)(2,1)S(1)}, u32[]{:S(2)}, u32[]{:S(2)}) collective-permute-start(bf16[96,768]{1,0:T(8,128)(2,1)S(1)} %constant_dynamic-update-slice_fusion.refs_3_), channel_id=1, source_target_pairs={{0,2},{1,3},{2,0},{3,1},{4,6},{5,7},{6,4},{7,5},{8,10},{9,11},{10,... | collective-permute-start | bytes 442376 | tf_op jit(solution)/shard_map/ppermute | solution.py:775
  36.7 6.7 %collective-permute-start.9 = (bf16[96,768]{1,0:T(8,128)(2,1)S(1)}, bf16[96,768]{1,0:T(8,128)(2,1)S(1)}, u32[]{:S(2)}, u32[]{:S(2)}) collective-permute-start(bf16[96,768]{1,0:T(8,128)(2,1)S(1)} %collective-permute-done.5.refs_4_), channel_id=1, source_target_pairs={{0,2},{1,3},{2,0},{3,1},{4,6},{5,7},{6,4},{7,5},{8,10},{9,11},{10,... | collective-permute-start | bytes 442376 | tf_op jit(solution)/shard_map/ppermute | solution.py:775
  39.8 3.6 %collective-permute-start.10 = (bf16[96,768]{1,0:T(8,128)(2,1)S(1)}, bf16[96,768]{1,0:T(8,128)(2,1)S(1)}, u32[]{:S(2)}, u32[]{:S(2)}) collective-permute-start(bf16[96,768]{1,0:T(8,128)(2,1)S(1)} %collective-permute-done.6.refs_5_), channel_id=1, source_target_pairs={{0,2},{1,3},{2,0},{3,1},{4,6},{5,7},{6,4},{7,5},{8,10},{9,11},{10,... | collective-permute-start | bytes 442376 | tf_op jit(solution)/shard_map/ppermute | solution.py:775
  41.4 2.0 collective-permute-start.11
  49.8 11.8 %collective-permute-start.12 = (bf16[512,384]{1,0:T(8,128)(2,1)}, bf16[512,384]{1,0:T(8,128)(2,1)S(1)}, u32[]{:S(2)}, u32[]{:S(2)}) collective-permute-start(bf16[512,384]{1,0:T(8,128)(2,1)} %get-tuple-element.66.refs_0_), channel_id=1, source_target_pairs={{0,4},{1,5},{2,3},{3,2},{4,0},{5,1},{6,7},{7,6},{8,12},{9,13},{10,... | collective-permute-start | bytes 1179656 | tf_op jit(solution)/shard_map/ppermute | solution.py:775
  51.3 12.2 %collective-permute-start.13 = (bf16[512,384]{1,0:T(8,128)(2,1)}, bf16[512,384]{1,0:T(8,128)(2,1)S(1)}, u32[]{:S(2)}, u32[]{:S(2)}) collective-permute-start(bf16[512,384]{1,0:T(8,128)(2,1)} %get-tuple-element.66.refs_0_), channel_id=1, source_target_pairs={{0,1},{1,0},{2,6},{3,7},{4,5},{5,4},{6,2},{7,3},{8,9},{9,8},{10,14... | collective-permute-start | bytes 1179656 | tf_op jit(solution)/shard_map/ppermute | solution.py:775
  61.6 12.4 %collective-permute-start.14 = (bf16[512,384]{1,0:T(8,128)(2,1)S(1)}, bf16[512,384]{1,0:T(8,128)(2,1)S(1)}, u32[]{:S(2)}, u32[]{:S(2)}) collective-permute-start(bf16[512,384]{1,0:T(8,128)(2,1)S(1)} %collective-permute-done.12.refs_1_), channel_id=1, source_target_pairs={{0,1},{1,0},{2,6},{3,7},{4,5},{5,4},{6,2},{7,3},{8,9},{9,8},{10,14... | collective-permute-start | bytes 1179656 | tf_op jit(solution)/shard_map/ppermute | solution.py:775
  63.0 11.0 %collective-permute-start.15 = (bf16[512,384]{1,0:T(8,128)(2,1)}, bf16[512,384]{1,0:T(8,128)(2,1)S(1)}, u32[]{:S(2)}, u32[]{:S(2)}) collective-permute-start(bf16[512,384]{1,0:T(8,128)(2,1)} %get-tuple-element.66.refs_0_), channel_id=1, source_target_pairs={{0,2},{1,3},{2,0},{3,1},{4,6},{5,7},{6,4},{7,5},{8,10},{9,11},{10,... | collective-permute-start | bytes 1179656 | tf_op jit(solution)/shard_map/ppermute | solution.py:775
  63.0 11.0 %collective-permute-start.16 = (bf16[512,384]{1,0:T(8,128)(2,1)S(1)}, bf16[512,384]{1,0:T(8,128)(2,1)S(1)}, u32[]{:S(2)}, u32[]{:S(2)}) collective-permute-start(bf16[512,384]{1,0:T(8,128)(2,1)S(1)} %collective-permute-done.12.refs_1_), channel_id=1, source_target_pairs={{0,2},{1,3},{2,0},{3,1},{4,6},{5,7},{6,4},{7,5},{8,10},{9,11},{10,... | collective-permute-start | bytes 1179656 | tf_op jit(solution)/shard_map/ppermute | solution.py:775
  63.5 10.6 %collective-permute-start.17 = (bf16[512,384]{1,0:T(8,128)(2,1)S(1)}, bf16[512,384]{1,0:T(8,128)(2,1)S(1)}, u32[]{:S(2)}, u32[]{:S(2)}) collective-permute-start(bf16[512,384]{1,0:T(8,128)(2,1)S(1)} %collective-permute-done.13.refs_2_), channel_id=1, source_target_pairs={{0,2},{1,3},{2,0},{3,1},{4,6},{5,7},{6,4},{7,5},{8,10},{9,11},{10,... | collective-permute-start | bytes 1179656 | tf_op jit(solution)/shard_map/ppermute | solution.py:775
  92.9 8.6 %collective-permute-start.19 = (bf16[128,256]{1,0:T(8,128)(2,1)}, bf16[128,256]{1,0:T(8,128)(2,1)S(1)}, u32[]{:S(2)}, u32[]{:S(2)}) collective-permute-start(bf16[128,256]{1,0:T(8,128)(2,1)} %get-tuple-element.68), channel_id=1, source_target_pairs={{0,8},{1,9},{2,10},{3,11},{4,12},{5,13},{6,14},{7,15},{8,0},{9,1},... | collective-permute-start | bytes 196616 | tf_op jit(solution)/shard_map/ppermute | solution.py:775
  101.5 32.4 %collective-permute-start.27 = (bf16[512,256]{1,0:T(8,128)(2,1)S(1)}, bf16[512,256]{1,0:T(8,128)(2,1)S(1)}, u32[]{:S(2)}, u32[]{:S(2)}) collective-permute-start(bf16[512,256]{1,0:T(8,128)(2,1)S(1)} %copy-done.2), channel_id=1, source_target_pairs={{0,4},{1,5},{2,3},{3,2},{4,0},{5,1},{6,7},{7,6},{8,12},{9,13},{10,... | collective-permute-start | bytes 786440 | tf_op jit(solution)/shard_map/ppermute | solution.py:775
  101.6 8.9 %collective-permute-start.20 = (bf16[128,256]{1,0:T(8,128)(2,1)}, bf16[128,256]{1,0:T(8,128)(2,1)S(1)}, u32[]{:S(2)}, u32[]{:S(2)}) collective-permute-start(bf16[128,256]{1,0:T(8,128)(2,1)} %get-tuple-element.70), channel_id=1, source_target_pairs={{0,16},{1,17},{2,18},{3,19},{4,20},{5,21},{6,22},{7,23},{8,24},{9,... | collective-permute-start | bytes 196616 | tf_op jit(solution)/shard_map/ppermute | solution.py:775
  108.0 6.3 %collective-permute-start.21 = (bf16[128,256]{1,0:T(8,128)(2,1)}, bf16[128,256]{1,0:T(8,128)(2,1)S(1)}, u32[]{:S(2)}, u32[]{:S(2)}) collective-permute-start(bf16[128,256]{1,0:T(8,128)(2,1)} %get-tuple-element.71), channel_id=1, source_target_pairs={{0,24},{1,25},{2,26},{3,27},{4,28},{5,29},{6,30},{7,31},{8,16},{9,... | collective-permute-start | bytes 196616 | tf_op jit(solution)/shard_map/ppermute | solution.py:775
  129.4 4.5 %collective-permute-start.22 = (bf16[128,256]{1,0:T(8,128)(2,1)}, bf16[128,256]{1,0:T(8,128)(2,1)S(1)}, u32[]{:S(2)}, u32[]{:S(2)}) collective-permute-start(bf16[128,256]{1,0:T(8,128)(2,1)} %get-tuple-element.78), channel_id=1, source_target_pairs={{0,8},{1,9},{2,10},{3,11},{4,12},{5,13},{6,14},{7,15},{8,0},{9,1},... | collective-permute-start | bytes 196616 | tf_op jit(solution)/shard_map/ppermute | solution.py:775
  129.5 6.5 %collective-permute-start.23 = (bf16[128,256]{1,0:T(8,128)(2,1)}, bf16[128,256]{1,0:T(8,128)(2,1)S(1)}, u32[]{:S(2)}, u32[]{:S(2)}) collective-permute-start(bf16[128,256]{1,0:T(8,128)(2,1)} %get-tuple-element.79), channel_id=1, source_target_pairs={{0,16},{1,17},{2,18},{3,19},{4,20},{5,21},{6,22},{7,23},{8,24},{9,... | collective-permute-start | bytes 196616 | tf_op jit(solution)/shard_map/ppermute | solution.py:775
  130.7 6.3 %collective-permute-start.24 = (bf16[128,256]{1,0:T(8,128)(2,1)}, bf16[128,256]{1,0:T(8,128)(2,1)S(1)}, u32[]{:S(2)}, u32[]{:S(2)}) collective-permute-start(bf16[128,256]{1,0:T(8,128)(2,1)} %get-tuple-element.80), channel_id=1, source_target_pairs={{0,24},{1,25},{2,26},{3,27},{4,28},{5,29},{6,30},{7,31},{8,16},{9,... | collective-permute-start | bytes 196616 | tf_op jit(solution)/shard_map/ppermute | solution.py:775
  133.9 19.5 %collective-permute-start.28 = (bf16[512,256]{1,0:T(8,128)(2,1)S(1)}, bf16[512,256]{1,0:T(8,128)(2,1)S(1)}, u32[]{:S(2)}, u32[]{:S(2)}) collective-permute-start(bf16[512,256]{1,0:T(8,128)(2,1)S(1)} %copy-done.2), channel_id=1, source_target_pairs={{0,1},{1,0},{2,6},{3,7},{4,5},{5,4},{6,2},{7,3},{8,9},{9,8},{10,14... | collective-permute-start | bytes 786440 | tf_op jit(solution)/shard_map/ppermute | solution.py:775
  133.9 20.3 %collective-permute-start.30 = (bf16[512,256]{1,0:T(8,128)(2,1)S(1)}, bf16[512,256]{1,0:T(8,128)(2,1)S(1)}, u32[]{:S(2)}, u32[]{:S(2)}) collective-permute-start(bf16[512,256]{1,0:T(8,128)(2,1)S(1)} %copy-done.2), channel_id=1, source_target_pairs={{0,2},{1,3},{2,0},{3,1},{4,6},{5,7},{6,4},{7,5},{8,10},{9,11},{10,... | collective-permute-start | bytes 786440 | tf_op jit(solution)/shard_map/ppermute | solution.py:775
  134.0 20.0 %collective-permute-start.29 = (bf16[512,256]{1,0:T(8,128)(2,1)S(1)}, bf16[512,256]{1,0:T(8,128)(2,1)S(1)}, u32[]{:S(2)}, u32[]{:S(2)}) collective-permute-start(bf16[512,256]{1,0:T(8,128)(2,1)S(1)} %collective-permute-done.27.refs_4_), channel_id=1, source_target_pairs={{0,1},{1,0},{2,6},{3,7},{4,5},{5,4},{6,2},{7,3},{8,9},{9,8},{10,14... | collective-permute-start | bytes 786440 | tf_op jit(solution)/shard_map/ppermute | solution.py:775
  140.3 13.2 %collective-permute-start.25 = (bf16[512,256]{1,0:T(8,128)(2,1)}, bf16[512,256]{1,0:T(8,128)(2,1)S(1)}, u32[]{:S(2)}, u32[]{:S(2)}) collective-permute-start(bf16[512,256]{1,0:T(8,128)(2,1)} %delta.1.g_ref.refs_11_), channel_id=1, source_target_pairs={{0,4},{1,5},{2,3},{3,2},{4,0},{5,1},{6,7},{7,6},{8,12},{9,13},{10,... | collective-permute-start | bytes 786440 | tf_op jit(solution)/shard_map/ppermute | solution.py:775
  142.3 11.7 %collective-permute-start.26 = (bf16[512,256]{1,0:T(8,128)(2,1)}, bf16[512,256]{1,0:T(8,128)(2,1)S(1)}, u32[]{:S(2)}, u32[]{:S(2)}) collective-permute-start(bf16[512,256]{1,0:T(8,128)(2,1)} %delta.1.g_ref.refs_11_), channel_id=1, source_target_pairs={{0,1},{1,0},{2,6},{3,7},{4,5},{5,4},{6,2},{7,3},{8,9},{9,8},{10,14... | collective-permute-start | bytes 786440 | tf_op jit(solution)/shard_map/ppermute | solution.py:775
  154.0 6.4 %collective-permute-start.34 = (bf16[512,256]{1,0:T(8,128)(2,1)S(1)}, bf16[512,256]{1,0:T(8,128)(2,1)S(1)}, u32[]{:S(2)}, u32[]{:S(2)}) collective-permute-start(bf16[512,256]{1,0:T(8,128)(2,1)S(1)} %collective-permute-done.25.refs_12_), channel_id=1, source_target_pairs={{0,1},{1,0},{2,6},{3,7},{4,5},{5,4},{6,2},{7,3},{8,9},{9,8},{10,14... | collective-permute-start | bytes 786440 | tf_op jit(solution)/shard_map/ppermute | solution.py:775
  154.0 6.4 %collective-permute-start.33 = (bf16[512,256]{1,0:T(8,128)(2,1)S(1)}, bf16[512,256]{1,0:T(8,128)(2,1)S(1)}, u32[]{:S(2)}, u32[]{:S(2)}) collective-permute-start(bf16[512,256]{1,0:T(8,128)(2,1)S(1)} %collective-permute-done.29.refs_6_), channel_id=1, source_target_pairs={{0,2},{1,3},{2,0},{3,1},{4,6},{5,7},{6,4},{7,5},{8,10},{9,11},{10,... | collective-permute-start | bytes 786440 | tf_op jit(solution)/shard_map/ppermute | solution.py:775
  154.2 6.2 %collective-permute-start.36 = (bf16[512,256]{1,0:T(8,128)(2,1)S(1)}, bf16[512,256]{1,0:T(8,128)(2,1)S(1)}, u32[]{:S(2)}, u32[]{:S(2)}) collective-permute-start(bf16[512,256]{1,0:T(8,128)(2,1)S(1)} %collective-permute-done.25.refs_12_), channel_id=1, source_target_pairs={{0,2},{1,3},{2,0},{3,1},{4,6},{5,7},{6,4},{7,5},{8,10},{9,11},{10,... | collective-permute-start | bytes 786440 | tf_op jit(solution)/shard_map/ppermute | solution.py:775
  155.0 5.4 %collective-permute-start.35 = (bf16[512,256]{1,0:T(8,128)(2,1)S(1)}, bf16[512,256]{1,0:T(8,128)(2,1)S(1)}, u32[]{:S(2)}, u32[]{:S(2)}) collective-permute-start(bf16[512,256]{1,0:T(8,128)(2,1)S(1)} %copy-done.3), channel_id=1, source_target_pairs={{0,2},{1,3},{2,0},{3,1},{4,6},{5,7},{6,4},{7,5},{8,10},{9,11},{10,... | collective-permute-start | bytes 786440 | tf_op jit(solution)/shard_map/ppermute | solution.py:775
  155.4 5.0 %collective-permute-start.37 = (bf16[512,256]{1,0:T(8,128)(2,1)S(1)}, bf16[512,256]{1,0:T(8,128)(2,1)S(1)}, u32[]{:S(2)}, u32[]{:S(2)}) collective-permute-start(bf16[512,256]{1,0:T(8,128)(2,1)S(1)} %collective-permute-done.26.refs_13_), channel_id=1, source_target_pairs={{0,2},{1,3},{2,0},{3,1},{4,6},{5,7},{6,4},{7,5},{8,10},{9,11},{10,... | collective-permute-start | bytes 786440 | tf_op jit(solution)/shard_map/ppermute | solution.py:775
  193.7 5.7 %collective-permute-start.43 = (bf16[40,768]{1,0:T(8,128)(2,1)S(1)}, bf16[40,768]{1,0:T(8,128)(2,1)S(1)}, u32[]{:S(2)}, u32[]{:S(2)}) collective-permute-start(bf16[40,768]{1,0:T(8,128)(2,1)S(1)} %get-tuple-element.115), channel_id=1, source_target_pairs={{0,5},{1,4},{2,7},{3,6},{4,1},{5,0},{6,3},{7,2},{8,13},{9,12},{10,... | collective-permute-start | bytes 184328 | tf_op jit(solution)/shard_map/ppermute | solution.py:775
  193.8 5.6 %collective-permute-start.42 = (bf16[40,768]{1,0:T(8,128)(2,1)S(1)}, bf16[40,768]{1,0:T(8,128)(2,1)S(1)}, u32[]{:S(2)}, u32[]{:S(2)}) collective-permute-start(bf16[40,768]{1,0:T(8,128)(2,1)S(1)} %get-tuple-element.116), channel_id=1, source_target_pairs={{0,4},{1,5},{2,6},{3,7},{4,0},{5,1},{6,2},{7,3},{8,12},{9,13},{10,... | collective-permute-start | bytes 184328 | tf_op jit(solution)/shard_map/ppermute | solution.py:775
  193.9 6.2 %collective-permute-start.41 = (bf16[40,768]{1,0:T(8,128)(2,1)S(1)}, bf16[40,768]{1,0:T(8,128)(2,1)S(1)}, u32[]{:S(2)}, u32[]{:S(2)}) collective-permute-start(bf16[40,768]{1,0:T(8,128)(2,1)S(1)} %get-tuple-element.114), channel_id=1, source_target_pairs={{0,1},{1,0},{2,3},{3,2},{4,5},{5,4},{6,7},{7,6},{8,9},{9,8},{10,11... | collective-permute-start | bytes 184328 | tf_op jit(solution)/shard_map/ppermute | solution.py:775
  200.1 6.2 %collective-permute-start.46 = (bf16[40,768]{1,0:T(8,128)(2,1)S(1)}, bf16[40,768]{1,0:T(8,128)(2,1)S(1)}, u32[]{:S(2)}, u32[]{:S(2)}) collective-permute-start(bf16[40,768]{1,0:T(8,128)(2,1)S(1)} %fusion.2), channel_id=1, source_target_pairs={{0,24},{1,25},{2,26},{3,27},{4,28},{5,29},{6,30},{7,31},{8,16},{9,... | collective-permute-start | bytes 184328 | tf_op jit(solution)/shard_map/ppermute | solution.py:775
  203.2 5.2 %collective-permute-start.45 = (bf16[40,768]{1,0:T(8,128)(2,1)S(1)}, bf16[40,768]{1,0:T(8,128)(2,1)S(1)}, u32[]{:S(2)}, u32[]{:S(2)}) collective-permute-start(bf16[40,768]{1,0:T(8,128)(2,1)S(1)} %fusion.2), channel_id=1, source_target_pairs={{0,16},{1,17},{2,18},{3,19},{4,20},{5,21},{6,22},{7,23},{8,24},{9,... | collective-permute-start | bytes 184328 | tf_op jit(solution)/shard_map/ppermute | solution.py:775
  203.2 5.5 %collective-permute-start.44 = (bf16[40,768]{1,0:T(8,128)(2,1)S(1)}, bf16[40,768]{1,0:T(8,128)(2,1)S(1)}, u32[]{:S(2)}, u32[]{:S(2)}) collective-permute-start(bf16[40,768]{1,0:T(8,128)(2,1)S(1)} %fusion.2), channel_id=1, source_target_pairs={{0,8},{1,9},{2,10},{3,11},{4,12},{5,13},{6,14},{7,15},{8,0},{9,1},... | collective-permute-start | bytes 184328 | tf_op jit(solution)/shard_map/ppermute | solution.py:775
  208.7 4.7 %collective-permute-start.49 = (bf16[40,768]{1,0:T(8,128)(2,1)S(1)}, bf16[40,768]{1,0:T(8,128)(2,1)S(1)}, u32[]{:S(2)}, u32[]{:S(2)}) collective-permute-start(bf16[40,768]{1,0:T(8,128)(2,1)S(1)} %add_convert_fusion.refs_0_), channel_id=1, source_target_pairs={{0,1},{1,0},{2,3},{3,2},{4,5},{5,4},{6,7},{7,6},{8,9},{9,8},{10,11... | collective-permute-start | bytes 184328 | tf_op jit(solution)/shard_map/ppermute | solution.py:775
  209.9 14.1 %collective-permute-start.39 = (bf16[128,768]{1,0:T(8,128)(2,1)S(1)}, bf16[128,768]{1,0:T(8,128)(2,1)S(1)}, u32[]{:S(2)}, u32[]{:S(2)}) collective-permute-start(bf16[128,768]{1,0:T(8,128)(2,1)S(1)} %copy-done.55), channel_id=1, source_target_pairs={{0,8},{1,9},{2,10},{3,11},{4,12},{5,13},{6,14},{7,15},{8,0},{9,1},... | collective-permute-start | bytes 589832 | tf_op jit(solution)/shard_map/ppermute | solution.py:775
  210.4 13.7 %collective-permute-start.48 = (bf16[128,768]{1,0:T(8,128)(2,1)S(1)}, bf16[128,768]{1,0:T(8,128)(2,1)S(1)}, u32[]{:S(2)}, u32[]{:S(2)}) collective-permute-start(bf16[128,768]{1,0:T(8,128)(2,1)S(1)} %copy-done.54), channel_id=1, source_target_pairs={{0,24},{1,25},{2,26},{3,27},{4,28},{5,29},{6,30},{7,31},{8,16},{9,... | collective-permute-start | bytes 589832 | tf_op jit(solution)/shard_map/ppermute | solution.py:775
  213.4 15.3 %collective-permute-start.47 = (bf16[128,768]{1,0:T(8,128)(2,1)S(1)}, bf16[128,768]{1,0:T(8,128)(2,1)S(1)}, u32[]{:S(2)}, u32[]{:S(2)}) collective-permute-start(bf16[128,768]{1,0:T(8,128)(2,1)S(1)} %copy-done.53), channel_id=1, source_target_pairs={{0,16},{1,17},{2,18},{3,19},{4,20},{5,21},{6,22},{7,23},{8,24},{9,... | collective-permute-start | bytes 589832 | tf_op jit(solution)/shard_map/ppermute | solution.py:775
  213.4 4.2 %collective-permute-start.50 = (bf16[40,768]{1,0:T(8,128)(2,1)S(1)}, bf16[40,768]{1,0:T(8,128)(2,1)S(1)}, u32[]{:S(2)}, u32[]{:S(2)}) collective-permute-start(bf16[40,768]{1,0:T(8,128)(2,1)S(1)} %add_convert_fusion.refs_0_), channel_id=1, source_target_pairs={{0,4},{1,5},{2,6},{3,7},{4,0},{5,1},{6,2},{7,3},{8,12},{9,13},{10,... | collective-permute-start | bytes 184328 | tf_op jit(solution)/shard_map/ppermute | solution.py:775
  213.5 5.2 %collective-permute-start.51 = (bf16[40,768]{1,0:T(8,128)(2,1)S(1)}, bf16[40,768]{1,0:T(8,128)(2,1)S(1)}, u32[]{:S(2)}, u32[]{:S(2)}) collective-permute-start(bf16[40,768]{1,0:T(8,128)(2,1)S(1)} %add_convert_fusion.refs_0_), channel_id=1, source_target_pairs={{0,5},{1,4},{2,7},{3,6},{4,1},{5,0},{6,3},{7,2},{8,13},{9,12},{10,... | collective-permute-start | bytes 184328 | tf_op jit(solution)/shard_map/ppermute | solution.py:775
  (65 other events, 451.6 us)
Sparse Core Ops, SparseCore 0:
  10.9 94.3 all-gather.1

commit v2 on v1

--- a/solution.py
+++ b/solution.py
@@ -300,7 +300,7 @@
             return (state[0] + dense_mul(low, values), state[1] + dense_mul(rest, values))
 
         zero = jnp.zeros((height, WIDE), f32)
-        context, rest = lax.fori_loop(0, chunks, mix, (zero, zero))
+        context, rest = lax.fori_loop(0, chunks, mix, (zero, zero), unroll=2)
         for n in range(at_once):
             here = slice(STACK * n, STACK * (n + 1))
             finish(2 * a + first + n, context[here], (context + rest)[here], top[here], total[here])
@@ -413,7 +413,7 @@
             def add(c, total):
                 return total + query_side(stack, outer, block_rows(k_ref, c * 8, 8), block_rows(v_ref, c * 8, 8))
 
-            total = lax.fori_loop(0, block_total // 8, add, jnp.zeros((2 * STACK, WIDE), f32))
+            total = lax.fori_loop(0, block_total // 8, add, jnp.zeros((2 * STACK, WIDE), f32), unroll=2)
             put_query(2 * a, total[:STACK])
             put_query(2 * a + 1, total[STACK:])
 
@@ -421,12 +421,30 @@
         copy.wait()
 
 
-def far_kernel(fast, meta_ref, rand_ref, k_ref, v_ref, dq_ref, w_ref, u_ref, early_ref, *refs):
+def collect_kernel(fast, block_total, meta_ref, rand_ref, pair_ref):
+    place = meta_ref[0]
+
+    def collect(block, count):
+        for r in range(3):
+            target = rand_at(fast, rand_ref, block, r)
+            mine = (((target // 2) ^ place) & ~24) == 0
+
+            @pl.when(mine)
+            def _(target=target, count=count):
+                pair_ref[count + 1] = target * 65536 + block
+
+            count = count + mine.astype(jnp.int32)
+        return count
+
+    pair_ref[0] = lax.fori_loop(2, block_total, collect, jnp.int32(0))
+
+
+def far_kernel(fast, meta_ref, pair_ref, k_ref, v_ref, dq_ref, w_ref, u_ref, early_ref, *refs):
     count = 3 if fast else 4
     tok_refs, refs = refs[:count], refs[count:]
-    slab_refs, refs = refs[:-14], refs[-14:]
-    part_refs, near_ref, away_ref, refs = refs[:4], refs[4], refs[5], refs[6:]
-    q_ref, g_ref, dk_ref, dv_ref, grad_ref, tok_ref, terms_ref, pair_ref = refs
+    slab_refs, refs = refs[:-11], refs[-11:]
+    part_refs, near_ref, away_ref, refs = refs[:2], refs[2], refs[3], refs[4:]
+    q_ref, g_ref, dk_ref, dv_ref, grad_ref, tok_ref, terms_ref = refs
     place = meta_ref[0]
     group = meta_ref[2]
     block_total = k_ref.shape[0] // BLOCK
@@ -474,26 +492,14 @@
         values = block_rows(v_ref, first, 2)
         dk_ref[here, :], dv_ref[here, :] = key_side(keys, values, blocks, allowed)
 
-    def collect(block, count):
-        for r in range(3):
-            target = rand_at(fast, rand_ref, block, r)
-            mine = (((target // 2) ^ place) & ~24) == 0
-
-            @pl.when(mine)
-            def _(target=target, count=count):
-                pair_ref[count] = target * 65536 + block
-
-            count = count + mine.astype(jnp.int32)
-        return count
-
-    pair_total = lax.fori_loop(2, block_total, collect, jnp.int32(0))
+    pair_total = pair_ref[0]
 
     def random_pairs(step, carry):
         grads = []
         for k in range(4):
             number = 4 * step + k
             live = number < pair_total
-            code = pair_ref[jnp.minimum(number, pair_total - 1)]
+            code = pair_ref[jnp.minimum(number, pair_total - 1) + 1]
             target = code // 65536
             block = code - target * 65536
             start = ((((target // 2) ^ place) >> 3) & 3) * rows + (target & 1) * BLOCK
@@ -519,7 +525,7 @@
             put(here, key_side(keys, values, [4 * step + k for k in range(4)], None))
             return carry
 
-        lax.fori_loop(0, block_total // 4, every, 0)
+        lax.fori_loop(0, block_total // 4, every, 0, unroll=2)
 
     data = lanes(rows) < SHARE
     for a in range(4):
@@ -551,8 +557,9 @@
         terms_ref[where, RANK:] = early
     near_ref[...] = terms_ref[:4]
     away_ref[...] = terms_ref[4:].astype(away_ref.dtype)
-    for a in range(4):
-        part_refs[a][...] = dense_right_t(grad_ref[rows * a : rows * (a + 1), :], w_ref[...]).astype(bf16)
+    for n, a in enumerate((0, 2, 1, 3)):
+        part = dense_right_t(grad_ref[rows * a : rows * (a + 1), :], w_ref[...]).astype(bf16)
+        part_refs[n // 2][rows * (n % 2) : rows * (n % 2 + 1), :] = part
 
 
 def normal(hidden):
@@ -800,8 +807,11 @@
         slabs = slabs + [two(slabs[1])]
         return slabs + [swap(slab, 2) for slab in slabs]
 
-    def gather_group(value):
-        return gather_end(gather_start(value))
+    def gather_direct(value):
+        return gather_start(value) + ([swap(value, 5)] if fast else [])
+
+    def gather_hand(slabs):
+        return slabs + [swap(slab, 2) for slab in slabs] if fast else slabs
 
     def gather_all(value):
         return lax.all_gather(value, AXES, axis=0, tiled=True)
@@ -825,7 +835,7 @@
         far_tokens = swap(tokens, PEERS[2])
         near_tokens = swap(jnp.concatenate([tokens, far_tokens], axis=0), PEERS[1])
         token_refs = [tokens, far_tokens, near_tokens]
-        w_slabs = gather_group(jnp.concatenate(mine, axis=0))
+        w_slabs = gather_hand(gather_direct(jnp.concatenate(mine, axis=0)))
     else:
         late = gather_all(
             jnp.concatenate([w_output, w_inner] + [w_outer[slab * c : slab * (c + 1)] for c in range(FF // D)], axis=1)
@@ -863,7 +873,16 @@
     )(meta, attn_down, attn_up, *token_refs, *w_slabs)
     if fast:
         rand_flat = rand_table
-    pair_slabs = gather_group(pair_own)
+    pair_list = pl.pallas_call(
+        functools.partial(collect_kernel, fast, block_total),
+        in_specs=[SMEM, SMEM],
+        out_specs=SMEM,
+        out_shape=jax.ShapeDtypeStruct((3 * block_total + 8,), jnp.int32),
+        name="collect",
+    )(meta, rand_flat)
+    pair_slabs = gather_start(pair_own)
+    pair_list, pair_slabs[1] = together((pair_list, pair_slabs[1]))
+    pair_slabs = gather_end(pair_slabs)
     key_all, value_all, *ctx, aux = pl.pallas_call(
         functools.partial(attend_kernel, fast),
         in_specs=[SMEM, SMEM] + [VMEM] * (1 + len(pair_slabs)),
@@ -874,8 +893,6 @@
         name="attend",
     )(meta, rand_flat, query_own, *pair_slabs)
     ctx_pieces = exchange(ctx)
-    query_send, ctx_pieces[1] = together((query_own, ctx_pieces[1]))
-    query_slabs = gather_group(query_send)
 
     gains = jnp.stack([gain_first, shift_first, gain_second, shift_second])
     middle_in = [tokens, cotangent, late, gains, attn_down, attn_up, inner_down, inner_up, outer_down, outer_up]
@@ -916,6 +933,8 @@
         compiler_params=pltpu.CompilerParams(vmem_limit_bytes=VMEM_LIMIT),
         name="middle",
     )(meta, *ctx_pieces, *middle_in)
+    query_send, grad_pieces[0] = together((query_own, grad_pieces[0]))
+    query_slabs = gather_hand(gather_direct(query_send))
     grad_wide = pl.pallas_call(
         delta_kernel,
         in_specs=[VMEM] * 5,
@@ -950,16 +969,16 @@
         out_shape=[jax.ShapeDtypeStruct((chunk, WIDE), bf16)] + zero_shapes,
         scratch_shapes=[pltpu.VMEM((4, RANK, D), f32), pltpu.SemaphoreType.DMA((ADAPTERS * 12,))],
         compiler_params=pltpu.CompilerParams(vmem_limit_bytes=VMEM_LIMIT),
-        cost_estimate=pl.CostEstimate(flops=4000000000, bytes_accessed=8000000, transcendentals=1000000),
+        cost_estimate=pl.CostEstimate(flops=12000000000, bytes_accessed=8000000, transcendentals=1000000),
         name="near",
     )(meta, rand_flat, query_own, key_all, value_all, grad_wide)
     query_grad, *grad_slabs = together((query_grad, *grad_slabs))
     grad_slabs = gather_end(grad_slabs)
-    *parts, near_terms, away_terms = pl.pallas_call(
+    kept, given, near_terms, away_terms = pl.pallas_call(
         functools.partial(far_kernel, fast),
         in_specs=[SMEM, SMEM] + [VMEM] * (6 + len(token_refs) + 2 * len(grad_slabs)),
-        out_specs=[VMEM] * 6,
-        out_shape=[jax.ShapeDtypeStruct((local_rows, D), bf16)] * 4
+        out_specs=[VMEM] * 4,
+        out_shape=[jax.ShapeDtypeStruct((2 * local_rows, D), bf16)] * 2
         + [jax.ShapeDtypeStruct((4, RANK + EARLY_PART, D), kind) for kind in (f32, bf16 if fast else f32)],
         scratch_shapes=[
             pltpu.VMEM((rows_total, WIDE), bf16),
@@ -969,13 +988,12 @@
             pltpu.VMEM((chunk, 3 * WIDE), bf16),
             pltpu.VMEM((chunk, D), bf16),
             pltpu.VMEM((8, RANK + EARLY_PART, D), f32),
-            pltpu.SMEM((3 * block_total + 8,), jnp.int32),
         ],
         compiler_params=pltpu.CompilerParams(vmem_limit_bytes=VMEM_LIMIT),
         name="far",
     )(
         meta,
-        rand_flat,
+        pair_list,
         key_all,
         value_all,
         query_grad,
@@ -986,20 +1004,16 @@
         *query_slabs,
         *grad_slabs,
     )
-    def token_sum(pieces):
-        pieces = [piece.astype(f32) for piece in pieces]
-        return grad_attended + ((pieces[0] + pieces[1]) + (pieces[2] + pieces[3]))
-
-    arrived = [parts[0], swap(parts[1], PEERS[1])]
+    kept = kept.astype(f32) + swap(given, PEERS[1]).astype(f32)
+    passed = swap(kept[local_rows:].astype(bf16), PEERS[2])
+    grad_tokens = grad_attended + (kept[:local_rows] + passed.astype(f32))
+
     if fast:
         paired = near_terms + swap(away_terms, 2).astype(f32)
         moved = [paired[0]] + [swap(paired[a].astype(bf16), PLANE[a]).astype(f32) for a in range(1, 4)]
         part = ((moved[0] + moved[1]) + (moved[2] + moved[3])).astype(bf16)
         moved = [piece.astype(f32) for piece in exchange([part] * 4)]
         part = ((moved[0] + moved[1]) + (moved[2] + moved[3])).astype(bf16)
-        part, parts[2], parts[3] = together((part, parts[2], parts[3]))
-    arrived += [swap(parts[a], PEERS[a]) for a in (2, 3)]
-    if fast:
         part_list = exchange([part] * 4, PLANE)
         part_list = part_list + [swap(value, 2) for value in part_list]
         sums = pl.pallas_call(
@@ -1014,7 +1028,7 @@
             input_output_aliases={9 + n: n for n in range(6)},
             name="spread",
         )(meta, *part_list, *zeros)
-        return (output, token_sum(arrived), *sums)
+        return (output, grad_tokens, *sums)
 
     terms = jnp.concatenate([near_terms, away_terms], axis=0)
     terms = jnp.concatenate([terms[:, :RANK].reshape(-1, D), terms[:, RANK:].reshape(-1, D)], axis=0)
@@ -1041,7 +1055,7 @@
     ]
     return (
         output,
-        token_sum(arrived),
+        grad_tokens,
         *[value.reshape(leaf.shape) for value, leaf in zip(sums, out_shapes, strict=True)],
     )
 

time: 236 us -> 222 us (0.941)
  starting transfers between devices: 57.8 us -> 51 us
  waiting for transfers between devices: 71 us -> 65.7 us
    ppermute x56 -> x55, waiting for transfers between devices: 71 us -> 58.1 us  [send(): lax.ppermute(value, AXES, [(j, j ^ (odd if j >> 1 & 1 else even)) for j i...]
    all_gather x1, waiting for transfers between devices: 0.01 us -> 7.51 us  [gather_all(): return lax.all_gather(value, AXES, axis=0, tiled=True)]
    ppermute x56 -> x55, starting transfers between devices: 57.7 us -> 51 us  [send(): lax.ppermute(value, AXES, [(j, j ^ (odd if j >> 1 & 1 else even)) for j i...]
    pallas_call x1, Pallas kernels: 28.2 us -> 24.4 us  [shards(): pl.pallas_call(functools.partial(far_kernel, fast), in_specs=[SMEM, SMEM]...]
    pallas_call x0 -> x1, Pallas kernels: none -> 3.75 us  [shards(): pl.pallas_call(functools.partial(collect_kernel, fast, block_total), in_s...]
    unnamed x115 -> x111, local copies, waits for them, and re-layouts: 4.87 us -> 4.94 us
  transfers between devices with their start and end apart: 57 -> 56, of which waited for: 29 -> 26; matrix products, arithmetic and copies ran while one was open for 1% -> 2% of each run, Pallas kernels for 22% -> 18%
where the time goes in v2:
time: 222 us; the launch traced here: 223 us
  Pallas kernels  80.7 us (36%)
  waiting for transfers between devices  65.7 us (30%)
  starting transfers between devices  51 us (23%)
  between operations  16.1 us (7%)
  local copies, waits for them, and re-layouts  4.99 us (2%)
  other arithmetic  4.32 us (2%)
    ppermute x55, waiting for transfers between devices, send(): lax.ppermute(value, AXES, [(j, j ^ (odd if j >> 1 & 1 else even)) for j i...  58.1 us
    ppermute x55, starting transfers between devices, send(): lax.ppermute(value, AXES, [(j, j ^ (odd if j >> 1 & 1 else even)) for j i...  51 us
    pallas_call x1, Pallas kernels, shards(): pl.pallas_call(functools.partial(far_kernel, fast), in_specs=[SMEM, SMEM]...  24.4 us
    pallas_call x1, Pallas kernels, shards(): pl.pallas_call(functools.partial(attend_kernel, fast), in_specs=[SMEM, SM...  15.5 us
    pallas_call x1, Pallas kernels, shards(): pl.pallas_call(middle, in_specs=[SMEM] + [VMEM] * 6 + [ANY] + [VMEM] * (c...  14.5 us
    pallas_call x1, Pallas kernels, shards(): pl.pallas_call(functools.partial(near_kernel, fast), in_specs=[SMEM, SMEM...  10.5 us
    all_gather x1, waiting for transfers between devices, gather_all(): return lax.all_gather(value, AXES, axis=0, tiled=True)  7.51 us
    unnamed x111, local copies, waits for them, and re-layouts  4.94 us
  transfers between devices with their start and end apart: 56, of which 26 were waited for; matrix products, arithmetic and copies ran while one was open for 2% of the time, Pallas kernels for 18%

profile of v2, /device:TPU:0, one launch (start us, length us, event | category | flops | bytes accessed | tf_op | source)
XLA Modules:
  0.0 222.8 jit_solution(15188988103848841770)
XLA Ops:
  7.2 2.8 %pack.1 = (bf16[24,6912]{1,0:T(8,128)(2,1)}, bf16[24,768]{1,0:T(8,128)(2,1)}, bf16[24,768]{1,0:T(8,128)(2,1)}, bf16[24,768]{1,0:T(8,128)(2,1)}, bf16[24,768]{1,0:T(8,128)(2,1)}) custom-call(s32[4,3]{1,0:T(4,128)} %rand_ref.1, bf16[24,768]{1,0:T(8,128)(2,1)} %query_ref.1, bf16[24,768]{1,0:T(8,128)(2,1)} %key_ref.1, bf16[24,768]{1,0:T(8,128)(2,1)} %value_ref.1, ...), custom_call_target="tpu_custom_call" | custom-call | tf_op jit(solution)/shard_map/pack/pallas_call | solution.py:825
  10.0 4.1 %collective-permute-start = (bf16[128,768]{1,0:T(8,128)(2,1)}, bf16[128,768]{1,0:T(8,128)(2,1)S(1)}, u32[]{:S(2)}, u32[]{:S(2)}) collective-permute-start(bf16[128,768]{1,0:T(8,128)(2,1)} %refs_0_.3), channel_id=1, source_target_pairs={{0,16},{1,17},{2,18},{3,19},{4,20},{5,21},{6,22},{7,23},{8,24},{9,... | collective-permute-start | bytes 589832 | tf_op jit(solution)/shard_map/ppermute | solution.py:782
  14.1 1.6 collective-permute-start.2
  16.0 2.5 %collective-permute-start.4 = (bf16[24,768]{1,0:T(8,128)(2,1)}, bf16[24,768]{1,0:T(8,128)(2,1)S(1)}, u32[]{:S(2)}, u32[]{:S(2)}) collective-permute-start(bf16[24,768]{1,0:T(8,128)(2,1)} %get-tuple-element.60), channel_id=1, source_target_pairs={{0,24},{1,25},{2,26},{3,27},{4,28},{5,29},{6,30},{7,31},{8,16},{9,... | collective-permute-start | bytes 110600 | tf_op jit(solution)/shard_map/ppermute | solution.py:782
  20.2 6.1 %collective-permute-done.3 = bf16[24,768]{1,0:T(8,128)(2,1)S(1)} collective-permute-done((bf16[24,768]{1,0:T(8,128)(2,1)}, bf16[24,768]{1,0:T(8,128)(2,1)S(1)}, u32[]{:S(2)}, u32[]{:S(2)}) %collective-permute-start.3) | collective-permute-done | bytes 36896 | tf_op jit(solution)/shard_map/ppermute | solution.py:782
  27.4 3.2 %collective-permute-start.1 = (bf16[256,768]{1,0:T(8,128)(2,1)S(1)}, bf16[256,768]{1,0:T(8,128)(2,1)S(1)}, u32[]{:S(2)}, u32[]{:S(2)}) collective-permute-start(bf16[256,768]{1,0:T(8,128)(2,1)S(1)} %pad_maximum_fusion), channel_id=1, source_target_pairs={{0,8},{1,9},{2,10},{3,11},{4,12},{5,13},{6,14},{7,15},{8,0},{9,1},... | collective-permute-start | bytes 1179656 | tf_op jit(solution)/shard_map/ppermute | solution.py:782
  30.6 1.6 collective-permute-start.5
  32.2 1.5 collective-permute-start.6
  34.2 3.2 %collective-permute-done.5.refs_4_ = bf16[96,768]{1,0:T(8,128)(2,1)S(1)} collective-permute-done((bf16[96,768]{1,0:T(8,128)(2,1)S(1)}, bf16[96,768]{1,0:T(8,128)(2,1)S(1)}, u32[]{:S(2)}, u32[]{:S(2)}) %collective-permute-start.5) | collective-permute-done | bytes 147488 | tf_op jit(solution)/shard_map/ppermute | solution.py:782
  37.4 3.1 %collective-permute-done.6.refs_5_ = bf16[96,768]{1,0:T(8,128)(2,1)S(1)} collective-permute-done((bf16[96,768]{1,0:T(8,128)(2,1)S(1)}, bf16[96,768]{1,0:T(8,128)(2,1)S(1)}, u32[]{:S(2)}, u32[]{:S(2)}) %collective-permute-start.6) | collective-permute-done | bytes 147488 | tf_op jit(solution)/shard_map/ppermute | solution.py:782
  44.5 4.5 %project.1 = (bf16[768,768]{1,0:T(8,128)(2,1)}, bf16[3,128,256]{2,1,0:T(8,128)(2,1)}, bf16[512,256]{1,0:T(8,128)(2,1)}, bf16[512,384]{1,0:T(8,128)(2,1)}, s32[32,128]{1,0:T(8,128)}) custom-call(s32[4]{0:T(128)} %pad_add_fusion.meta_ref, bf16[8,4,16,768]{3,2,1,0:T(8,128)(2,1)} %refs_8_.1, bf16[8,4,16,768]{3,2,1,0:T(8,128)(2,1)} %refs_9_.1, ...), custom_call_target="tpu_custom_call" | custom-call | tf_op jit(solution)/shard_map/project/pallas_call | solution.py:859
  49.9 1.5 collective-permute-start.13
  51.4 3.8 %collect.1.pair_ref = s32[200]{0:T(256)} custom-call(s32[4]{0:T(128)} %pad_add_fusion.meta_ref, s32[32,128]{1,0:T(8,128)} %get-tuple-element.61.rand_ref), custom_call_target="tpu_custom_call" | custom-call | tf_op jit(solution)/shard_map/collect/pallas_call | solution.py:876
  55.2 7.2 %collective-permute-done.12.refs_1_ = bf16[512,384]{1,0:T(8,128)(2,1)S(1)} collective-permute-done((bf16[512,384]{1,0:T(8,128)(2,1)}, bf16[512,384]{1,0:T(8,128)(2,1)S(1)}, u32[]{:S(2)}, u32[]{:S(2)}) %collective-permute-start.12) | collective-permute-done | bytes 393248 | tf_op jit(solution)/shard_map/ppermute | solution.py:782
  62.4 1.8 collective-permute-start.14
  64.8 6.7 %collective-permute-done.14.refs_3_ = bf16[512,384]{1,0:T(8,128)(2,1)S(1)} collective-permute-done((bf16[512,384]{1,0:T(8,128)(2,1)S(1)}, bf16[512,384]{1,0:T(8,128)(2,1)S(1)}, u32[]{:S(2)}, u32[]{:S(2)}) %collective-permute-start.14) | collective-permute-done | bytes 393248 | tf_op jit(solution)/shard_map/ppermute | solution.py:782
  71.6 1.7 collective-permute-done.18.refs_7_
  74.1 15.5 %attend.1 = (bf16[4096,256]{1,0:T(8,128)(2,1)}, bf16[4096,256]{1,0:T(8,128)(2,1)}, bf16[128,256]{1,0:T(8,128)(2,1)}, bf16[128,256]{1,0:T(8,128)(2,1)}, bf16[128,...) custom-call(s32[4]{0:T(128)} %pad_add_fusion.meta_ref, s32[32,128]{1,0:T(8,128)} %get-tuple-element.61.rand_ref, ...), custom_call_target="tpu_custom_call" | custom-call | tf_op jit(solution)/shard_map/attend/pallas_call | solution.py:886
  90.5 2.3 %collective-permute-start.20 = (bf16[128,256]{1,0:T(8,128)(2,1)}, bf16[128,256]{1,0:T(8,128)(2,1)S(1)}, u32[]{:S(2)}, u32[]{:S(2)}) collective-permute-start(bf16[128,256]{1,0:T(8,128)(2,1)} %get-tuple-element.67), channel_id=1, source_target_pairs={{0,16},{1,17},{2,18},{3,19},{4,20},{5,21},{6,22},{7,23},{8,24},{9,... | collective-permute-start | bytes 196616 | tf_op jit(solution)/shard_map/ppermute | solution.py:782
  92.8 1.1 collective-permute-start.21
  94.5 3.2 %collective-permute-done.19.refs_1_ = bf16[128,256]{1,0:T(8,128)(2,1)S(1)} collective-permute-done((bf16[128,256]{1,0:T(8,128)(2,1)}, bf16[128,256]{1,0:T(8,128)(2,1)S(1)}, u32[]{:S(2)}, u32[]{:S(2)}) %collective-permute-start.19) | collective-permute-done | bytes 65568 | tf_op jit(solution)/shard_map/ppermute | solution.py:782
  97.7 2.3 %collective-permute-done.20.refs_2_ = bf16[128,256]{1,0:T(8,128)(2,1)S(1)} collective-permute-done((bf16[128,256]{1,0:T(8,128)(2,1)}, bf16[128,256]{1,0:T(8,128)(2,1)S(1)}, u32[]{:S(2)}, u32[]{:S(2)}) %collective-permute-start.20) | collective-permute-done | bytes 65568 | tf_op jit(solution)/shard_map/ppermute | solution.py:782
  100.5 7.5 %all-gather.2.cloned.1.call-done.refs_6_ = bf16[768,6912]{1,0:T(8,128)(2,1)} async-done(((bf16[24,6912]{1,0:T(8,128)(2,1)}), bf16[768,6912]{1,0:T(8,128)(2,1)}) %all-gather.2.cloned.1.call-update) | async-done | bytes 10616848 | tf_op jit(solution)/shard_map/all_gather | solution.py:817
  108.0 14.5 %middle.1 = (bf16[128,768]{1,0:T(8,128)(2,1)}, f32[128,768]{1,0:T(8,128)}, bf16[128,256]{1,0:T(8,128)(2,1)}, bf16[128,256]{1,0:T(8,128)(2,1)}, bf16[128,256]{1,0...) custom-call(s32[4]{0:T(128)} %pad_add_fusion.meta_ref, bf16[128,256]{1,0:T(8,128)(2,1)} %get-tuple-element.65.refs_0_, ...), custom_call_target="tpu_custom_call" | custom-call | tf_op jit(solution)/shard_map/middle/pallas_call | solution.py:915
  122.6 2.2 collective-permute-start.23
  124.8 2.2 collective-permute-start.24
  127.0 1.2 collective-permute-start.27
  128.3 1.5 collective-permute-start.28
  132.2 2.6 %delta.1.g_ref.refs_11_ = bf16[512,256]{1,0:T(8,128)(2,1)} custom-call(bf16[128,256]{1,0:T(8,128)(2,1)} %get-tuple-element.76.refs_0_, bf16[128,256]{1,0:T(8,128)(2,1)} %copy-done.40, bf16[128,256]{1,0:T(8,128)(2,1)} %copy-done.41, bf16[128,256]{1,0:T(8,128)(2,1)} %copy-done.42, f32[512,256]{1,0:T(8,128)} %get-tuple-element.80.refs_4_), custom_call_target="tpu_custom_call" | custom-call | tf_op jit(solution)/shard_map/delta/pallas_call | solution.py:938
  134.8 1.2 collective-permute-start.25
  136.1 1.5 collective-permute-start.26
  137.5 10.5 %near.1 = (bf16[512,256]{1,0:T(8,128)(2,1)}, f32[8,4,16,768]{3,2,1,0:T(8,128)}, f32[8,4,16,768]{3,2,1,0:T(8,128)}, f32[8,16,768]{2,1,0:T(8,128)}, f32[8,16,3072]...) custom-call(s32[4]{0:T(128)} %pad_add_fusion.meta_ref, s32[32,128]{1,0:T(8,128)} %get-tuple-element.61.rand_ref, ...), custom_call_target="tpu_custom_call" | custom-call | flops 12000000000 | bytes 8000000 | tf_op jit(solution)/shard_map/near/pallas_call | solution.py:965
  150.5 4.6 %collective-permute-done.34.refs_14_ = bf16[512,256]{1,0:T(8,128)(2,1)S(1)} collective-permute-done((bf16[512,256]{1,0:T(8,128)(2,1)S(1)}, bf16[512,256]{1,0:T(8,128)(2,1)S(1)}, u32[]{:S(2)}, u32[]{:S(2)}) %collective-permute-start.34) | collective-permute-done | bytes 262176 | tf_op jit(solution)/shard_map/ppermute | solution.py:782
  155.2 1.5 collective-permute-done.38.refs_18_
  157.4 24.4 %far.1 = (bf16[256,768]{1,0:T(8,128)(2,1)}, bf16[256,768]{1,0:T(8,128)(2,1)}, f32[4,40,768]{2,1,0:T(8,128)}, bf16[4,40,768]{2,1,0:T(8,128)(2,1)}) custom-call(s32[4]{0:T(128)} %pad_add_fusion.meta_ref, s32[200]{0:T(256)} %collect.1.pair_ref, bf16[4096,256]{1,0:T(8,128)(2,1)} %get-tuple-element.73.k_ref, bf16[4096,256]{1,0:T(8,128)(2,1)} %get-tuple-element.74.v_ref, ...), custom_call_target="tpu_custom_call" | custom-call | tf_op jit(solution)/shard_map/far/pallas_call | solution.py:977
  181.8 1.4 collective-permute-start.39
  183.5 1.1 fusion.4
  184.8 3.4 %collective-permute-start.42 = (bf16[40,768]{1,0:T(8,128)(2,1)S(1)}, bf16[40,768]{1,0:T(8,128)(2,1)S(1)}, u32[]{:S(2)}, u32[]{:S(2)}) collective-permute-start(bf16[40,768]{1,0:T(8,128)(2,1)S(1)} %get-tuple-element.108), channel_id=1, source_target_pairs={{0,1},{1,0},{2,3},{3,2},{4,5},{5,4},{6,7},{7,6},{8,9},{9,8},{10,11... | collective-permute-start | bytes 184328 | tf_op jit(solution)/shard_map/ppermute | solution.py:782
  188.2 2.1 collective-permute-done.44
  191.0 1.9 collective-permute-start.47
  193.8 1.6 collective-permute-start.45
  196.1 1.3 collective-permute-done.47
  197.3 7.2 %collective-permute-done.46 = bf16[40,768]{1,0:T(8,128)(2,1)S(1)} collective-permute-done((bf16[40,768]{1,0:T(8,128)(2,1)S(1)}, bf16[40,768]{1,0:T(8,128)(2,1)S(1)}, u32[]{:S(2)}, u32[]{:S(2)}) %collective-permute-start.46) | collective-permute-done | bytes 61472 | tf_op jit(solution)/shard_map/ppermute | solution.py:782
  205.4 2.8 %collective-permute-start.50 = (bf16[40,768]{1,0:T(8,128)(2,1)S(1)}, bf16[40,768]{1,0:T(8,128)(2,1)S(1)}, u32[]{:S(2)}, u32[]{:S(2)}) collective-permute-start(bf16[40,768]{1,0:T(8,128)(2,1)S(1)} %add_convert_fusion.refs_0_), channel_id=1, source_target_pairs={{0,5},{1,4},{2,7},{3,6},{4,1},{5,0},{6,3},{7,2},{8,13},{9,12},{10,... | collective-permute-start | bytes 184328 | tf_op jit(solution)/shard_map/ppermute | solution.py:782
  208.2 1.1 collective-permute-done.48.refs_1_
  209.8 1.2 collective-permute-done.50.refs_3_
  211.1 1.2 collective-permute-done.54.refs_7_
  212.9 2.2 %spread.1 = (f32[8,4,16,768]{3,2,1,0:T(8,128)}, f32[8,4,16,768]{3,2,1,0:T(8,128)}, f32[8,16,768]{2,1,0:T(8,128)}, f32[8,16,3072]{2,1,0:T(8,128)}, f32[8,16,3072]{2,1,0:T(8,128)}, /*index=5*/f32[8,16,768]{2,1,0:T(8,128)}) custom-call(s32[4]{0:T(128)} %pad_add_fusion.meta_ref, ...), custom_call_target="tpu_custom_call", output_to_operand_aliasing={{0}: (9, {}), {1}: (10, {}), {2}: (11, {}), {3}: (12, {}), ... | custom-call | tf_op jit(solution)/shard_map/spread/pallas_call | solution.py:1019
  (200 shorter events, 21.7 us)
Async XLA Ops:
  7.2 100.8 %all-gather.2.cloned.1.call-start = ((), (), s32[]{:S(2)}) async-start(), calls=%async_computation | async-start | bytes 10948608 | tf_op jit(solution)/shard_map/all_gather | solution.py:817
  10.0 16.3 %collective-permute-start = (bf16[128,768]{1,0:T(8,128)(2,1)}, bf16[128,768]{1,0:T(8,128)(2,1)S(1)}, u32[]{:S(2)}, u32[]{:S(2)}) collective-permute-start(bf16[128,768]{1,0:T(8,128)(2,1)} %refs_0_.3), channel_id=1, source_target_pairs={{0,16},{1,17},{2,18},{3,19},{4,20},{5,21},{6,22},{7,23},{8,24},{9,... | collective-permute-start | bytes 589832 | tf_op jit(solution)/shard_map/ppermute | solution.py:782
  14.1 6.1 %collective-permute-start.2 = (bf16[24,768]{1,0:T(8,128)(2,1)}, bf16[24,768]{1,0:T(8,128)(2,1)S(1)}, u32[]{:S(2)}, u32[]{:S(2)}) collective-permute-start(bf16[24,768]{1,0:T(8,128)(2,1)} %get-tuple-element.58), channel_id=1, source_target_pairs={{0,8},{1,9},{2,10},{3,11},{4,12},{5,13},{6,14},{7,15},{8,0},{9,1},... | collective-permute-start | bytes 110600 | tf_op jit(solution)/shard_map/ppermute | solution.py:782
  15.7 10.7 %collective-permute-start.3 = (bf16[24,768]{1,0:T(8,128)(2,1)}, bf16[24,768]{1,0:T(8,128)(2,1)S(1)}, u32[]{:S(2)}, u32[]{:S(2)}) collective-permute-start(bf16[24,768]{1,0:T(8,128)(2,1)} %get-tuple-element.59), channel_id=1, source_target_pairs={{0,16},{1,17},{2,18},{3,19},{4,20},{5,21},{6,22},{7,23},{8,24},{9,... | collective-permute-start | bytes 110600 | tf_op jit(solution)/shard_map/ppermute | solution.py:782
  16.0 14.6 %collective-permute-start.4 = (bf16[24,768]{1,0:T(8,128)(2,1)}, bf16[24,768]{1,0:T(8,128)(2,1)S(1)}, u32[]{:S(2)}, u32[]{:S(2)}) collective-permute-start(bf16[24,768]{1,0:T(8,128)(2,1)} %get-tuple-element.60), channel_id=1, source_target_pairs={{0,24},{1,25},{2,26},{3,27},{4,28},{5,29},{6,30},{7,31},{8,16},{9,... | collective-permute-start | bytes 110600 | tf_op jit(solution)/shard_map/ppermute | solution.py:782
  27.4 15.6 %collective-permute-start.1 = (bf16[256,768]{1,0:T(8,128)(2,1)S(1)}, bf16[256,768]{1,0:T(8,128)(2,1)S(1)}, u32[]{:S(2)}, u32[]{:S(2)}) collective-permute-start(bf16[256,768]{1,0:T(8,128)(2,1)S(1)} %pad_maximum_fusion), channel_id=1, source_target_pairs={{0,8},{1,9},{2,10},{3,11},{4,12},{5,13},{6,14},{7,15},{8,0},{9,1},... | collective-permute-start | bytes 1179656 | tf_op jit(solution)/shard_map/ppermute | solution.py:782
  30.6 6.8 %collective-permute-start.5 = (bf16[96,768]{1,0:T(8,128)(2,1)S(1)}, bf16[96,768]{1,0:T(8,128)(2,1)S(1)}, u32[]{:S(2)}, u32[]{:S(2)}) collective-permute-start(bf16[96,768]{1,0:T(8,128)(2,1)S(1)} %constant_dynamic-update-slice_fusion.refs_3_), channel_id=1, source_target_pairs={{0,4},{1,5},{2,3},{3,2},{4,0},{5,1},{6,7},{7,6},{8,12},{9,13},{10,... | collective-permute-start | bytes 442376 | tf_op jit(solution)/shard_map/ppermute | solution.py:782
  32.2 8.3 %collective-permute-start.6 = (bf16[96,768]{1,0:T(8,128)(2,1)S(1)}, bf16[96,768]{1,0:T(8,128)(2,1)S(1)}, u32[]{:S(2)}, u32[]{:S(2)}) collective-permute-start(bf16[96,768]{1,0:T(8,128)(2,1)S(1)} %constant_dynamic-update-slice_fusion.refs_3_), channel_id=1, source_target_pairs={{0,1},{1,0},{2,6},{3,7},{4,5},{5,4},{6,2},{7,3},{8,9},{9,8},{10,14... | collective-permute-start | bytes 442376 | tf_op jit(solution)/shard_map/ppermute | solution.py:782
  33.7 6.8 %collective-permute-start.7 = (bf16[96,768]{1,0:T(8,128)(2,1)S(1)}, bf16[96,768]{1,0:T(8,128)(2,1)S(1)}, u32[]{:S(2)}, u32[]{:S(2)}) collective-permute-start(bf16[96,768]{1,0:T(8,128)(2,1)S(1)} %constant_dynamic-update-slice_fusion.refs_3_), channel_id=1, source_target_pairs={{0,5},{1,4},{2,7},{3,6},{4,1},{5,0},{6,3},{7,2},{8,13},{9,12},{10,... | collective-permute-start | bytes 442376 | tf_op jit(solution)/shard_map/ppermute | solution.py:782
  34.2 8.8 %collective-permute-start.8 = (bf16[96,768]{1,0:T(8,128)(2,1)S(1)}, bf16[96,768]{1,0:T(8,128)(2,1)S(1)}, u32[]{:S(2)}, u32[]{:S(2)}) collective-permute-start(bf16[96,768]{1,0:T(8,128)(2,1)S(1)} %constant_dynamic-update-slice_fusion.refs_3_), channel_id=1, source_target_pairs={{0,2},{1,3},{2,0},{3,1},{4,6},{5,7},{6,4},{7,5},{8,10},{9,11},{10,... | collective-permute-start | bytes 442376 | tf_op jit(solution)/shard_map/ppermute | solution.py:782
  37.4 5.6 %collective-permute-start.9 = (bf16[96,768]{1,0:T(8,128)(2,1)S(1)}, bf16[96,768]{1,0:T(8,128)(2,1)S(1)}, u32[]{:S(2)}, u32[]{:S(2)}) collective-permute-start(bf16[96,768]{1,0:T(8,128)(2,1)S(1)} %collective-permute-done.5.refs_4_), channel_id=1, source_target_pairs={{0,2},{1,3},{2,0},{3,1},{4,6},{5,7},{6,4},{7,5},{8,10},{9,11},{10,... | collective-permute-start | bytes 442376 | tf_op jit(solution)/shard_map/ppermute | solution.py:782
  40.5 2.5 %collective-permute-start.10 = (bf16[96,768]{1,0:T(8,128)(2,1)S(1)}, bf16[96,768]{1,0:T(8,128)(2,1)S(1)}, u32[]{:S(2)}, u32[]{:S(2)}) collective-permute-start(bf16[96,768]{1,0:T(8,128)(2,1)S(1)} %collective-permute-done.6.refs_5_), channel_id=1, source_target_pairs={{0,2},{1,3},{2,0},{3,1},{4,6},{5,7},{6,4},{7,5},{8,10},{9,11},{10,... | collective-permute-start | bytes 442376 | tf_op jit(solution)/shard_map/ppermute | solution.py:782
  40.5 2.5 %collective-permute-start.11 = (bf16[96,768]{1,0:T(8,128)(2,1)S(1)}, bf16[96,768]{1,0:T(8,128)(2,1)S(1)}, u32[]{:S(2)}, u32[]{:S(2)}) collective-permute-start(bf16[96,768]{1,0:T(8,128)(2,1)S(1)} %collective-permute-done.7.refs_6_), channel_id=1, source_target_pairs={{0,2},{1,3},{2,0},{3,1},{4,6},{5,7},{6,4},{7,5},{8,10},{9,11},{10,... | collective-permute-start | bytes 442376 | tf_op jit(solution)/shard_map/ppermute | solution.py:782
  49.1 13.3 %collective-permute-start.12 = (bf16[512,384]{1,0:T(8,128)(2,1)}, bf16[512,384]{1,0:T(8,128)(2,1)S(1)}, u32[]{:S(2)}, u32[]{:S(2)}) collective-permute-start(bf16[512,384]{1,0:T(8,128)(2,1)} %get-tuple-element.63.refs_0_), channel_id=1, source_target_pairs={{0,4},{1,5},{2,3},{3,2},{4,0},{5,1},{6,7},{7,6},{8,12},{9,13},{10,... | collective-permute-start | bytes 1179656 | tf_op jit(solution)/shard_map/ppermute | solution.py:782
  49.9 14.8 %collective-permute-start.13 = (bf16[512,384]{1,0:T(8,128)(2,1)}, bf16[512,384]{1,0:T(8,128)(2,1)S(1)}, u32[]{:S(2)}, u32[]{:S(2)}) collective-permute-start(bf16[512,384]{1,0:T(8,128)(2,1)} %get-tuple-element.63.refs_0_), channel_id=1, source_target_pairs={{0,1},{1,0},{2,6},{3,7},{4,5},{5,4},{6,2},{7,3},{8,9},{9,8},{10,14... | collective-permute-start | bytes 1179656 | tf_op jit(solution)/shard_map/ppermute | solution.py:782
  62.4 9.1 %collective-permute-start.14 = (bf16[512,384]{1,0:T(8,128)(2,1)S(1)}, bf16[512,384]{1,0:T(8,128)(2,1)S(1)}, u32[]{:S(2)}, u32[]{:S(2)}) collective-permute-start(bf16[512,384]{1,0:T(8,128)(2,1)S(1)} %collective-permute-done.12.refs_1_), channel_id=1, source_target_pairs={{0,1},{1,0},{2,6},{3,7},{4,5},{5,4},{6,2},{7,3},{8,9},{9,8},{10,14... | collective-permute-start | bytes 1179656 | tf_op jit(solution)/shard_map/ppermute | solution.py:782
  64.2 7.4 %collective-permute-start.15 = (bf16[512,384]{1,0:T(8,128)(2,1)}, bf16[512,384]{1,0:T(8,128)(2,1)S(1)}, u32[]{:S(2)}, u32[]{:S(2)}) collective-permute-start(bf16[512,384]{1,0:T(8,128)(2,1)} %get-tuple-element.63.refs_0_), channel_id=1, source_target_pairs={{0,2},{1,3},{2,0},{3,1},{4,6},{5,7},{6,4},{7,5},{8,10},{9,11},{10,... | collective-permute-start | bytes 1179656 | tf_op jit(solution)/shard_map/ppermute | solution.py:782
  64.2 7.4 %collective-permute-start.16 = (bf16[512,384]{1,0:T(8,128)(2,1)S(1)}, bf16[512,384]{1,0:T(8,128)(2,1)S(1)}, u32[]{:S(2)}, u32[]{:S(2)}) collective-permute-start(bf16[512,384]{1,0:T(8,128)(2,1)S(1)} %collective-permute-done.12.refs_1_), channel_id=1, source_target_pairs={{0,2},{1,3},{2,0},{3,1},{4,6},{5,7},{6,4},{7,5},{8,10},{9,11},{10,... | collective-permute-start | bytes 1179656 | tf_op jit(solution)/shard_map/ppermute | solution.py:782
  64.7 6.9 %collective-permute-start.17 = (bf16[512,384]{1,0:T(8,128)(2,1)S(1)}, bf16[512,384]{1,0:T(8,128)(2,1)S(1)}, u32[]{:S(2)}, u32[]{:S(2)}) collective-permute-start(bf16[512,384]{1,0:T(8,128)(2,1)S(1)} %collective-permute-done.13.refs_2_), channel_id=1, source_target_pairs={{0,2},{1,3},{2,0},{3,1},{4,6},{5,7},{6,4},{7,5},{8,10},{9,11},{10,... | collective-permute-start | bytes 1179656 | tf_op jit(solution)/shard_map/ppermute | solution.py:782
  89.5 8.2 %collective-permute-start.19 = (bf16[128,256]{1,0:T(8,128)(2,1)}, bf16[128,256]{1,0:T(8,128)(2,1)S(1)}, u32[]{:S(2)}, u32[]{:S(2)}) collective-permute-start(bf16[128,256]{1,0:T(8,128)(2,1)} %get-tuple-element.66), channel_id=1, source_target_pairs={{0,8},{1,9},{2,10},{3,11},{4,12},{5,13},{6,14},{7,15},{8,0},{9,1},... | collective-permute-start | bytes 196616 | tf_op jit(solution)/shard_map/ppermute | solution.py:782
  90.5 9.5 %collective-permute-start.20 = (bf16[128,256]{1,0:T(8,128)(2,1)}, bf16[128,256]{1,0:T(8,128)(2,1)S(1)}, u32[]{:S(2)}, u32[]{:S(2)}) collective-permute-start(bf16[128,256]{1,0:T(8,128)(2,1)} %get-tuple-element.67), channel_id=1, source_target_pairs={{0,16},{1,17},{2,18},{3,19},{4,20},{5,21},{6,22},{7,23},{8,24},{9,... | collective-permute-start | bytes 196616 | tf_op jit(solution)/shard_map/ppermute | solution.py:782
  92.8 7.7 %collective-permute-start.21 = (bf16[128,256]{1,0:T(8,128)(2,1)}, bf16[128,256]{1,0:T(8,128)(2,1)S(1)}, u32[]{:S(2)}, u32[]{:S(2)}) collective-permute-start(bf16[128,256]{1,0:T(8,128)(2,1)} %get-tuple-element.68), channel_id=1, source_target_pairs={{0,24},{1,25},{2,26},{3,27},{4,28},{5,29},{6,30},{7,31},{8,16},{9,... | collective-permute-start | bytes 196616 | tf_op jit(solution)/shard_map/ppermute | solution.py:782
  122.6 7.2 %collective-permute-start.22 = (bf16[128,256]{1,0:T(8,128)(2,1)}, bf16[128,256]{1,0:T(8,128)(2,1)S(1)}, u32[]{:S(2)}, u32[]{:S(2)}) collective-permute-start(bf16[128,256]{1,0:T(8,128)(2,1)} %get-tuple-element.77), channel_id=1, source_target_pairs={{0,8},{1,9},{2,10},{3,11},{4,12},{5,13},{6,14},{7,15},{8,0},{9,1},... | collective-permute-start | bytes 196616 | tf_op jit(solution)/shard_map/ppermute | solution.py:782
  122.6 8.9 %collective-permute-start.23 = (bf16[128,256]{1,0:T(8,128)(2,1)}, bf16[128,256]{1,0:T(8,128)(2,1)S(1)}, u32[]{:S(2)}, u32[]{:S(2)}) collective-permute-start(bf16[128,256]{1,0:T(8,128)(2,1)} %get-tuple-element.78), channel_id=1, source_target_pairs={{0,16},{1,17},{2,18},{3,19},{4,20},{5,21},{6,22},{7,23},{8,24},{9,... | collective-permute-start | bytes 196616 | tf_op jit(solution)/shard_map/ppermute | solution.py:782
  124.8 6.7 %collective-permute-start.24 = (bf16[128,256]{1,0:T(8,128)(2,1)}, bf16[128,256]{1,0:T(8,128)(2,1)S(1)}, u32[]{:S(2)}, u32[]{:S(2)}) collective-permute-start(bf16[128,256]{1,0:T(8,128)(2,1)} %get-tuple-element.79), channel_id=1, source_target_pairs={{0,24},{1,25},{2,26},{3,27},{4,28},{5,29},{6,30},{7,31},{8,16},{9,... | collective-permute-start | bytes 196616 | tf_op jit(solution)/shard_map/ppermute | solution.py:782
  127.0 21.0 %collective-permute-start.27 = (bf16[512,256]{1,0:T(8,128)(2,1)S(1)}, bf16[512,256]{1,0:T(8,128)(2,1)S(1)}, u32[]{:S(2)}, u32[]{:S(2)}) collective-permute-start(bf16[512,256]{1,0:T(8,128)(2,1)S(1)} %copy-done.2), channel_id=1, source_target_pairs={{0,4},{1,5},{2,3},{3,2},{4,0},{5,1},{6,7},{7,6},{8,12},{9,13},{10,... | collective-permute-start | bytes 786440 | tf_op jit(solution)/shard_map/ppermute | solution.py:782
  128.3 19.9 %collective-permute-start.28 = (bf16[512,256]{1,0:T(8,128)(2,1)S(1)}, bf16[512,256]{1,0:T(8,128)(2,1)S(1)}, u32[]{:S(2)}, u32[]{:S(2)}) collective-permute-start(bf16[512,256]{1,0:T(8,128)(2,1)S(1)} %copy-done.2), channel_id=1, source_target_pairs={{0,1},{1,0},{2,6},{3,7},{4,5},{5,4},{6,2},{7,3},{8,9},{9,8},{10,14... | collective-permute-start | bytes 786440 | tf_op jit(solution)/shard_map/ppermute | solution.py:782
  129.7 19.1 %collective-permute-start.29 = (bf16[512,256]{1,0:T(8,128)(2,1)S(1)}, bf16[512,256]{1,0:T(8,128)(2,1)S(1)}, u32[]{:S(2)}, u32[]{:S(2)}) collective-permute-start(bf16[512,256]{1,0:T(8,128)(2,1)S(1)} %copy-done.2), channel_id=1, source_target_pairs={{0,5},{1,4},{2,7},{3,6},{4,1},{5,0},{6,3},{7,2},{8,13},{9,12},{10,... | collective-permute-start | bytes 786440 | tf_op jit(solution)/shard_map/ppermute | solution.py:782
  134.8 13.8 %collective-permute-start.25 = (bf16[512,256]{1,0:T(8,128)(2,1)}, bf16[512,256]{1,0:T(8,128)(2,1)S(1)}, u32[]{:S(2)}, u32[]{:S(2)}) collective-permute-start(bf16[512,256]{1,0:T(8,128)(2,1)} %delta.1.g_ref.refs_11_), channel_id=1, source_target_pairs={{0,4},{1,5},{2,3},{3,2},{4,0},{5,1},{6,7},{7,6},{8,12},{9,13},{10,... | collective-permute-start | bytes 786440 | tf_op jit(solution)/shard_map/ppermute | solution.py:782
  136.1 12.7 %collective-permute-start.26 = (bf16[512,256]{1,0:T(8,128)(2,1)}, bf16[512,256]{1,0:T(8,128)(2,1)S(1)}, u32[]{:S(2)}, u32[]{:S(2)}) collective-permute-start(bf16[512,256]{1,0:T(8,128)(2,1)} %delta.1.g_ref.refs_11_), channel_id=1, source_target_pairs={{0,1},{1,0},{2,6},{3,7},{4,5},{5,4},{6,2},{7,3},{8,9},{9,8},{10,14... | collective-permute-start | bytes 786440 | tf_op jit(solution)/shard_map/ppermute | solution.py:782
  148.1 1.9 collective-permute-start.31
  148.7 6.4 %collective-permute-start.34 = (bf16[512,256]{1,0:T(8,128)(2,1)S(1)}, bf16[512,256]{1,0:T(8,128)(2,1)S(1)}, u32[]{:S(2)}, u32[]{:S(2)}) collective-permute-start(bf16[512,256]{1,0:T(8,128)(2,1)S(1)} %collective-permute-done.25.refs_12_), channel_id=1, source_target_pairs={{0,1},{1,0},{2,6},{3,7},{4,5},{5,4},{6,2},{7,3},{8,9},{9,8},{10,14... | collective-permute-start | bytes 786440 | tf_op jit(solution)/shard_map/ppermute | solution.py:782
  148.8 6.3 %collective-permute-start.33 = (bf16[512,256]{1,0:T(8,128)(2,1)S(1)}, bf16[512,256]{1,0:T(8,128)(2,1)S(1)}, u32[]{:S(2)}, u32[]{:S(2)}) collective-permute-start(bf16[512,256]{1,0:T(8,128)(2,1)S(1)} %collective-permute-done.29.refs_6_), channel_id=1, source_target_pairs={{0,2},{1,3},{2,0},{3,1},{4,6},{5,7},{6,4},{7,5},{8,10},{9,11},{10,... | collective-permute-start | bytes 786440 | tf_op jit(solution)/shard_map/ppermute | solution.py:782
  149.6 5.5 %collective-permute-start.36 = (bf16[512,256]{1,0:T(8,128)(2,1)S(1)}, bf16[512,256]{1,0:T(8,128)(2,1)S(1)}, u32[]{:S(2)}, u32[]{:S(2)}) collective-permute-start(bf16[512,256]{1,0:T(8,128)(2,1)S(1)} %collective-permute-done.25.refs_12_), channel_id=1, source_target_pairs={{0,2},{1,3},{2,0},{3,1},{4,6},{5,7},{6,4},{7,5},{8,10},{9,11},{10,... | collective-permute-start | bytes 786440 | tf_op jit(solution)/shard_map/ppermute | solution.py:782
  150.0 5.1 %collective-permute-start.35 = (bf16[512,256]{1,0:T(8,128)(2,1)S(1)}, bf16[512,256]{1,0:T(8,128)(2,1)S(1)}, u32[]{:S(2)}, u32[]{:S(2)}) collective-permute-start(bf16[512,256]{1,0:T(8,128)(2,1)S(1)} %copy-done.4), channel_id=1, source_target_pairs={{0,2},{1,3},{2,0},{3,1},{4,6},{5,7},{6,4},{7,5},{8,10},{9,11},{10,... | collective-permute-start | bytes 786440 | tf_op jit(solution)/shard_map/ppermute | solution.py:782
  150.4 4.8 %collective-permute-start.37 = (bf16[512,256]{1,0:T(8,128)(2,1)S(1)}, bf16[512,256]{1,0:T(8,128)(2,1)S(1)}, u32[]{:S(2)}, u32[]{:S(2)}) collective-permute-start(bf16[512,256]{1,0:T(8,128)(2,1)S(1)} %collective-permute-done.26.refs_13_), channel_id=1, source_target_pairs={{0,2},{1,3},{2,0},{3,1},{4,6},{5,7},{6,4},{7,5},{8,10},{9,11},{10,... | collective-permute-start | bytes 786440 | tf_op jit(solution)/shard_map/ppermute | solution.py:782
  181.8 13.6 %collective-permute-start.39 = (bf16[256,768]{1,0:T(8,128)(2,1)}, bf16[256,768]{1,0:T(8,128)(2,1)S(1)}, u32[]{:S(2)}, u32[]{:S(2)}) collective-permute-start(bf16[256,768]{1,0:T(8,128)(2,1)} %get-tuple-element.91), channel_id=1, source_target_pairs={{0,8},{1,9},{2,10},{3,11},{4,12},{5,13},{6,14},{7,15},{8,0},{9,1},... | collective-permute-start | bytes 1179656 | tf_op jit(solution)/shard_map/ppermute | solution.py:782
  184.6 5.7 %collective-permute-start.44 = (bf16[40,768]{1,0:T(8,128)(2,1)S(1)}, bf16[40,768]{1,0:T(8,128)(2,1)S(1)}, u32[]{:S(2)}, u32[]{:S(2)}) collective-permute-start(bf16[40,768]{1,0:T(8,128)(2,1)S(1)} %get-tuple-element.109), channel_id=1, source_target_pairs={{0,5},{1,4},{2,7},{3,6},{4,1},{5,0},{6,3},{7,2},{8,13},{9,12},{10,... | collective-permute-start | bytes 184328 | tf_op jit(solution)/shard_map/ppermute | solution.py:782
  184.7 5.6 %collective-permute-start.43 = (bf16[40,768]{1,0:T(8,128)(2,1)S(1)}, bf16[40,768]{1,0:T(8,128)(2,1)S(1)}, u32[]{:S(2)}, u32[]{:S(2)}) collective-permute-start(bf16[40,768]{1,0:T(8,128)(2,1)S(1)} %get-tuple-element.110), channel_id=1, source_target_pairs={{0,4},{1,5},{2,6},{3,7},{4,0},{5,1},{6,2},{7,3},{8,12},{9,13},{10,... | collective-permute-start | bytes 184328 | tf_op jit(solution)/shard_map/ppermute | solution.py:782
  184.8 6.2 %collective-permute-start.42 = (bf16[40,768]{1,0:T(8,128)(2,1)S(1)}, bf16[40,768]{1,0:T(8,128)(2,1)S(1)}, u32[]{:S(2)}, u32[]{:S(2)}) collective-permute-start(bf16[40,768]{1,0:T(8,128)(2,1)S(1)} %get-tuple-element.108), channel_id=1, source_target_pairs={{0,1},{1,0},{2,3},{3,2},{4,5},{5,4},{6,7},{7,6},{8,9},{9,8},{10,11... | collective-permute-start | bytes 184328 | tf_op jit(solution)/shard_map/ppermute | solution.py:782
  191.0 6.3 %collective-permute-start.47 = (bf16[40,768]{1,0:T(8,128)(2,1)S(1)}, bf16[40,768]{1,0:T(8,128)(2,1)S(1)}, u32[]{:S(2)}, u32[]{:S(2)}) collective-permute-start(bf16[40,768]{1,0:T(8,128)(2,1)S(1)} %fusion.3), channel_id=1, source_target_pairs={{0,24},{1,25},{2,26},{3,27},{4,28},{5,29},{6,30},{7,31},{8,16},{9,... | collective-permute-start | bytes 184328 | tf_op jit(solution)/shard_map/ppermute | solution.py:782
  192.9 11.7 %collective-permute-start.46 = (bf16[40,768]{1,0:T(8,128)(2,1)S(1)}, bf16[40,768]{1,0:T(8,128)(2,1)S(1)}, u32[]{:S(2)}, u32[]{:S(2)}) collective-permute-start(bf16[40,768]{1,0:T(8,128)(2,1)S(1)} %fusion.3), channel_id=1, source_target_pairs={{0,16},{1,17},{2,18},{3,19},{4,20},{5,21},{6,22},{7,23},{8,24},{9,... | collective-permute-start | bytes 184328 | tf_op jit(solution)/shard_map/ppermute | solution.py:782
  193.8 10.7 %collective-permute-start.45 = (bf16[40,768]{1,0:T(8,128)(2,1)S(1)}, bf16[40,768]{1,0:T(8,128)(2,1)S(1)}, u32[]{:S(2)}, u32[]{:S(2)}) collective-permute-start(bf16[40,768]{1,0:T(8,128)(2,1)S(1)} %fusion.3), channel_id=1, source_target_pairs={{0,8},{1,9},{2,10},{3,11},{4,12},{5,13},{6,14},{7,15},{8,0},{9,1},... | collective-permute-start | bytes 184328 | tf_op jit(solution)/shard_map/ppermute | solution.py:782
  195.6 19.6 %collective-permute-start.40 = (bf16[128,768]{1,0:T(8,128)(2,1)S(1)}, bf16[128,768]{1,0:T(8,128)(2,1)S(1)}, u32[]{:S(2)}, u32[]{:S(2)}) collective-permute-start(bf16[128,768]{1,0:T(8,128)(2,1)S(1)} %slice.48), channel_id=1, source_target_pairs={{0,16},{1,17},{2,18},{3,19},{4,20},{5,21},{6,22},{7,23},{8,24},{9,... | collective-permute-start | bytes 589832 | tf_op jit(solution)/shard_map/ppermute | solution.py:782
  204.6 4.7 %collective-permute-start.48 = (bf16[40,768]{1,0:T(8,128)(2,1)S(1)}, bf16[40,768]{1,0:T(8,128)(2,1)S(1)}, u32[]{:S(2)}, u32[]{:S(2)}) collective-permute-start(bf16[40,768]{1,0:T(8,128)(2,1)S(1)} %add_convert_fusion.refs_0_), channel_id=1, source_target_pairs={{0,1},{1,0},{2,3},{3,2},{4,5},{5,4},{6,7},{7,6},{8,9},{9,8},{10,11... | collective-permute-start | bytes 184328 | tf_op jit(solution)/shard_map/ppermute | solution.py:782
  205.3 4.2 %collective-permute-start.49 = (bf16[40,768]{1,0:T(8,128)(2,1)S(1)}, bf16[40,768]{1,0:T(8,128)(2,1)S(1)}, u32[]{:S(2)}, u32[]{:S(2)}) collective-permute-start(bf16[40,768]{1,0:T(8,128)(2,1)S(1)} %add_convert_fusion.refs_0_), channel_id=1, source_target_pairs={{0,4},{1,5},{2,6},{3,7},{4,0},{5,1},{6,2},{7,3},{8,12},{9,13},{10,... | collective-permute-start | bytes 184328 | tf_op jit(solution)/shard_map/ppermute | solution.py:782
  205.4 5.6 %collective-permute-start.50 = (bf16[40,768]{1,0:T(8,128)(2,1)S(1)}, bf16[40,768]{1,0:T(8,128)(2,1)S(1)}, u32[]{:S(2)}, u32[]{:S(2)}) collective-permute-start(bf16[40,768]{1,0:T(8,128)(2,1)S(1)} %add_convert_fusion.refs_0_), channel_id=1, source_target_pairs={{0,5},{1,4},{2,7},{3,6},{4,1},{5,0},{6,3},{7,2},{8,13},{9,12},{10,... | collective-permute-start | bytes 184328 | tf_op jit(solution)/shard_map/ppermute | solution.py:782
  208.2 2.9 %collective-permute-start.51 = (bf16[40,768]{1,0:T(8,128)(2,1)S(1)}, bf16[40,768]{1,0:T(8,128)(2,1)S(1)}, u32[]{:S(2)}, u32[]{:S(2)}) collective-permute-start(bf16[40,768]{1,0:T(8,128)(2,1)S(1)} %add_convert_fusion.refs_0_), channel_id=1, source_target_pairs={{0,2},{1,3},{2,0},{3,1},{4,6},{5,7},{6,4},{7,5},{8,10},{9,11},{10,... | collective-permute-start | bytes 184328 | tf_op jit(solution)/shard_map/ppermute | solution.py:782
  (62 other events, 373.7 us)
Sparse Core Ops, SparseCore 0:
  10.9 97.0 all-gather.1
